TPU v7x, 512 devices: a whole 4x4x16 slice. The times are simulated.
512 devices in a mesh: grid: 128 (over z, x, core), layer: 4 (over y).
Axes of the slice: x: 4, y: 4, z: 16, core: 2. Of those that a mesh axis runs over, the one named last changes fastest.
Arguments:
- lower_inverse: bfloat16 [4, 256, 128, 128], P('layer', 'grid'), as said below
- upper_inverse: bfloat16 [4, 256, 128, 128], P('layer', 'grid'), as said below
- lower_link: bfloat16 [4, 256, 128, 128], P('layer', 'grid'), may hold values from -1 to 1
- upper_link: bfloat16 [4, 256, 128, 128], P('layer', 'grid'), may hold values from -1 to 1
- lower_root: bfloat16 [4, 256, 512, 128], P('layer', 'grid'), may hold values from -0.03125 to 0.03125
- upper_root: bfloat16 [4, 256, 128, 512], P('layer', 'grid'), may hold values from -0.125 to 0.125
- rhs_blocks: bfloat16 [4, 256, 128, 128], P('layer', 'grid'), may hold values from -0.29882812 to 0.29882812
- rhs_root: bfloat16 [512, 128], replicated, may hold values from -3 to 3
- root_lower_inverse: bfloat16 [512, 512], replicated, as said below
- root_upper_inverse: bfloat16 [512, 512], replicated, as said below
- live_counts: int32 [4, 128], P('layer', 'grid'), may hold values from 1 to 2
Outputs:
- solution: float32 [4, 256, 128, 128], P('layer', 'grid')
- root_solution: float32 [512, 128], P(None, 'grid')
Inputs may be any that keep to these rules, and one draw needn't show every extreme that they name: `lower_inverse`: unit lower triangular. `upper_inverse`: upper triangular with diagonal entries between 0.5 and 1.5. `root_lower_inverse`: unit lower triangular. `root_upper_inverse`: upper triangular with diagonal entries between 0.5 and 1.5.
All inputs are finite; a program needn't handle non-finite values.
Results may differ from a plain program's by a relative error of at most 0.0003.
Values sent between devices are 32-bit elements; how exact they have to be, the bound alone decides.
No kernel may reach another device: no remote copies, remote signals or barrier semaphores. Data moves between devices by JAX's collectives and lax.ppermute only.
A program may use at most 128 MiB of HBM per device.

v0:
```python
import jax
import jax.numpy as jnp
from jax import lax
from jax.sharding import PartitionSpec as P


def prefix_2(part, axis, combine, identity, reverse):
    count = lax.axis_size(axis)
    place = lax.axis_index(axis)
    ahead = count - 1 - place if reverse else place
    gathered = jax.tree.map(lambda a: lax.all_gather(a, axis), part)
    state = jax.tree.map(lambda a, e: jnp.zeros_like(a) + jnp.asarray(e, a.dtype), part, identity)

    def one(step, state):
        source = count - 1 - step if reverse else step
        return combine(
            state, jax.tree.map(lambda a: lax.dynamic_index_in_dim(a, source, 0, False), gathered)
        )

    return lax.fori_loop(0, ahead, one, state)


def product(left, right):
    return jnp.matmul(
        left.astype(jnp.float32), right.astype(jnp.float32), precision=lax.Precision.HIGHEST
    )


def native(left, right):
    return jnp.dot(left, right, preferred_element_type=jnp.float32)


def compose(earlier, later):
    head = product(later[0], earlier[0])
    rest = [product(later[0], piece) + own for piece, own in zip(earlier[1:], later[1:])]
    return tuple([head] + rest)


def on_device(
    lower_inverse,
    upper_inverse,
    lower_link,
    upper_link,
    lower_root,
    upper_root,
    rhs_blocks,
    rhs_root,
    root_lower_inverse,
    root_upper_inverse,
    live_counts,
):
    active_count = live_counts[0, 0]
    slot_total = lower_inverse.shape[1]
    block_width = lower_inverse.shape[2]
    columns = rhs_blocks.shape[3]
    root_width = rhs_root.shape[0]
    identity_block = jnp.eye(block_width, dtype=jnp.float32)
    empty_block = jnp.zeros((block_width, block_width), jnp.float32)
    empty_rhs = jnp.zeros((block_width, columns), jnp.float32)
    step_maps = []
    step_offsets = []
    composite = (identity_block, empty_rhs)
    for slot in range(slot_total):

        def build_forward(carried, slot=slot):
            inverse = lower_inverse[0, slot]
            step_map = -native(inverse, lower_link[0, slot])
            step_offset = native(inverse, rhs_blocks[0, slot])
            return (compose(carried, (step_map, step_offset)), step_map, step_offset)

        def skip_forward(carried):
            return (carried, empty_block, empty_rhs)

        composite, step_map, step_offset = lax.cond(
            slot < active_count, build_forward, skip_forward, composite
        )
        step_maps.append(step_map)
        step_offsets.append(step_offset)
    prefix = prefix_2(composite, "grid", compose, (identity_block, empty_rhs), False)
    carried = prefix[1]
    solved = []
    root_term = jnp.zeros((root_width, columns), jnp.float32)
    for slot in range(slot_total):
        alive = slot < active_count
        value = jnp.where(
            alive, step_offsets[slot] + product(step_maps[slot], carried), jnp.float32(0.0)
        )
        carried = jnp.where(alive, value, carried)
        solved.append(value)
        root_term = root_term + product(lower_root[0, slot], value)
    back_maps = []
    back_plain = []
    back_links = []
    for slot in range(slot_total):
        inverse = upper_inverse[0, slot]
        back_maps.append(-native(inverse, upper_link[0, slot]))
        back_plain.append(product(inverse, solved[slot]))
        back_links.append(-native(inverse, upper_root[0, slot]))
    per_device = columns // lax.axis_size("grid")
    summed = lax.psum(root_term, ("grid", "layer"))
    root_full = product(
        root_upper_inverse, product(root_lower_inverse, rhs_root.astype(jnp.float32) - summed)
    )
    root_own = lax.dynamic_slice_in_dim(
        root_full, lax.axis_index("grid") * per_device, per_device, 1
    )
    back_offsets = [
        back_plain[slot] + product(back_links[slot], root_full) for slot in range(slot_total)
    ]
    backward_maps = (identity_block, empty_rhs)
    for slot in reversed(range(slot_total)):

        def build_backward(carried_maps, slot=slot):
            return compose(carried_maps, (back_maps[slot], back_offsets[slot]))

        def skip_backward(carried_maps):
            return carried_maps

        backward_maps = lax.cond(slot < active_count, build_backward, skip_backward, backward_maps)
    backward_prefix = prefix_2(backward_maps, "grid", compose, (identity_block, empty_rhs), True)
    inflow = backward_prefix[1]
    carried = inflow
    answers = [None] * slot_total
    for slot in reversed(range(slot_total)):
        alive = slot < active_count
        value = jnp.where(
            alive, back_offsets[slot] + product(back_maps[slot], carried), jnp.float32(0.0)
        )
        carried = jnp.where(alive, value, carried)
        answers[slot] = value
    return (jnp.stack(answers)[None], root_own)


def solution(mesh):
    return jax.shard_map(
        on_device,
        mesh=mesh,
        in_specs=(
            P("layer", "grid", None, None),
            P("layer", "grid", None, None),
            P("layer", "grid", None, None),
            P("layer", "grid", None, None),
            P("layer", "grid", None, None),
            P("layer", "grid", None, None),
            P("layer", "grid", None, None),
            P(),
            P(),
            P(),
            P("layer", "grid"),
        ),
        out_specs=(P("layer", "grid", None, None), P(None, "grid")),
        check_vma=False,
    )
```

profile of v0, /device:TPU:6, one launch (start us, length us, event | category | flops | bytes accessed | tf_op | source)
XLA Modules:
  0.0 1348.1 jit_solution(663387009504411779)
XLA Ops:
  8.0 5.2 conditional.4
  8.0 1.5 convolution_negate_fusion
  9.6 1.5 fusion
  13.2 5.2 conditional.5
  13.2 1.5 convolution_negate_fusion.1
  14.8 1.5 fusion.11
  20.8 1.1 convolution_negate_fusion.3
  21.9 1.1 convolution_negate_fusion.2
  23.0 145.7 %all-gather.9.cloned.1.call-done = f32[16384,128]{1,0:T(8,128)} async-done(((f32[128,128]{1,0:T(8,128)}), f32[16384,128]{1,0:T(8,128)}) %all-gather.9.cloned.1.call-update) | async-done | bytes 8388624 | tf_op jit(solution)/shard_map/all_gather | solution.py:11
  168.7 145.2 %all-gather.11.cloned.1.call-done = f32[16384,128]{1,0:T(8,128)} async-done(((f32[128,128]{1,0:T(8,128)}), f32[16384,128]{1,0:T(8,128)}) %all-gather.11.cloned.1.call-update) | async-done | bytes 8388624 | tf_op jit(solution)/shard_map/all_gather | solution.py:11
  313.9 6.7 while.26
  313.9 1.1 convolution_add_fusion.12
  316.2 1.1 convolution_add_fusion.12
  319.6 1.1 convolution_add_fusion.12
  321.7 1.2 fusion.39
  324.0 1.9 fusion.26
  326.9 585.6 %all-reduce.2.cloned.1.call-done = f32[512,128]{1,0:T(8,128)} async-done(((f32[512,128]{1,0:T(8,128)}), f32[512,128]{1,0:T(8,128)}) %all-reduce.2.cloned.1.call-update) | async-done | bytes 262160 | tf_op jit(solution)/shard_map/psum | solution.py:100
  912.4 1.7 fusion.34
  918.7 139.8 %all-gather.13.cloned.1.call-done = f32[16384,128]{1,0:T(8,128)} async-done(((f32[128,128]{1,0:T(8,128)}), f32[16384,128]{1,0:T(8,128)}) %all-gather.13.cloned.1.call-update) | async-done | bytes 8388624 | tf_op jit(solution)/shard_map/all_gather | solution.py:11
  1058.5 145.5 %all-gather.15.cloned.1.call-done = f32[16384,128]{1,0:T(8,128)} async-done(((f32[128,128]{1,0:T(8,128)}), f32[16384,128]{1,0:T(8,128)}) %all-gather.15.cloned.1.call-update) | async-done | bytes 8388624 | tf_op jit(solution)/shard_map/all_gather | solution.py:11
  1204.0 136.4 %while.27 = (s32[]{:T(128)}, f32[128,128]{1,0:T(8,128)S(1)}, s32[]{:T(128)}, f32[128,128,128]{2,1,0:T(8,128)}, f32[128,128,128]{2,1,0:T(8,128)}, /*index=5*/s32[]{:T(128)}, s32[]{:T(128)}, s32[]{:T(128)}, s32[]{:T(128)}) while((s32[]{:T(128)}, f32[128,128]{1,0:T(8,128)S(1)}, s32[]{:T(128)}, f32[128,128,128]{2,1,0:T(8,128)}, ...), condition=%wide.region_13.14_spmd, body=%wide.region_12.13_spmd.sunk | while | flops 25182212 | bytes 394379 | solution.py:20
  1207.4 1.1 convolution_add_fusion.13
  1209.7 1.1 convolution_add_fusion.13
  1210.8 1.1 convolution_add_fusion.13
  1214.2 1.1 convolution_add_fusion.13
  1218.7 1.1 convolution_add_fusion.13
  1219.8 1.1 convolution_add_fusion.13
  1223.2 1.1 convolution_add_fusion.13
  1224.3 1.1 convolution_add_fusion.13
  1232.2 1.1 convolution_add_fusion.13
  1233.4 1.1 convolution_add_fusion.13
  1236.8 1.1 convolution_add_fusion.13
  (296 shorter events, 139.0 us)
Async XLA Ops:
  7.2 905.2 %copy-start = (bf16[512,512]{1,0:T(8,128)(2,1)S(1)}, bf16[512,512]{1,0:T(8,128)(2,1)}, u32[]{:S(2)}) copy-start(bf16[512,512]{1,0:T(8,128)(2,1)} %param.31) | copy-start | bytes 1572868
  7.2 908.0 %copy-start.5 = (bf16[1,2,128,128]{3,2,1,0:T(8,128)(2,1)S(1)}, bf16[1,2,128,128]{3,2,1,0:T(8,128)(2,1)}, u32[]{:S(2)}) copy-start(bf16[1,2,128,128]{3,2,1,0:T(8,128)(2,1)} %param.24) | copy-start | bytes 196612
  7.2 906.9 %copy-start.6 = (bf16[512,512]{1,0:T(8,128)(2,1)S(1)}, bf16[512,512]{1,0:T(8,128)(2,1)}, u32[]{:S(2)}) copy-start(bf16[512,512]{1,0:T(8,128)(2,1)} %param.32) | copy-start | bytes 1572868
  7.2 161.5 %all-gather.9.cloned.1.call-start = ((), (), s32[]{:S(2)}) async-start(), calls=%async_computation.1 | async-start | bytes 8454144 | tf_op jit(solution)/shard_map/all_gather | solution.py:11
  18.5 0.6 copy-start.2
  18.5 0.7 copy-start.3
  19.1 294.8 %all-gather.11.cloned.1.call-start = ((), (), s32[]{:S(2)}) async-start(), calls=%async_computation.2 | async-start | bytes 8454144 | tf_op jit(solution)/shard_map/all_gather | solution.py:11
  19.8 892.6 %all-reduce.2.cloned.1.call-start = ((), (), s32[]{:S(2)}) async-start(), calls=%async_computation | async-start | bytes 524288 | tf_op jit(solution)/shard_map/psum | solution.py:100
  325.9 732.6 %all-gather.13.cloned.1.call-start = ((), (), s32[]{:S(2)}) async-start(), calls=%async_computation.3 | async-start | bytes 8454144 | tf_op jit(solution)/shard_map/all_gather | solution.py:11
  916.8 0.6 copy-start.1
  916.9 0.7 copy-start.4
  917.5 286.5 %all-gather.15.cloned.1.call-start = ((), (), s32[]{:S(2)}) async-start(), calls=%async_computation.4 | async-start | bytes 8454144 | tf_op jit(solution)/shard_map/all_gather | solution.py:11
Sparse Core Ops, SparseCore 0:
  19.2 149.4 all-gather.8
  171.8 142.0 all-gather.10
  326.0 586.3 all-reduce.1
  917.6 140.8 all-gather.12
  1062.0 142.0 all-gather.14
where the time goes:
time: 1360 us; the launch traced here: 1350 us
  waiting for transfers between devices  1160 us (85%)
  matrix products  161 us (12%)
  between operations  14.8 us (1%)
    psum x1, waiting for transfers between devices, on_device(): summed = lax.psum(root_term, ('grid', 'layer'))  586 us
    all_gather x4, waiting for transfers between devices, prefix_2(): gathered = jax.tree.map(lambda a: lax.all_gather(a, axis), part)  576 us
    dot_general x146, matrix products, product(): jnp.matmul(left.astype(jnp.float32), right.astype(jnp.float32), precision...  151 us
  transfers between devices with their start and end apart: 5, of which 5 were waited for; matrix products, arithmetic and copies ran while one was open for 0% of the time, Pallas kernels for 0%

commit v1 on v0

v1 whole, which is shorter than its diff:
```python
import jax
import jax.numpy as jnp
from jax import lax
from jax.experimental import pallas as pl
from jax.experimental.pallas import tpu as pltpu
from jax.sharding import Mesh
from jax.sharding import PartitionSpec as P

W = 128
F32 = jnp.float32
BF16 = jnp.bfloat16
CHAIN = ("zh", "zl", "x", "c")


def dot(left, right):
    return jnp.dot(left, right, preferred_element_type=F32)


def halves(value):
    high = value.astype(BF16)
    return high, (value - high.astype(F32)).astype(BF16)


def mul2(exact, right):
    high, low = halves(right)
    return dot(exact, high) + dot(exact, low)


def mul3(left, right):
    left_high, left_low = halves(left)
    right_high, right_low = halves(right)
    return dot(
        jnp.concatenate([left_high, left_low, left_high], 1),
        jnp.concatenate([right_high, right_high, right_low], 0),
    )


def shift(offset):
    return jnp.concatenate([jnp.zeros_like(offset), offset], 1)


def pack(square):
    return jnp.concatenate([square[: W // 2], square[W // 2 :]], 1)


def unpack(packed):
    return jnp.concatenate([packed[:, :W], packed[:, W:]], 0)


def eye():
    rows = lax.broadcasted_iota(jnp.int32, (W, W), 0)
    cols = lax.broadcasted_iota(jnp.int32, (W, W), 1)
    return jnp.where(rows == cols, F32(1), F32(0))


def slots_kernel(where, linv, llink, rhs, uinv, ulink, lroot, own, keep, send):
    core, both = where[3], where[5] == 2
    maps = []
    for slot in range(2):
        made = dot(linv[0, slot], jnp.concatenate([llink[0, slot], rhs[0, slot]], 1))
        maps.append(jnp.concatenate([-made[:, :W], made[:, W:]], 1))
    chain = mul3(maps[1][:, :W], maps[0]) + shift(maps[1][:, W:])
    chain = jnp.where(both, chain, maps[0])
    back = [-dot(uinv[0, slot], ulink[0, slot]) for slot in range(2)]
    back = jnp.where(both, mul3(back[0], back[1]), back[0])
    own[:W] = chain
    own[W:] = pack(back)
    send[:W] = chain
    send[W : W + W // 2] = pack(back)
    for half, target, at in ((core, keep, 0), (1 - core, send, W + W // 2)):
        rows = pl.ds(pl.multiple_of(half * 256, 256), 256)
        second = jnp.where(both, mul2(lroot[0, 1, rows], chain), F32(0))
        target[at : at + 256] = mul2(lroot[0, 0, rows], maps[0]) + second


def chip_kernel(where, own, keep, send, out, early, back):
    first = where[3] == 0
    mine, theirs = own[:W], send[:W]
    head = jnp.where(first, mine, theirs)
    tail = jnp.where(first, theirs, mine)
    chain = mul3(tail[:, :W], head) + shift(tail[:, W:])
    back_mine, back_theirs = unpack(own[W:]), unpack(send[W : W + W // 2])
    back_head = jnp.where(first, back_mine, back_theirs)
    back_tail = jnp.where(first, back_theirs, back_mine)
    both = pack(mul3(back_head, back_tail))
    root_mine, root_theirs = keep[...], send[W + W // 2 :]
    root_head = jnp.where(first, root_mine, root_theirs)
    root_tail = jnp.where(first, root_theirs, root_mine)
    root = root_head + mul3(root_tail[:, :W], head) + shift(root_tail[:, W:])
    early[...] = head
    back[0] = back_head
    back[1] = back_tail
    for other in range(4):
        out[other, :W] = chain
        out[other, W : W + W // 2] = both
        out[other, W + W // 2 :] = root[64 * other : 64 * other + 64]


def later_weights(place, b1, b2, b12):
    one, none = eye(), jnp.zeros((W, W), F32)
    return [
        jnp.where(place == 0, one, none),
        jnp.where(place == 0, b1, jnp.where(place == 1, one, none)),
        jnp.where(place == 0, b12, jnp.where(place == 1, b2, jnp.where(place == 2, one, none))),
    ]


def level_kernel(axis, where, parts, out, before, behind, weights):
    place = where[axis]
    maps = [parts[k, :W] for k in range(4)]
    backs = [unpack(parts[k, W : W + W // 2]) for k in range(4)]
    roots = [parts[k, W + W // 2 :] for k in range(4)]
    prefix = maps[0]
    prefixes = [prefix]
    root = roots[0]
    for k in range(1, 4):
        stacked = mul3(jnp.concatenate([maps[k][:, :W], roots[k][:, :W]], 0), prefix)
        prefix = stacked[:W] + shift(maps[k][:, W:])
        root = root + stacked[W:] + shift(roots[k][:, W:])
        prefixes.append(prefix)
    start = jnp.concatenate([eye(), jnp.zeros((W, W), F32)], 1)
    before[...] = jnp.where(
        place == 0,
        start,
        jnp.where(place == 1, prefixes[0], jnp.where(place == 2, prefixes[1], prefixes[2])),
    )
    b01 = mul3(backs[0], backs[1])
    b12 = mul3(backs[1], backs[2])
    b23 = mul3(backs[2], backs[3])
    b012 = mul3(b01, backs[2])
    b123 = mul3(backs[1], b23)
    behind[...] = jnp.where(
        place == 0, b123, jnp.where(place == 1, b23, jnp.where(place == 2, backs[3], eye()))
    )
    out[:W] = prefix
    out[W : W + W // 2] = pack(mul3(b01, b23))
    out[W + W // 2 :] = root
    weights[:W] = jnp.concatenate([backs[0], b01, b012], 1)
    weights[W:] = jnp.concatenate(later_weights(place, backs[1], backs[2], b12), 1)


def top_kernel(where, parts, root, carry, weights):
    place = where[0]
    maps = [parts[k, :W] for k in range(4)]
    backs = [unpack(parts[k, W : W + W // 2]) for k in range(1, 3)]
    roots = [parts[k, W + W // 2 :] for k in range(4)]
    total = roots[0][:, W:]
    state = maps[0][:, W:]
    states = [jnp.zeros((W, W), F32), state]
    for k in range(1, 4):
        stacked = mul3(jnp.concatenate([maps[k][:, :W], roots[k][:, :W]], 0), state)
        total = total + stacked[W:] + roots[k][:, W:]
        state = stacked[:W] + maps[k][:, W:]
        states.append(state)
    carry[...] = jnp.where(
        place == 0,
        states[0],
        jnp.where(place == 1, states[1], jnp.where(place == 2, states[2], states[3])),
    )
    for other in range(4):
        root[other] = total
    weights[...] = jnp.concatenate(
        later_weights(place, backs[0], backs[1], mul3(backs[0], backs[1])), 1
    )


def sum_kernel(parts, out):
    total = (parts[0] + parts[1]) + (parts[2] + parts[3])
    for other in range(8):
        out[other] = total


def root_kernel(
    where, sums, rhs_root, root_lower, root_upper, carry, before_low, before_x, early,
    linv, llink, rhs, uinv, ulink, uroot, own_root, plain, offset,
):
    core, both = where[3], where[5] == 2
    summed = jnp.concatenate([sums[2 * (k % 4) + k // 4] for k in range(8)], 0)
    inner = mul2(root_lower[...], rhs_root[...].astype(F32) - summed)
    root = mul2(root_upper[...], inner)
    lanes = lax.broadcasted_iota(jnp.int32, (512, W), 1)
    own_root[...] = jnp.sum(jnp.where(lanes == where[4], root, F32(0)), 1, keepdims=True)
    state = carry[...]
    for ref in (before_low, before_x):
        state = mul3(ref[:, :W], state) + ref[:, W:]
    state = jnp.where(core == 0, state, mul3(early[:, :W], state) + early[:, W:])
    root_high, root_low = halves(root)
    offsets = []
    for slot in range(2):
        state = mul2(
            linv[0, slot], rhs[0, slot].astype(F32) - mul2(llink[0, slot], state)
        )
        inner = state - (dot(uroot[0, slot], root_high) + dot(uroot[0, slot], root_low))
        offsets.append(mul2(uinv[0, slot], inner))
    link = -dot(uinv[0, 0], ulink[0, 0])
    plain[0] = offsets[0]
    plain[1] = offsets[1]
    offset[...] = jnp.where(both, offsets[0] + mul3(link, offsets[1]), offsets[0])


def pair_kernel(back, parts, out):
    out[...] = parts[0] + mul3(back[0], parts[1])


def offsets_kernel(parts, weights, out, behind):
    later = jnp.concatenate([parts[1], parts[2], parts[3]], 0)
    made = mul3(weights[...], later)
    out[...] = parts[0] + made[:W]
    behind[...] = made[W:]


def answer_kernel(
    where, parts, weights, maps_low, behind_low, maps_x, behind_x, back, pair, plain,
    uinv, ulink, out,
):
    core, both = where[3], where[5] == 2
    state = mul3(weights[...], jnp.concatenate([parts[1], parts[2], parts[3]], 0))
    state = mul3(maps_low[...], state) + behind_low[...]
    state = mul3(maps_x[...], state) + behind_x[...]
    state = jnp.where(core == 0, mul3(back[1], state) + pair[1], state)
    links = [-dot(uinv[0, slot], ulink[0, slot]) for slot in range(2)]
    last = mul3(links[1], state) + plain[1]
    state = jnp.where(both, last, state)
    out[0, 1] = jnp.where(both, last, F32(0))
    out[0, 0] = mul3(links[0], state) + plain[0]


def call(kernel, inputs, shapes):
    vmem = pl.BlockSpec(memory_space=pltpu.VMEM)
    smem = pl.BlockSpec(memory_space=pltpu.SMEM)
    outs = [jax.ShapeDtypeStruct(shape, F32) for shape in shapes]
    return pl.pallas_call(
        kernel,
        out_shape=outs,
        in_specs=[smem if a.dtype == jnp.int32 else vmem for a in inputs],
        out_specs=[vmem] * len(outs),
        compiler_params=pltpu.CompilerParams(vmem_limit_bytes=32 * 1024 * 1024),
    )(*inputs)


def on_device(
    lower_inverse,
    upper_inverse,
    lower_link,
    upper_link,
    lower_root,
    upper_root,
    rhs_blocks,
    rhs_root,
    root_lower_inverse,
    root_upper_inverse,
    live_counts,
):
    places = [lax.axis_index(name) for name in CHAIN]
    column = ((places[0] * 4 + places[1]) * 4 + places[2]) * 2 + places[3]
    where = jnp.stack(places + [column, live_counts[0, 0]]).astype(jnp.int32)
    square, wide, message = (W, W), (W, 2 * W), (2 * W, 2 * W)

    own, keep, send = call(
        slots_kernel,
        [where, lower_inverse, lower_link, rhs_blocks, upper_inverse, upper_link, lower_root],
        [(192, 256), (256, 256), (448, 256)],
    )
    send = lax.ppermute(send, "c", [(0, 1), (1, 0)])
    out, early, back = call(
        chip_kernel, [where, own, keep, send], [(4,) + message, wide, (2,) + square]
    )
    parts = lax.all_to_all(out, "x", 0, 0, tiled=True)

    def level(axis, parts):
        return call(
            lambda *refs: level_kernel(axis, *refs),
            [where, parts],
            [message, wide, square, (2 * W, 3 * W)],
        )

    out, before_x, maps_x, weights_x = level(2, parts)
    parts = lax.all_gather(out, "zl")
    out, before_low, maps_low, weights_low = level(1, parts)
    parts = lax.all_gather(out, "zh")
    root, carry, weights_high = call(
        top_kernel, [where, parts], [(4, 64, W), square, (W, 3 * W)]
    )
    parts = lax.all_to_all(root, "y", 0, 0, tiled=True)
    (root,) = call(sum_kernel, [parts], [(8, 64, W)])
    sums = lax.all_to_all(root, ("x", "c"), 0, 0, tiled=True)
    own_root, plain, offset = call(
        root_kernel,
        [
            where, sums, rhs_root, root_lower_inverse, root_upper_inverse, carry, before_low,
            before_x, early, lower_inverse, lower_link, rhs_blocks, upper_inverse, upper_link,
            upper_root,
        ],
        [(512, 1), (2,) + square, square],
    )
    pair = lax.all_gather(offset, "c")
    (offset,) = call(pair_kernel, [back, pair], [square])
    parts = lax.all_gather(offset, "x")
    offset, behind_x = call(offsets_kernel, [parts, weights_x], [square, square])
    parts = lax.all_gather(offset, "zl")
    offset, behind_low = call(offsets_kernel, [parts, weights_low], [square, square])
    parts = lax.all_gather(offset, "zh")
    (answers,) = call(
        answer_kernel,
        [
            where, parts, weights_high, maps_low, behind_low, maps_x, behind_x, back, pair,
            plain, upper_inverse, upper_link,
        ],
        [(1, 2, W, W)],
    )
    return answers, own_root


def solution(mesh):
    fine = Mesh(mesh.devices.reshape(4, 4, 4, 2, 4), CHAIN + ("y",))
    split = P("y", CHAIN)
    return jax.shard_map(
        on_device,
        mesh=fine,
        in_specs=(split,) * 7 + (P(), P(), P(), split),
        out_specs=(split, P(None, CHAIN)),
        check_vma=False,
    )
```

time: 1360 us -> 231 us (0.17)
  waiting for transfers between devices: 1160 us -> 100 us
  matrix products: 161 us -> 0 us
  blocking collectives: 0 us -> 91.1 us
  Pallas kernels: 0 us -> 13.9 us
    psum x1 -> x0, waiting for transfers between devices: 586 us -> none  [on_device(): summed = lax.psum(root_term, ('grid', 'layer'))]
    all_gather x4 -> x2, waiting for transfers between devices: 576 us -> 98.5 us  [the longest x1 59.6 us: on_device(): parts = lax.all_gather(out, 'zh')]
    dot_general x154 -> x0, matrix products: 161 us -> none  [the longest x146 151 us: product(): jnp.matmul(left.astype(jnp.float32), right.astype(jnp.float32), precision...]
    all_gather x0 -> x4, blocking collectives: none -> 48.3 us  [the longest x1 19.8 us: on_device(): parts = lax.all_gather(offset, 'zh')]
    all_to_all x0 -> x3, blocking collectives: none -> 42.8 us  [the longest x1 21.9 us: on_device(): parts = lax.all_to_all(out, 'x', 0, 0, tiled=True)]
    pallas_call x0 -> x11, Pallas kernels: none -> 13.9 us  [call(): pl.pallas_call(kernel, out_shape=outs, in_specs=[smem if a.dtype == jnp.i...]
  transfers between devices with their start and end apart: 5 -> 3, of which waited for: 5 -> 3; matrix products, arithmetic and copies ran while one was open for 0% -> 0% of each run, Pallas kernels for 0% -> 0%
where the time goes in v1:
time: 231 us
  waiting for transfers between devices  100 us (43%)
  blocking collectives  91.1 us (39%)
  between operations  14.9 us (6%)
  Pallas kernels  13.9 us (6%)
  local copies, waits for them, and re-layouts  8.42 us (4%)
    all_gather x1, waiting for transfers between devices, on_device(): parts = lax.all_gather(out, 'zh')  59.6 us
    all_gather x1, waiting for transfers between devices, on_device(): parts = lax.all_gather(out, 'zl')  38.9 us
    all_to_all x1, blocking collectives, on_device(): parts = lax.all_to_all(out, 'x', 0, 0, tiled=True)  21.9 us
    all_gather x1, blocking collectives, on_device(): parts = lax.all_gather(offset, 'zh')  19.8 us
    all_gather x1, blocking collectives, on_device(): parts = lax.all_gather(offset, 'zl')  14.3 us
    pallas_call x11, Pallas kernels, call(): pl.pallas_call(kernel, out_shape=outs, in_specs=[smem if a.dtype == jnp.i...  13.9 us
    all_gather x1, blocking collectives, on_device(): parts = lax.all_gather(offset, 'x')  12.3 us
    all_to_all x1, blocking collectives, on_device(): sums = lax.all_to_all(root, ('x', 'c'), 0, 0, tiled=True)  10.8 us
  transfers between devices with their start and end apart: 3, of which 3 were waited for; matrix products, arithmetic and copies ran while one was open for 0% of the time, Pallas kernels for 0%

profile of v1, /device:TPU:6, one launch (start us, length us, event | category | flops | bytes accessed | tf_op | source)
XLA Modules:
  0.0 230.7 jit_solution(15523888672689936308)
XLA Ops:
  7.9 0.1 stack.23.where.refs_0_
  8.0 0.8 copy-done.2
  8.8 0.8 copy-done.4
  9.6 0.9 copy-done.8
  10.6 0.8 copy-done.9
  11.4 0.8 copy-done.11
  12.3 0.8 copy-done.13
  13.1 1.3 shard_map.122
  14.4 1.9 collective-permute-start
  16.4 1.8 collective-permute-done.send
  18.2 0.8 shard_map.123
  19.0 21.9 %all_to_all.15.refs_1_ = f32[4,256,256]{2,1,0:T(8,128)S(1)} all-to-all(f32[4,256,256]{2,1,0:T(8,128)S(1)} %get-tuple-element.30), channel_id=1, replica_groups=mesh['zh'=4,'zl'=4,'x'=4,'c'=2,'y'=4] {'x'}, dimensions={0} | all-to-all | bytes 2097152 | tf_op jit(solution)/shard_map/all_to_all | solution.py:268
  40.9 2.2 shard_map.124
  43.1 0.0 all-gather.11.cloned.1.call-start
  43.1 38.9 %all-gather.9.cloned.1.call-done = f32[1024,256]{1,0:T(8,128)} async-done(((f32[256,256]{1,0:T(8,128)}), f32[1024,256]{1,0:T(8,128)}) %all-gather.9.cloned.1.call-update) | async-done | bytes 1048592 | tf_op jit(solution)/shard_map/all_gather | solution.py:278
  82.1 1.2 copy-done
  83.3 2.2 shard_map.125
  85.5 59.6 %all-gather.11.cloned.1.call-done = f32[1024,256]{1,0:T(8,128)} async-done(((f32[256,256]{1,0:T(8,128)}), f32[1024,256]{1,0:T(8,128)}) %all-gather.11.cloned.1.call-update) | async-done | bytes 1048592 | tf_op jit(solution)/shard_map/all_gather | solution.py:280
  145.1 1.2 copy-done.1
  146.3 1.1 shard_map.126
  147.5 10.2 %all_to_all.16.parts = f32[4,64,128]{2,1,0:T(8,128)S(1)} all-to-all(f32[4,64,128]{2,1,0:T(8,128)S(1)} %get-tuple-element.33), channel_id=1, replica_groups=mesh['zh'=4,'zl'=4,'x'=4,'c'=2,'y'=4] {'y'}, dimensions={0} | all-to-all | bytes 262144 | tf_op jit(solution)/shard_map/all_to_all | solution.py:284
  157.7 10.8 %all_to_all.17.sums = f32[8,64,128]{2,1,0:T(8,128)S(1)} all-to-all(f32[8,64,128]{2,1,0:T(8,128)S(1)} %shard_map.127), channel_id=1, replica_groups=mesh['zh'=4,'zl'=4,'x'=4,'c'=2,'y'=4] {'x','c'}, dimensions={0} | all-to-all | bytes 524288 | tf_op jit(solution)/shard_map/all_to_all | solution.py:286
  168.6 3.2 %shard_map.128 = (f32[512,1]{1,0:T(8,128)S(1)}, f32[2,128,128]{2,1,0:T(8,128)S(1)}, f32[128,128]{1,0:T(8,128)S(1)}) custom-call(s32[6]{0:T(128)S(1)} %stack.23.where.refs_0_, f32[8,64,128]{2,1,0:T(8,128)S(1)} %all_to_all.17.sums, bf16[512,128]{1,0:T(8,128)(2,1)S(1)} %copy-done.16, bf16[512,512]{1,0:T(8,128)(2,1)S(1)} %copy-done.6, ...), custom_call_target="tpu_custom_call" | custom-call | tf_op jit(solution)/shard_map/pallas_call | solution.py:232
  171.8 0.7 copy.13
  172.5 1.9 all-gather.2
  174.4 0.2 shard_map.129
  174.5 12.3 %all-gather.3 = f32[512,128]{1,0:T(8,128)S(1)} all-gather(f32[128,128]{1,0:T(8,128)S(1)} %shard_map.129), channel_id=5, replica_groups=mesh['zh'=4,'zl'=4,'x'=4,'c'=2,'y'=4] {'x'}, dimensions={0}, use_global_device_ids=true | all-gather | bytes 327680 | tf_op jit(solution)/shard_map/all_gather | solution.py:298
  186.8 0.3 shard_map.130
  187.1 14.3 %all-gather.4 = f32[512,128]{1,0:T(8,128)S(1)} all-gather(f32[128,128]{1,0:T(8,128)S(1)} %get-tuple-element.40), channel_id=6, replica_groups=mesh['zh'=4,'zl'=4,'x'=4,'c'=2,'y'=4] {'zl'}, dimensions={0}, use_global_device_ids=true | all-gather | bytes 327680 | tf_op jit(solution)/shard_map/all_gather | solution.py:300
  201.4 0.3 shard_map.131
  201.7 19.8 %all-gather.5 = f32[512,128]{1,0:T(8,128)S(1)} all-gather(f32[128,128]{1,0:T(8,128)S(1)} %get-tuple-element.42), channel_id=7, replica_groups=mesh['zh'=4,'zl'=4,'x'=4,'c'=2,'y'=4] {'zh'}, dimensions={0}, use_global_device_ids=true | all-gather | bytes 327680 | tf_op jit(solution)/shard_map/all_gather | solution.py:302
  221.6 2.2 shard_map.132
  (30 shorter events, 0.1 us)
Async XLA Ops:
  7.2 74.9 %all-gather.9.cloned.1.call-start = ((), (), s32[]{:S(2)}) async-start(), calls=%async_computation.3 | async-start | bytes 1310720 | tf_op jit(solution)/shard_map/all_gather | solution.py:278
  7.9 0.8 copy-start.2
  8.8 0.8 copy-start.4
  9.6 0.9 copy-start.8
  10.6 0.8 copy-start.9
  11.4 0.8 copy-start.11
  12.3 0.8 copy-start.13
  14.4 3.7 %collective-permute-start = (f32[448,256]{1,0:T(8,128)S(1)}, f32[448,256]{1,0:T(8,128)S(1)}, u32[]{:S(2)}, u32[]{:S(2)}) collective-permute-start(f32[448,256]{1,0:T(8,128)S(1)} %get-tuple-element.28), channel_id=1, source_target_pairs={{0,4},{4,0},{1,5},{5,1},{2,6},{6,2},{3,7},{7,3},{8,12},{12,8},{9,1... | collective-permute-start | bytes 1376264 | tf_op jit(solution)/shard_map/ppermute | solution.py:264
  43.1 102.0 %all-gather.11.cloned.1.call-start = ((), (), s32[]{:S(2)}) async-start(), calls=%async_computation.4 | async-start | bytes 1310720 | tf_op jit(solution)/shard_map/all_gather | solution.py:280
  82.0 1.2 copy-start
  145.1 1.2 copy-start.1
  146.3 22.2 %copy-start.10 = (bf16[1,2,128,128]{3,2,1,0:T(8,128)(2,1)S(1)}, bf16[1,2,128,128]{3,2,1,0:T(8,128)(2,1)}, u32[]{:S(2)}) copy-start(bf16[1,2,128,128]{3,2,1,0:T(8,128)(2,1)} %linv.3) | copy-start | bytes 196612
  146.3 22.2 %copy-start.12 = (bf16[1,2,128,128]{3,2,1,0:T(8,128)(2,1)S(1)}, bf16[1,2,128,128]{3,2,1,0:T(8,128)(2,1)}, u32[]{:S(2)}) copy-start(bf16[1,2,128,128]{3,2,1,0:T(8,128)(2,1)} %llink.3) | copy-start | bytes 196612
  146.3 22.2 %copy-start.14 = (bf16[1,2,128,128]{3,2,1,0:T(8,128)(2,1)S(1)}, bf16[1,2,128,128]{3,2,1,0:T(8,128)(2,1)}, u32[]{:S(2)}) copy-start(bf16[1,2,128,128]{3,2,1,0:T(8,128)(2,1)} %rhs.3) | copy-start | bytes 196612
  146.3 22.2 %copy-start.15 = (bf16[1,2,128,512]{3,2,1,0:T(8,128)(2,1)S(1)}, bf16[1,2,128,512]{3,2,1,0:T(8,128)(2,1)}, u32[]{:S(2)}) copy-start(bf16[1,2,128,512]{3,2,1,0:T(8,128)(2,1)} %uroot.1) | copy-start | bytes 786436
  146.3 22.2 %copy-start.16 = (bf16[512,128]{1,0:T(8,128)(2,1)S(1)}, bf16[512,128]{1,0:T(8,128)(2,1)}, u32[]{:S(2)}) copy-start(bf16[512,128]{1,0:T(8,128)(2,1)} %rhs_root.1) | copy-start | bytes 393220
  147.5 21.1 %copy-start.7 = (bf16[512,512]{1,0:T(8,128)(2,1)S(1)}, bf16[512,512]{1,0:T(8,128)(2,1)}, u32[]{:S(2)}) copy-start(bf16[512,512]{1,0:T(8,128)(2,1)} %root_upper.1) | copy-start | bytes 1572868
  157.7 10.9 %copy-start.6 = (bf16[512,512]{1,0:T(8,128)(2,1)S(1)}, bf16[512,512]{1,0:T(8,128)(2,1)}, u32[]{:S(2)}) copy-start(bf16[512,512]{1,0:T(8,128)(2,1)} %root_lower.1) | copy-start | bytes 1572868
  157.7 10.9 %copy-start.3 = (bf16[1,2,128,128]{3,2,1,0:T(8,128)(2,1)S(1)}, bf16[1,2,128,128]{3,2,1,0:T(8,128)(2,1)}, u32[]{:S(2)}) copy-start(bf16[1,2,128,128]{3,2,1,0:T(8,128)(2,1)} %uinv.5) | copy-start | bytes 196612
  157.7 10.9 %copy-start.5 = (bf16[1,2,128,128]{3,2,1,0:T(8,128)(2,1)S(1)}, bf16[1,2,128,128]{3,2,1,0:T(8,128)(2,1)}, u32[]{:S(2)}) copy-start(bf16[1,2,128,128]{3,2,1,0:T(8,128)(2,1)} %ulink.5) | copy-start | bytes 196612
Sparse Core Ops, SparseCore 0:
  43.2 38.7 all-gather.8
  85.6 59.4 all-gather.10

commit v2 on v1

v2 whole, which is shorter than its diff:
```python
import jax
import jax.numpy as jnp
from jax import lax
from jax.experimental import pallas as pl
from jax.experimental.pallas import tpu as pltpu
from jax.sharding import Mesh
from jax.sharding import PartitionSpec as P

W = 128
F32 = jnp.float32
BF16 = jnp.bfloat16
CHAIN = ("zh", "zl", "x", "c")


def dot(left, right):
    return jnp.dot(left, right, preferred_element_type=F32)


def halves(value):
    high = value.astype(BF16)
    return high, (value - high.astype(F32)).astype(BF16)


def mul2(exact, right):
    high, low = halves(right)
    return dot(exact, high) + dot(exact, low)


def mul3(left, right):
    left_high, left_low = halves(left)
    right_high, right_low = halves(right)
    return dot(
        jnp.concatenate([left_high, left_low, left_high], 1),
        jnp.concatenate([right_high, right_high, right_low], 0),
    )


def shift(offset):
    return jnp.concatenate([jnp.zeros_like(offset), offset], 1)


def pack(square):
    return jnp.concatenate([square[: W // 2], square[W // 2 :]], 1)


def unpack(packed):
    return jnp.concatenate([packed[:, :W], packed[:, W:]], 0)


def eye():
    rows = lax.broadcasted_iota(jnp.int32, (W, W), 0)
    cols = lax.broadcasted_iota(jnp.int32, (W, W), 1)
    return jnp.where(rows == cols, F32(1), F32(0))


def copy_all(pairs, sems):
    copies = [
        pltpu.make_async_copy(source, target, sems.at[k])
        for k, (source, target) in enumerate(pairs)
    ]
    for copy in copies:
        copy.start()
    for copy in copies:
        copy.wait()


def slots_kernel(
    where, linv_in, llink_in, rhs_in, uinv_in, ulink_in, lroot_in, own, keep, send,
    linv, llink, rhs, uinv, ulink, lroot, sems,
):
    sources = (linv_in, llink_in, rhs_in, uinv_in, ulink_in, lroot_in)
    copy_all(list(zip(sources, (linv, llink, rhs, uinv, ulink, lroot))), sems)
    core, both = where[3], where[5] == 2
    maps = []
    for slot in range(2):
        made = dot(linv[0, slot], jnp.concatenate([llink[0, slot], rhs[0, slot]], 1))
        maps.append(jnp.concatenate([-made[:, :W], made[:, W:]], 1))
    chain = mul3(maps[1][:, :W], maps[0]) + shift(maps[1][:, W:])
    chain = jnp.where(both, chain, maps[0])
    back = [-dot(uinv[0, slot], ulink[0, slot]) for slot in range(2)]
    back = pack(jnp.where(both, mul3(back[0], back[1]), back[0]).T)
    own[:W] = chain
    own[W:] = back
    send[:W] = chain
    send[W : W + W // 2] = back
    for half, target, at in ((core, keep, 0), (1 - core, send, W + W // 2)):
        rows = pl.ds(pl.multiple_of(half * 256, 256), 256)
        second = jnp.where(both, mul2(lroot[0, 1, rows], chain), F32(0))
        target[at : at + 256] = mul2(lroot[0, 0, rows], maps[0]) + second


def chip_kernel(where, own, keep, send, out, early):
    first = where[3] == 0
    mine, theirs = own[:W], send[:W]
    head = jnp.where(first, mine, theirs)
    tail = jnp.where(first, theirs, mine)
    chain = mul3(tail[:, :W], head) + shift(tail[:, W:])
    back_mine, back_theirs = own[W:], send[W : W + W // 2]
    back_head = jnp.where(first, back_mine, back_theirs)
    back_tail = jnp.where(first, back_theirs, back_mine)
    root_mine, root_theirs = keep[...], send[W + W // 2 :]
    root_head = jnp.where(first, root_mine, root_theirs)
    root_tail = jnp.where(first, root_theirs, root_mine)
    root = root_head + mul3(root_tail[:, :W], head) + shift(root_tail[:, W:])
    early[...] = head
    for other in range(4):
        out[other, :128] = chain
        out[other, 128:192] = back_head
        out[other, 192:256] = back_tail
        out[other, 256:] = root[64 * other : 64 * other + 64]


def compose(place, maps, roots):
    prefix = maps[0]
    prefixes = [prefix]
    root = roots[0]
    for k in range(1, 4):
        stacked = mul3(jnp.concatenate([maps[k][:, :W], roots[k][:, :W]], 0), prefix)
        prefix = stacked[:W] + shift(maps[k][:, W:])
        root = root + stacked[W:] + shift(roots[k][:, W:])
        prefixes.append(prefix)
    start = jnp.concatenate([eye(), jnp.zeros((W, W), F32)], 1)
    before = jnp.where(
        place == 0,
        start,
        jnp.where(place == 1, prefixes[0], jnp.where(place == 2, prefixes[1], prefixes[2])),
    )
    return prefix, root, before


def plane_kernel(where, parts, out, before, backs, back):
    maps = [parts[k, :128] for k in range(4)]
    roots = [parts[k, 256:] for k in range(4)]
    chain, root, prefix = compose(where[2], maps, roots)
    before[...] = prefix
    out[:64] = jnp.where(where[3] == 0, chain[:64], chain[64:])
    out[64:] = root
    every = []
    for k in range(4):
        every += [unpack(parts[k, 128:192]), unpack(parts[k, 192:256])]
    for k in range(8):
        backs[k] = every[k]
    while len(every) > 1:
        every = [mul3(every[k + 1], every[k]) for k in range(0, len(every), 2)]
    back[...] = every[0]


def group_kernel(where, parts, pieces, out, before):
    maps = [jnp.concatenate([pieces[0, k], pieces[1, k]], 0) for k in range(4)]
    roots = [parts[k, 64:] for k in range(4)]
    chain, root, prefix = compose(where[1], maps, roots)
    before[...] = prefix
    out[:64] = jnp.where(where[3] == 0, chain[:64], chain[64:])
    out[64:] = root


def top_kernel(where, parts, pieces, root, carry):
    place = where[0]
    maps = [jnp.concatenate([pieces[0, k], pieces[1, k]], 0) for k in range(4)]
    roots = [parts[k, 64:] for k in range(4)]
    total = roots[0][:, W:]
    state = maps[0][:, W:]
    states = [jnp.zeros((W, W), F32), state]
    for k in range(1, 4):
        stacked = mul3(jnp.concatenate([maps[k][:, :W], roots[k][:, :W]], 0), state)
        total = total + stacked[W:] + roots[k][:, W:]
        state = stacked[:W] + maps[k][:, W:]
        states.append(state)
    carry[...] = jnp.where(
        place == 0,
        states[0],
        jnp.where(place == 1, states[1], jnp.where(place == 2, states[2], states[3])),
    )
    for other in range(4):
        root[other] = total


def sum_kernel(parts, out):
    total = (parts[0] + parts[1]) + (parts[2] + parts[3])
    for other in range(8):
        out[other] = total


def root_kernel(
    where, sums, rhs_root, root_lower, root_upper, carry, before_low, before_x, early,
    linv, llink, rhs, uinv, ulink, uroot, own_root, plain, offset,
):
    core, both = where[3], where[5] == 2
    summed = jnp.concatenate([sums[2 * (k % 4) + k // 4] for k in range(8)], 0)
    inner = mul2(root_lower[...], rhs_root[...].astype(F32) - summed)
    root = mul2(root_upper[...], inner)
    lanes = lax.broadcasted_iota(jnp.int32, (512, W), 1)
    own_root[...] = jnp.sum(jnp.where(lanes == where[4], root, F32(0)), 1, keepdims=True)
    state = carry[...]
    for ref in (before_low, before_x):
        state = mul3(ref[:, :W], state) + ref[:, W:]
    state = jnp.where(core == 0, state, mul3(early[:, :W], state) + early[:, W:])
    root_high, root_low = halves(root)
    offsets = []
    for slot in range(2):
        state = mul2(
            linv[0, slot], rhs[0, slot].astype(F32) - mul2(llink[0, slot], state)
        )
        inner = state - (dot(uroot[0, slot], root_high) + dot(uroot[0, slot], root_low))
        offsets.append(mul2(uinv[0, slot], inner))
    link = -dot(uinv[0, 0], ulink[0, 0])
    plain[0] = offsets[0]
    plain[1] = offsets[1]
    turned = jnp.where(both, offsets[0] + mul3(link, offsets[1]), offsets[0]).T
    for other in range(8):
        offset[other] = turned[16 * other : 16 * other + 16]


def plane_offset_kernel(parts, backs, out):
    state = parts[7]
    for k in reversed(range(7)):
        state = parts[k] + mul3(state, backs[k])
    for other in range(16):
        out[other] = state


def carry_kernel(where, planes, plane_backs, parts, backs, out):
    place = where[0] * 4 + where[1]
    state = jnp.zeros((16, W), F32)
    for k in reversed(range(1, 16)):
        state = jnp.where(place < k, planes[k] + mul3(state, plane_backs[k]), state)
    for k in reversed(range(8)):
        out[k] = state
        if k:
            state = parts[k] + mul3(state, backs[k])


def answer_kernel(where, parts, plain, uinv, ulink, out):
    both = where[5] == 2
    state = jnp.concatenate([parts[k] for k in range(8)], 0).T
    links = [-dot(uinv[0, slot], ulink[0, slot]) for slot in range(2)]
    last = mul3(links[1], state) + plain[1]
    state = jnp.where(both, last, state)
    out[0, 1] = jnp.where(both, last, F32(0))
    out[0, 0] = mul3(links[0], state) + plain[0]


def call(kernel, inputs, shapes, fetched=False):
    vmem = pl.BlockSpec(memory_space=pltpu.VMEM)
    smem = pl.BlockSpec(memory_space=pltpu.SMEM)
    block = pl.BlockSpec(memory_space=pltpu.HBM) if fetched else vmem
    scratch = []
    if fetched:
        scratch = [pltpu.VMEM(a.shape, a.dtype) for a in inputs if a.dtype == BF16]
        scratch.append(pltpu.SemaphoreType.DMA((len(scratch),)))
    return pl.pallas_call(
        kernel,
        out_shape=[jax.ShapeDtypeStruct(shape, F32) for shape in shapes],
        in_specs=[
            smem if a.dtype == jnp.int32 else block if a.dtype == BF16 else vmem for a in inputs
        ],
        out_specs=[vmem] * len(shapes),
        scratch_shapes=scratch,
        compiler_params=pltpu.CompilerParams(vmem_limit_bytes=32 * 1024 * 1024),
    )(*inputs)


def on_device(
    lower_inverse,
    upper_inverse,
    lower_link,
    upper_link,
    lower_root,
    upper_root,
    rhs_blocks,
    rhs_root,
    root_lower_inverse,
    root_upper_inverse,
    live_counts,
):
    places = [lax.axis_index(name) for name in CHAIN]
    column = ((places[0] * 4 + places[1]) * 4 + places[2]) * 2 + places[3]
    where = jnp.stack(places + [column, live_counts[0, 0]]).astype(jnp.int32)
    square, wide = (W, W), (W, 2 * W)

    own, keep, send = call(
        slots_kernel,
        [where, lower_inverse, lower_link, rhs_blocks, upper_inverse, upper_link, lower_root],
        [(192, 256), (256, 256), (448, 256)],
        fetched=True,
    )
    send = lax.ppermute(send, "c", [(0, 1), (1, 0)])
    out, early = call(chip_kernel, [where, own, keep, send], [(4, 320, 256), wide])
    parts = lax.all_to_all(out, "x", 0, 0, tiled=True)
    out, before_x, backs, back = call(
        plane_kernel, [where, parts], [(128, 256), wide, (8,) + square, square]
    )
    plane_backs = lax.all_gather(back, ("zh", "zl"))
    parts = lax.all_gather(out, "zl")
    pieces = lax.all_gather(parts[:, :64], "c")
    out, before_low = call(group_kernel, [where, parts, pieces], [(128, 256), wide])
    parts = lax.all_gather(out, "zh")
    pieces = lax.all_gather(parts[:, :64], "c")
    root, carry = call(top_kernel, [where, parts, pieces], [(4, 64, W), square])
    parts = lax.all_to_all(root, "y", 0, 0, tiled=True)
    (root,) = call(sum_kernel, [parts], [(8, 64, W)])
    sums = lax.all_to_all(root, ("x", "c"), 0, 0, tiled=True)
    own_root, plain, offset = call(
        root_kernel,
        [
            where, sums, rhs_root, root_lower_inverse, root_upper_inverse, carry, before_low,
            before_x, early, lower_inverse, lower_link, rhs_blocks, upper_inverse, upper_link,
            upper_root,
        ],
        [(512, 1), (2,) + square, (8, 16, W)],
    )
    parts = lax.all_to_all(offset, ("x", "c"), 0, 0, tiled=True)
    (offset,) = call(plane_offset_kernel, [parts, backs], [(16, 16, W)])
    planes = lax.all_to_all(offset, ("zh", "zl"), 0, 0, tiled=True)
    (states,) = call(
        carry_kernel, [where, planes, plane_backs, parts, backs], [(8, 16, W)]
    )
    states = lax.all_to_all(states, ("x", "c"), 0, 0, tiled=True)
    (answers,) = call(
        answer_kernel, [where, states, plain, upper_inverse, upper_link], [(1, 2, W, W)]
    )
    return answers, own_root


def solution(mesh):
    fine = Mesh(mesh.devices.reshape(4, 4, 4, 2, 4), CHAIN + ("y",))
    split = P("y", CHAIN)
    return jax.shard_map(
        on_device,
        mesh=fine,
        in_specs=(split,) * 7 + (P(), P(), P(), split),
        out_specs=(split, P(None, CHAIN)),
        check_vma=False,
    )
```

time: 231 us -> 181 us (0.78); the launches traced: 231 us -> 178 us
  waiting for transfers between devices: 100 us -> 4.64 us
  blocking collectives: 91.1 us -> 127 us
  starting transfers between devices: 2 us -> 7.32 us
  Pallas kernels: 13.9 us -> 16.8 us
    all_gather x2 -> x1, waiting for transfers between devices: 98.5 us -> 0.01 us  [on_device(): plane_backs = lax.all_gather(back, ('zh', 'zl'))]
    all_to_all x0 -> x2, blocking collectives: none -> 29.1 us  [the longest x1 21.1 us: on_device(): planes = lax.all_to_all(offset, ('zh', 'zl'), 0, 0, tiled=True)]
    all_to_all x0 -> x1, starting transfers between devices: none -> 5.36 us  [on_device(): states = lax.all_to_all(states, ('x', 'c'), 0, 0, tiled=True)]
    all_gather x4, blocking collectives: 48.3 us -> 52.7 us  [the longest x1 32.5 us: on_device(): parts = lax.all_gather(out, 'zh')]
    pallas_call x11 -> x10, Pallas kernels: 13.9 us -> 16.8 us  [call(): pl.pallas_call(kernel, out_shape=[jax.ShapeDtypeStruct(shape, F32) for sh...]
    all_to_all x0 -> x1, waiting for transfers between devices: none -> 2.84 us  [on_device(): states = lax.all_to_all(states, ('x', 'c'), 0, 0, tiled=True)]
    all_to_all x1, blocking collectives: 21.9 us -> 24.7 us  [on_device(): parts = lax.all_to_all(out, 'x', 0, 0, tiled=True)]
    unnamed x35 -> x33, local copies, waits for them, and re-layouts: 8.33 us -> 7.11 us
  transfers between devices with their start and end apart: 3 -> 3, of which waited for: 3 -> 2; matrix products, arithmetic and copies ran while one was open for 0% -> 0% of each run, Pallas kernels for 0% -> 4%
where the time goes in v2:
time: 181 us; the launch traced here: 178 us
  blocking collectives  127 us (70%)
  Pallas kernels  16.8 us (9%)
  between operations  14.9 us (8%)
  starting transfers between devices  7.32 us (4%)
  local copies, waits for them, and re-layouts  7.23 us (4%)
  waiting for transfers between devices  4.64 us (3%)
    all_gather x1, blocking collectives, on_device(): parts = lax.all_gather(out, 'zh')  32.5 us
    all_to_all x1, blocking collectives, on_device(): parts = lax.all_to_all(out, 'x', 0, 0, tiled=True)  24.7 us
    all_to_all x1, blocking collectives, on_device(): planes = lax.all_to_all(offset, ('zh', 'zl'), 0, 0, tiled=True)  21.1 us
    pallas_call x10, Pallas kernels, call(): pl.pallas_call(kernel, out_shape=[jax.ShapeDtypeStruct(shape, F32) for sh...  16.8 us
    all_gather x1, blocking collectives, on_device(): parts = lax.all_gather(out, 'zl')  15.8 us
    all_to_all x1, blocking collectives, on_device(): parts = lax.all_to_all(root, 'y', 0, 0, tiled=True)  11 us
    all_to_all x1, blocking collectives, on_device(): sums = lax.all_to_all(root, ('x', 'c'), 0, 0, tiled=True)  9.78 us
    all_to_all x1, blocking collectives, on_device(): parts = lax.all_to_all(offset, ('x', 'c'), 0, 0, tiled=True)  7.99 us
  transfers between devices with their start and end apart: 3, of which 2 were waited for; matrix products, arithmetic and copies ran while one was open for 0% of the time, Pallas kernels for 4%

profile of v2, /device:TPU:6, one launch (start us, length us, event | category | flops | bytes accessed | tf_op | source)
XLA Modules:
  0.0 178.2 jit_solution(211699275278337650)
XLA Ops:
  7.2 0.0 all-gather.7.cloned.1.call-start
  7.9 0.1 stack.23.where
  8.0 0.8 copy-done.1
  8.8 0.8 copy-done.3
  9.6 0.9 copy-done.7
  10.6 0.8 copy-done.8
  11.4 0.8 copy-done.10
  12.3 0.8 copy-done.12
  13.1 1.8 %shard_map.122 = (f32[192,256]{1,0:T(8,128)S(1)}, f32[256,256]{1,0:T(8,128)S(1)}, f32[448,256]{1,0:T(8,128)S(1)}) custom-call(s32[6]{0:T(128)S(1)} %stack.23.where, bf16[1,2,128,128]{3,2,1,0:T(8,128)(2,1)S(1)} %copy-done.8, bf16[1,2,128,128]{3,2,1,0:T(8,128)(2,1)S(1)} %copy-done.10, bf16[1,2,128,128]{3,2,1,0:T(8,128)(2,1)S(1)} %copy-done.12, ...), custom_call_target="tpu_custom_call" | custom-call | tf_op jit(solution)/shard_map/pallas_call | solution.py:251
  14.9 1.9 %collective-permute-start = (f32[448,256]{1,0:T(8,128)S(1)}, f32[448,256]{1,0:T(8,128)S(1)}, u32[]{:S(2)}, u32[]{:S(2)}) collective-permute-start(f32[448,256]{1,0:T(8,128)S(1)} %get-tuple-element.20), channel_id=1, source_target_pairs={{0,4},{4,0},{1,5},{5,1},{2,6},{6,2},{3,7},{7,3},{8,12},{12,8},{9,1... | collective-permute-start | bytes 1376264 | tf_op jit(solution)/shard_map/ppermute | solution.py:287
  16.9 1.8 %collective-permute-done.send = f32[448,256]{1,0:T(8,128)S(1)} collective-permute-done((f32[448,256]{1,0:T(8,128)S(1)}, f32[448,256]{1,0:T(8,128)S(1)}, u32[]{:S(2)}, u32[]{:S(2)}) %collective-permute-start) | collective-permute-done | bytes 458784 | tf_op jit(solution)/shard_map/ppermute | solution.py:287
  18.7 0.8 shard_map.123
  19.5 24.7 %all_to_all.30.parts = f32[4,320,256]{2,1,0:T(8,128)S(1)} all-to-all(f32[4,320,256]{2,1,0:T(8,128)S(1)} %get-tuple-element.21), channel_id=1, replica_groups=mesh['zh'=4,'zl'=4,'x'=4,'c'=2,'y'=4] {'x'}, dimensions={0} | all-to-all | bytes 2621440 | tf_op jit(solution)/shard_map/all_to_all | solution.py:289
  44.2 2.2 %shard_map.124 = (f32[128,256]{1,0:T(8,128)S(1)}, f32[128,256]{1,0:T(8,128)S(1)}, f32[8,128,128]{2,1,0:T(8,128)S(1)}, f32[128,128]{1,0:T(8,128)}) custom-call(s32[6]{0:T(128)S(1)} %stack.23.where, f32[4,320,256]{2,1,0:T(8,128)S(1)} %all_to_all.30.parts), custom_call_target="tpu_custom_call" | custom-call | tf_op jit(solution)/shard_map/pallas_call | solution.py:251
  46.4 15.8 %all-gather = f32[512,256]{1,0:T(8,128)S(1)} all-gather(f32[128,256]{1,0:T(8,128)S(1)} %get-tuple-element.22), channel_id=2, replica_groups=mesh['zh'=4,'zl'=4,'x'=4,'c'=2,'y'=4] {'zl'}, dimensions={0}, use_global_device_ids=true | all-gather | bytes 655360 | tf_op jit(solution)/shard_map/all_gather | solution.py:294
  62.3 2.2 %all-gather.1 = f32[8,64,256]{2,1,0:T(8,128)S(1)} all-gather(f32[4,64,256]{2,1,0:T(8,128)S(1)} %slice.8), channel_id=3, replica_groups=mesh['zh'=4,'zl'=4,'x'=4,'c'=2,'y'=4] {'c'}, dimensions={0}, use_global_device_ids=true | all-gather | bytes 786432 | tf_op jit(solution)/shard_map/all_gather | solution.py:295
  64.4 1.2 shard_map.125
  65.6 32.5 %all-gather.2 = f32[512,256]{1,0:T(8,128)S(1)} all-gather(f32[128,256]{1,0:T(8,128)S(1)} %get-tuple-element.23), channel_id=4, replica_groups=mesh['zh'=4,'zl'=4,'x'=4,'c'=2,'y'=4] {'zh'}, dimensions={0}, use_global_device_ids=true | all-gather | bytes 655360 | tf_op jit(solution)/shard_map/all_gather | solution.py:297
  98.2 2.2 %all-gather.3 = f32[8,64,256]{2,1,0:T(8,128)S(1)} all-gather(f32[4,64,256]{2,1,0:T(8,128)S(1)} %slice.9), channel_id=5, replica_groups=mesh['zh'=4,'zl'=4,'x'=4,'c'=2,'y'=4] {'c'}, dimensions={0}, use_global_device_ids=true | all-gather | bytes 786432 | tf_op jit(solution)/shard_map/all_gather | solution.py:298
  100.5 1.1 shard_map.126
  101.5 11.0 %all_to_all.31.parts = f32[4,64,128]{2,1,0:T(8,128)S(1)} all-to-all(f32[4,64,128]{2,1,0:T(8,128)S(1)} %get-tuple-element.24), channel_id=1, replica_groups=mesh['zh'=4,'zl'=4,'x'=4,'c'=2,'y'=4] {'y'}, dimensions={0} | all-to-all | bytes 262144 | tf_op jit(solution)/shard_map/all_to_all | solution.py:300
  112.6 9.8 %all_to_all.32.sums = f32[8,64,128]{2,1,0:T(8,128)S(1)} all-to-all(f32[8,64,128]{2,1,0:T(8,128)S(1)} %shard_map.127), channel_id=1, replica_groups=mesh['zh'=4,'zl'=4,'x'=4,'c'=2,'y'=4] {'x','c'}, dimensions={0} | all-to-all | bytes 524288 | tf_op jit(solution)/shard_map/all_to_all | solution.py:302
  122.4 3.3 %shard_map.128 = (f32[512,1]{1,0:T(8,128)S(1)}, f32[2,128,128]{2,1,0:T(8,128)S(1)}, f32[8,16,128]{2,1,0:T(8,128)S(1)}) custom-call(s32[6]{0:T(128)S(1)} %stack.23.where, f32[8,64,128]{2,1,0:T(8,128)S(1)} %all_to_all.32.sums, bf16[512,128]{1,0:T(8,128)(2,1)S(1)} %copy-done.15, bf16[512,512]{1,0:T(8,128)(2,1)S(1)} %copy-done.5, ...), custom_call_target="tpu_custom_call" | custom-call | tf_op jit(solution)/shard_map/pallas_call | solution.py:251
  125.7 8.0 %all_to_all.33.parts = f32[8,16,128]{2,1,0:T(8,128)S(1)} all-to-all(f32[8,16,128]{2,1,0:T(8,128)S(1)} %get-tuple-element.29), channel_id=1, replica_groups=mesh['zh'=4,'zl'=4,'x'=4,'c'=2,'y'=4] {'x','c'}, dimensions={0} | all-to-all | bytes 131072 | tf_op jit(solution)/shard_map/all_to_all | solution.py:312
  133.7 0.9 shard_map.129
  134.6 21.1 %all_to_all.34.planes = f32[16,16,128]{2,1,0:T(8,128)S(1)} all-to-all(f32[16,16,128]{2,1,0:T(8,128)S(1)} %shard_map.129), channel_id=1, replica_groups=mesh['zh'=4,'zl'=4,'x'=4,'c'=2,'y'=4] {'zh','zl'}, dimensions={0} | all-to-all | bytes 262144 | tf_op jit(solution)/shard_map/all_to_all | solution.py:314
  155.6 1.2 copy-done
  156.9 3.9 %shard_map.130 = f32[8,16,128]{2,1,0:T(8,128)} custom-call(s32[6]{0:T(128)S(1)} %stack.23.where, f32[16,16,128]{2,1,0:T(8,128)S(1)} %all_to_all.34.planes, f32[16,128,128]{2,1,0:T(8,128)S(1)} %bitcast.18, f32[8,16,128]{2,1,0:T(8,128)S(1)} %all_to_all.33.parts, f32[8,128,128]{2,1,0:T(8,128)S(1)} %get-tuple-element.30.backs), custom_call_target="tpu_custom_call" | custom-call | tf_op jit(solution)/shard_map/pallas_call | solution.py:251
  160.8 5.4 %all-to-all-start.5 = ((f32[8,16,128]{2,1,0:T(8,128)}), f32[8,16,128]{2,1,0:T(8,128)S(1)}, u32[]{:S(2)}, u32[]{:S(2)}) async-start(f32[8,16,128]{2,1,0:T(8,128)} %shard_map.130), calls=%async_computation.5 | async-start | bytes 131072 | tf_op jit(solution)/shard_map/all_to_all | solution.py:318
  166.1 0.7 copy.14
  166.8 2.8 %all-to-all-done.5.parts = f32[8,16,128]{2,1,0:T(8,128)S(1)} async-done(((f32[8,16,128]{2,1,0:T(8,128)}), f32[8,16,128]{2,1,0:T(8,128)S(1)}, u32[]{:S(2)}, u32[]{:S(2)}) %all-to-all-start.5) | async-done | bytes 65568 | tf_op jit(solution)/shard_map/all_to_all | solution.py:318
  169.7 1.7 shard_map.131
  (30 shorter events, 0.1 us)
Async XLA Ops:
  7.2 148.5 %all-gather.7.cloned.1.call-start = ((), (), s32[]{:S(2)}) async-start(), calls=%async_computation.6 | async-start | bytes 1114112 | tf_op jit(solution)/shard_map/all_gather | solution.py:293
  7.9 0.8 copy-start.1
  8.8 0.8 copy-start.3
  9.6 0.9 copy-start.7
  10.6 0.8 copy-start.8
  11.4 0.8 copy-start.10
  12.3 0.8 copy-start.12
  14.9 3.7 %collective-permute-start = (f32[448,256]{1,0:T(8,128)S(1)}, f32[448,256]{1,0:T(8,128)S(1)}, u32[]{:S(2)}, u32[]{:S(2)}) collective-permute-start(f32[448,256]{1,0:T(8,128)S(1)} %get-tuple-element.20), channel_id=1, source_target_pairs={{0,4},{4,0},{1,5},{5,1},{2,6},{6,2},{3,7},{7,3},{8,12},{12,8},{9,1... | collective-permute-start | bytes 1376264 | tf_op jit(solution)/shard_map/ppermute | solution.py:287
  100.4 22.0 %copy-start.2 = (bf16[1,2,128,128]{3,2,1,0:T(8,128)(2,1)S(1)}, bf16[1,2,128,128]{3,2,1,0:T(8,128)(2,1)}, u32[]{:S(2)}) copy-start(bf16[1,2,128,128]{3,2,1,0:T(8,128)(2,1)} %uinv.3) | copy-start | bytes 196612
  100.4 22.0 %copy-start.4 = (bf16[1,2,128,128]{3,2,1,0:T(8,128)(2,1)S(1)}, bf16[1,2,128,128]{3,2,1,0:T(8,128)(2,1)}, u32[]{:S(2)}) copy-start(bf16[1,2,128,128]{3,2,1,0:T(8,128)(2,1)} %ulink.3) | copy-start | bytes 196612
  100.4 22.0 %copy-start.5 = (bf16[512,512]{1,0:T(8,128)(2,1)S(1)}, bf16[512,512]{1,0:T(8,128)(2,1)}, u32[]{:S(2)}) copy-start(bf16[512,512]{1,0:T(8,128)(2,1)} %root_lower.1) | copy-start | bytes 1572868
  100.4 22.0 %copy-start.6 = (bf16[512,512]{1,0:T(8,128)(2,1)S(1)}, bf16[512,512]{1,0:T(8,128)(2,1)}, u32[]{:S(2)}) copy-start(bf16[512,512]{1,0:T(8,128)(2,1)} %root_upper.1) | copy-start | bytes 1572868
  100.4 22.0 %copy-start.9 = (bf16[1,2,128,128]{3,2,1,0:T(8,128)(2,1)S(1)}, bf16[1,2,128,128]{3,2,1,0:T(8,128)(2,1)}, u32[]{:S(2)}) copy-start(bf16[1,2,128,128]{3,2,1,0:T(8,128)(2,1)} %linv.1) | copy-start | bytes 196612
  100.4 22.0 %copy-start.11 = (bf16[1,2,128,128]{3,2,1,0:T(8,128)(2,1)S(1)}, bf16[1,2,128,128]{3,2,1,0:T(8,128)(2,1)}, u32[]{:S(2)}) copy-start(bf16[1,2,128,128]{3,2,1,0:T(8,128)(2,1)} %llink.1) | copy-start | bytes 196612
  100.4 22.0 %copy-start.13 = (bf16[1,2,128,128]{3,2,1,0:T(8,128)(2,1)S(1)}, bf16[1,2,128,128]{3,2,1,0:T(8,128)(2,1)}, u32[]{:S(2)}) copy-start(bf16[1,2,128,128]{3,2,1,0:T(8,128)(2,1)} %rhs.1) | copy-start | bytes 196612
  100.4 22.0 %copy-start.14 = (bf16[1,2,128,512]{3,2,1,0:T(8,128)(2,1)S(1)}, bf16[1,2,128,512]{3,2,1,0:T(8,128)(2,1)}, u32[]{:S(2)}) copy-start(bf16[1,2,128,512]{3,2,1,0:T(8,128)(2,1)} %uroot.1) | copy-start | bytes 786436
  100.4 22.0 %copy-start.15 = (bf16[512,128]{1,0:T(8,128)(2,1)S(1)}, bf16[512,128]{1,0:T(8,128)(2,1)}, u32[]{:S(2)}) copy-start(bf16[512,128]{1,0:T(8,128)(2,1)} %rhs_root.1) | copy-start | bytes 393220
  155.6 1.2 copy-start
  160.8 8.9 %all-to-all-start.5 = ((f32[8,16,128]{2,1,0:T(8,128)}), f32[8,16,128]{2,1,0:T(8,128)S(1)}, u32[]{:S(2)}, u32[]{:S(2)}) async-start(f32[8,16,128]{2,1,0:T(8,128)} %shard_map.130), calls=%async_computation.5 | async-start | bytes 131072 | tf_op jit(solution)/shard_map/all_to_all | solution.py:318
Sparse Core Ops, SparseCore 0:
  46.5 76.1 all-gather.6

commit v3 on v2

--- a/solution.py
+++ b/solution.py
@@ -128,13 +128,16 @@
     return prefix, root, before
 
 
-def plane_kernel(where, parts, out, before, backs, back):
+def half(core, rows):
+    middle = rows.shape[0] // 2
+    return jnp.where(core == 0, rows[:middle], rows[middle:])
+
+
+def plane_kernel(where, parts, out, before, backs):
     maps = [parts[k, :128] for k in range(4)]
     roots = [parts[k, 256:] for k in range(4)]
     chain, root, prefix = compose(where[2], maps, roots)
     before[...] = prefix
-    out[:64] = jnp.where(where[3] == 0, chain[:64], chain[64:])
-    out[64:] = root
     every = []
     for k in range(4):
         every += [unpack(parts[k, 128:192]), unpack(parts[k, 192:256])]
@@ -142,22 +145,34 @@
         backs[k] = every[k]
     while len(every) > 1:
         every = [mul3(every[k + 1], every[k]) for k in range(0, len(every), 2)]
-    back[...] = every[0]
-
-
-def group_kernel(where, parts, pieces, out, before):
-    maps = [jnp.concatenate([pieces[0, k], pieces[1, k]], 0) for k in range(4)]
-    roots = [parts[k, 64:] for k in range(4)]
+    out[:64] = half(where[3], chain)
+    out[64:96] = half(where[3], pack(every[0]))
+    out[96:] = root
+
+
+def joined(pieces):
+    maps = [jnp.concatenate([pieces[0, k, :64], pieces[1, k, :64]], 0) for k in range(4)]
+    backs = [jnp.concatenate([pieces[0, k, 64:], pieces[1, k, 64:]], 0) for k in range(4)]
+    return maps, [unpack(packed) for packed in backs]
+
+
+def group_kernel(where, parts, pieces, out, before, backs):
+    maps, every = joined(pieces)
+    roots = [parts[k, 96:] for k in range(4)]
     chain, root, prefix = compose(where[1], maps, roots)
     before[...] = prefix
-    out[:64] = jnp.where(where[3] == 0, chain[:64], chain[64:])
-    out[64:] = root
-
-
-def top_kernel(where, parts, pieces, root, carry):
+    for k in range(4):
+        backs[k] = every[k]
+    back = mul3(mul3(every[3], every[2]), mul3(every[1], every[0]))
+    out[:64] = half(where[3], chain)
+    out[64:96] = half(where[3], pack(back))
+    out[96:] = root
+
+
+def top_kernel(where, parts, pieces, root, carry, backs):
     place = where[0]
-    maps = [jnp.concatenate([pieces[0, k], pieces[1, k]], 0) for k in range(4)]
-    roots = [parts[k, 64:] for k in range(4)]
+    maps, every = joined(pieces)
+    roots = [parts[k, 96:] for k in range(4)]
     total = roots[0][:, W:]
     state = maps[0][:, W:]
     states = [jnp.zeros((W, W), F32), state]
@@ -173,6 +188,7 @@
     )
     for other in range(4):
         root[other] = total
+        backs[other] = every[other]
 
 
 def sum_kernel(parts, out):
@@ -189,8 +205,8 @@
     summed = jnp.concatenate([sums[2 * (k % 4) + k // 4] for k in range(8)], 0)
     inner = mul2(root_lower[...], rhs_root[...].astype(F32) - summed)
     root = mul2(root_upper[...], inner)
-    lanes = lax.broadcasted_iota(jnp.int32, (512, W), 1)
-    own_root[...] = jnp.sum(jnp.where(lanes == where[4], root, F32(0)), 1, keepdims=True)
+    columns = lax.broadcasted_iota(jnp.int32, (W, 512), 0)
+    own_root[...] = jnp.sum(jnp.where(columns == where[4], root.T, F32(0)), 0, keepdims=True)
     state = carry[...]
     for ref in (before_low, before_x):
         state = mul3(ref[:, :W], state) + ref[:, W:]
@@ -211,19 +227,30 @@
         offset[other] = turned[16 * other : 16 * other + 16]
 
 
-def plane_offset_kernel(parts, backs, out):
+def offset_kernel(where, parts, backs, plane_backs, group_backs, out):
+    group, place = where[0], where[1]
     state = parts[7]
     for k in reversed(range(7)):
         state = parts[k] + mul3(state, backs[k])
-    for other in range(16):
-        out[other] = state
+    sent = state
+    for k in reversed(range(3)):
+        sent = jnp.where(place > k, mul3(sent, plane_backs[k]), sent)
+    for other in reversed(range(4)):
+        for k in range(4):
+            out[4 * other + k] = jnp.where(group == other, state, sent)
+        if other:
+            sent = jnp.where(group > other, mul3(sent, group_backs[other]), sent)
 
 
 def carry_kernel(where, planes, plane_backs, parts, backs, out):
-    place = where[0] * 4 + where[1]
+    group, place = where[0], where[1]
     state = jnp.zeros((16, W), F32)
-    for k in reversed(range(1, 16)):
-        state = jnp.where(place < k, planes[k] + mul3(state, plane_backs[k]), state)
+    for k in range(4, 16):
+        state = state + jnp.where(k // 4 > group, planes[k], F32(0))
+    for k in reversed(range(1, 4)):
+        state = jnp.where(
+            place < k, planes[4 * group + k] + mul3(state, plane_backs[k]), state
+        )
     for k in reversed(range(8)):
         out[k] = state
         if k:
@@ -248,6 +275,11 @@
     if fetched:
         scratch = [pltpu.VMEM(a.shape, a.dtype) for a in inputs if a.dtype == BF16]
         scratch.append(pltpu.SemaphoreType.DMA((len(scratch),)))
+    if fetched:
+        inputs = [
+            pltpu.with_memory_space_constraint(a, pltpu.HBM) if a.dtype == BF16 else a
+            for a in inputs
+        ]
     return pl.pallas_call(
         kernel,
         out_shape=[jax.ShapeDtypeStruct(shape, F32) for shape in shapes],
@@ -287,16 +319,19 @@
     send = lax.ppermute(send, "c", [(0, 1), (1, 0)])
     out, early = call(chip_kernel, [where, own, keep, send], [(4, 320, 256), wide])
     parts = lax.all_to_all(out, "x", 0, 0, tiled=True)
-    out, before_x, backs, back = call(
-        plane_kernel, [where, parts], [(128, 256), wide, (8,) + square, square]
-    )
-    plane_backs = lax.all_gather(back, ("zh", "zl"))
+    out, before_x, backs = call(
+        plane_kernel, [where, parts], [(160, 256), wide, (8,) + square]
+    )
     parts = lax.all_gather(out, "zl")
-    pieces = lax.all_gather(parts[:, :64], "c")
-    out, before_low = call(group_kernel, [where, parts, pieces], [(128, 256), wide])
+    pieces = lax.all_gather(parts[:, :96], "c")
+    out, before_low, low_backs = call(
+        group_kernel, [where, parts, pieces], [(160, 256), wide, (4,) + square]
+    )
     parts = lax.all_gather(out, "zh")
-    pieces = lax.all_gather(parts[:, :64], "c")
-    root, carry = call(top_kernel, [where, parts, pieces], [(4, 64, W), square])
+    pieces = lax.all_gather(parts[:, :96], "c")
+    root, carry, high_backs = call(
+        top_kernel, [where, parts, pieces], [(4, 64, W), square, (4,) + square]
+    )
     parts = lax.all_to_all(root, "y", 0, 0, tiled=True)
     (root,) = call(sum_kernel, [parts], [(8, 64, W)])
     sums = lax.all_to_all(root, ("x", "c"), 0, 0, tiled=True)
@@ -307,19 +342,19 @@
             before_x, early, lower_inverse, lower_link, rhs_blocks, upper_inverse, upper_link,
             upper_root,
         ],
-        [(512, 1), (2,) + square, (8, 16, W)],
+        [(1, 512), (2,) + square, (8, 16, W)],
     )
     parts = lax.all_to_all(offset, ("x", "c"), 0, 0, tiled=True)
-    (offset,) = call(plane_offset_kernel, [parts, backs], [(16, 16, W)])
+    (offset,) = call(
+        offset_kernel, [where, parts, backs, low_backs, high_backs], [(16, 16, W)]
+    )
     planes = lax.all_to_all(offset, ("zh", "zl"), 0, 0, tiled=True)
-    (states,) = call(
-        carry_kernel, [where, planes, plane_backs, parts, backs], [(8, 16, W)]
-    )
+    (states,) = call(carry_kernel, [where, planes, low_backs, parts, backs], [(8, 16, W)])
     states = lax.all_to_all(states, ("x", "c"), 0, 0, tiled=True)
     (answers,) = call(
         answer_kernel, [where, states, plain, upper_inverse, upper_link], [(1, 2, W, W)]
     )
-    return answers, own_root
+    return answers, own_root.reshape(512, 1)
 
 
 def solution(mesh):

time: 181 us -> 163 us (0.901)
  between operations: 14.9 us -> 1.44 us
  blocking collectives: 127 us -> 138 us
  local copies, waits for them, and re-layouts: 7.23 us -> 0.18 us
  starting transfers between devices: 7.32 us -> 1.92 us
  waiting for transfers between devices: 4.64 us -> 1.78 us
    all_to_all x0 -> x1, blocking collectives: none -> 8.01 us  [on_device(): states = lax.all_to_all(states, ('x', 'c'), 0, 0, tiled=True)]
    unnamed x33 -> x18, local copies, waits for them, and re-layouts: 7.11 us -> 0.05 us
    all_to_all x1 -> x0, starting transfers between devices: 5.36 us -> none  [on_device(): states = lax.all_to_all(states, ('x', 'c'), 0, 0, tiled=True)]
    all_to_all x1 -> x0, waiting for transfers between devices: 2.84 us -> none  [on_device(): states = lax.all_to_all(states, ('x', 'c'), 0, 0, tiled=True)]
    all_gather x1, blocking collectives: 32.5 us -> 34.7 us  [on_device(): parts = lax.all_gather(out, 'zh')]
  transfers between devices with their start and end apart: 3 -> 1, of which waited for: 2 -> 1; matrix products, arithmetic and copies ran while one was open for 0% -> 0% of each run, Pallas kernels for 4% -> 0%
where the time goes in v3:
time: 163 us; the launch traced here: 160 us
  blocking collectives  138 us (85%)
  Pallas kernels  16.5 us (10%)
  starting transfers between devices  1.92 us (1%)
  waiting for transfers between devices  1.78 us (1%)
    all_gather x1, blocking collectives, on_device(): parts = lax.all_gather(out, 'zh')  34.7 us
    all_to_all x1, blocking collectives, on_device(): parts = lax.all_to_all(out, 'x', 0, 0, tiled=True)  24.7 us
    all_to_all x1, blocking collectives, on_device(): planes = lax.all_to_all(offset, ('zh', 'zl'), 0, 0, tiled=True)  21.4 us
    all_gather x1, blocking collectives, on_device(): parts = lax.all_gather(out, 'zl')  16.8 us
    pallas_call x10, Pallas kernels, call(): pl.pallas_call(kernel, out_shape=[jax.ShapeDtypeStruct(shape, F32) for sh...  16.5 us
    all_to_all x1, blocking collectives, on_device(): parts = lax.all_to_all(root, 'y', 0, 0, tiled=True)  9.91 us
    all_to_all x1, blocking collectives, on_device(): sums = lax.all_to_all(root, ('x', 'c'), 0, 0, tiled=True)  9.82 us
    all_to_all x1, blocking collectives, on_device(): states = lax.all_to_all(states, ('x', 'c'), 0, 0, tiled=True)  8.01 us
  transfers between devices with their start and end apart: 1, of which 1 were waited for; matrix products, arithmetic and copies ran while one was open for 0% of the time, Pallas kernels for 0%

profile of v3, /device:TPU:6, one launch (start us, length us, event | category | flops | bytes accessed | tf_op | source)
XLA Modules:
  0.0 160.0 jit_solution(10043862227086823589)
XLA Ops:
  1.3 0.1 stack.23.where
  1.4 2.5 %shard_map.122 = (f32[192,256]{1,0:T(8,128)S(1)}, f32[256,256]{1,0:T(8,128)S(1)}, f32[448,256]{1,0:T(8,128)S(1)}) custom-call(s32[6]{0:T(128)S(1)} %stack.23.where, bf16[1,2,128,128]{3,2,1,0:T(8,128)(2,1)} %linv.1, bf16[1,2,128,128]{3,2,1,0:T(8,128)(2,1)} %llink.1, bf16[1,2,128,128]{3,2,1,0:T(8,128)(2,1)} %rhs.1, bf16[1,2,128,128]{3,2,1,0:T(8,128)(2,1)} %uinv.3, ...), custom_call_target="tpu_custom_call" | custom-call | tf_op jit(solution)/shard_map/pallas_call | solution.py:283
  3.9 1.9 %collective-permute-start = (f32[448,256]{1,0:T(8,128)S(1)}, f32[448,256]{1,0:T(8,128)S(1)}, u32[]{:S(2)}, u32[]{:S(2)}) collective-permute-start(f32[448,256]{1,0:T(8,128)S(1)} %get-tuple-element.21), channel_id=1, source_target_pairs={{0,4},{4,0},{1,5},{5,1},{2,6},{6,2},{3,7},{7,3},{8,12},{12,8},{9,1... | collective-permute-start | bytes 1376264 | tf_op jit(solution)/shard_map/ppermute | solution.py:319
  5.8 1.8 %collective-permute-done.send = f32[448,256]{1,0:T(8,128)S(1)} collective-permute-done((f32[448,256]{1,0:T(8,128)S(1)}, f32[448,256]{1,0:T(8,128)S(1)}, u32[]{:S(2)}, u32[]{:S(2)}) %collective-permute-start) | collective-permute-done | bytes 458784 | tf_op jit(solution)/shard_map/ppermute | solution.py:319
  7.6 0.8 shard_map.123
  8.4 24.7 %all_to_all.30.parts = f32[4,320,256]{2,1,0:T(8,128)S(1)} all-to-all(f32[4,320,256]{2,1,0:T(8,128)S(1)} %get-tuple-element.22), channel_id=1, replica_groups=mesh['zh'=4,'zl'=4,'x'=4,'c'=2,'y'=4] {'x'}, dimensions={0} | all-to-all | bytes 2621440 | tf_op jit(solution)/shard_map/all_to_all | solution.py:321
  33.1 1.6 shard_map.124
  34.7 16.8 %all-gather = f32[640,256]{1,0:T(8,128)S(1)} all-gather(f32[160,256]{1,0:T(8,128)S(1)} %get-tuple-element.23), channel_id=2, replica_groups=mesh['zh'=4,'zl'=4,'x'=4,'c'=2,'y'=4] {'zl'}, dimensions={0}, use_global_device_ids=true | all-gather | bytes 819200 | tf_op jit(solution)/shard_map/all_gather | solution.py:325
  51.6 2.4 %all-gather.1 = f32[8,96,256]{2,1,0:T(8,128)S(1)} all-gather(f32[4,96,256]{2,1,0:T(8,128)S(1)} %slice.8), channel_id=3, replica_groups=mesh['zh'=4,'zl'=4,'x'=4,'c'=2,'y'=4] {'c'}, dimensions={0}, use_global_device_ids=true | all-gather | bytes 1179648 | tf_op jit(solution)/shard_map/all_gather | solution.py:326
  54.0 1.3 shard_map.125
  55.2 34.7 %all-gather.2 = f32[640,256]{1,0:T(8,128)S(1)} all-gather(f32[160,256]{1,0:T(8,128)S(1)} %get-tuple-element.24), channel_id=4, replica_groups=mesh['zh'=4,'zl'=4,'x'=4,'c'=2,'y'=4] {'zh'}, dimensions={0}, use_global_device_ids=true | all-gather | bytes 819200 | tf_op jit(solution)/shard_map/all_gather | solution.py:330
  89.9 2.4 %all-gather.3 = f32[8,96,256]{2,1,0:T(8,128)S(1)} all-gather(f32[4,96,256]{2,1,0:T(8,128)S(1)} %slice.9), channel_id=5, replica_groups=mesh['zh'=4,'zl'=4,'x'=4,'c'=2,'y'=4] {'c'}, dimensions={0}, use_global_device_ids=true | all-gather | bytes 1179648 | tf_op jit(solution)/shard_map/all_gather | solution.py:331
  92.3 0.0 copy-start.4
  92.3 0.0 copy-start.5
  92.3 0.0 copy-start.6
  92.4 0.0 copy-start.7
  92.4 0.0 copy-start.8
  92.4 1.1 shard_map.126
  93.5 9.9 %all_to_all.31.parts = f32[4,64,128]{2,1,0:T(8,128)S(1)} all-to-all(f32[4,64,128]{2,1,0:T(8,128)S(1)} %get-tuple-element.25), channel_id=1, replica_groups=mesh['zh'=4,'zl'=4,'x'=4,'c'=2,'y'=4] {'y'}, dimensions={0} | all-to-all | bytes 262144 | tf_op jit(solution)/shard_map/all_to_all | solution.py:335
  103.4 9.8 %all_to_all.32.sums = f32[8,64,128]{2,1,0:T(8,128)S(1)} all-to-all(f32[8,64,128]{2,1,0:T(8,128)S(1)} %shard_map.127), channel_id=1, replica_groups=mesh['zh'=4,'zl'=4,'x'=4,'c'=2,'y'=4] {'x','c'}, dimensions={0} | all-to-all | bytes 524288 | tf_op jit(solution)/shard_map/all_to_all | solution.py:337
  113.3 0.0 copy-done.3
  113.3 0.0 copy-done.4
  113.3 0.0 copy-done.5
  113.3 0.0 copy-done.6
  113.3 0.0 copy-done.7
  113.3 3.7 %shard_map.128 = (f32[1,512]{1,0:T(1,128)}, f32[2,128,128]{2,1,0:T(8,128)S(1)}, f32[8,16,128]{2,1,0:T(8,128)S(1)}) custom-call(s32[6]{0:T(128)S(1)} %stack.23.where, f32[8,64,128]{2,1,0:T(8,128)S(1)} %all_to_all.32.sums, bf16[512,128]{1,0:T(8,128)(2,1)S(1)} %copy-done.8, bf16[512,512]{1,0:T(8,128)(2,1)S(1)} %copy-done.2, bf16[512,512]{1,0:T(8,128)(2,1)S(1)} %copy-done.3, ...), custom_call_target="tpu_custom_call" | custom-call | tf_op jit(solution)/shard_map/pallas_call | solution.py:283
  117.0 8.0 %all_to_all.33.parts = f32[8,16,128]{2,1,0:T(8,128)S(1)} all-to-all(f32[8,16,128]{2,1,0:T(8,128)S(1)} %get-tuple-element.30), channel_id=1, replica_groups=mesh['zh'=4,'zl'=4,'x'=4,'c'=2,'y'=4] {'x','c'}, dimensions={0} | all-to-all | bytes 131072 | tf_op jit(solution)/shard_map/all_to_all | solution.py:347
  125.0 2.1 %shard_map.129 = f32[16,16,128]{2,1,0:T(8,128)S(1)} custom-call(s32[6]{0:T(128)S(1)} %stack.23.where, f32[8,16,128]{2,1,0:T(8,128)S(1)} %all_to_all.33.parts, f32[8,128,128]{2,1,0:T(8,128)S(1)} %get-tuple-element.31.backs, f32[4,128,128]{2,1,0:T(8,128)S(1)} %get-tuple-element.32.plane_backs, f32[4,128,128]{2,1,0:T(8,128)S(1)} %get-tuple-element.33.group_backs), custom_call_target="tpu_custom_call" | custom-call | tf_op jit(solution)/shard_map/pallas_call | solution.py:283
  127.1 21.4 %all_to_all.34.planes = f32[16,16,128]{2,1,0:T(8,128)S(1)} all-to-all(f32[16,16,128]{2,1,0:T(8,128)S(1)} %shard_map.129), channel_id=1, replica_groups=mesh['zh'=4,'zl'=4,'x'=4,'c'=2,'y'=4] {'zh','zl'}, dimensions={0} | all-to-all | bytes 262144 | tf_op jit(solution)/shard_map/all_to_all | solution.py:351
  148.5 1.8 %shard_map.130 = f32[8,16,128]{2,1,0:T(8,128)S(1)} custom-call(s32[6]{0:T(128)S(1)} %stack.23.where, f32[16,16,128]{2,1,0:T(8,128)S(1)} %all_to_all.34.planes, f32[4,128,128]{2,1,0:T(8,128)S(1)} %get-tuple-element.32.plane_backs, f32[8,16,128]{2,1,0:T(8,128)S(1)} %all_to_all.33.parts, f32[8,128,128]{2,1,0:T(8,128)S(1)} %get-tuple-element.31.backs), custom_call_target="tpu_custom_call" | custom-call | tf_op jit(solution)/shard_map/pallas_call | solution.py:283
  150.3 8.0 %all_to_all.35.parts = f32[8,16,128]{2,1,0:T(8,128)S(1)} all-to-all(f32[8,16,128]{2,1,0:T(8,128)S(1)} %shard_map.130), channel_id=1, replica_groups=mesh['zh'=4,'zl'=4,'x'=4,'c'=2,'y'=4] {'x','c'}, dimensions={0} | all-to-all | bytes 131072 | tf_op jit(solution)/shard_map/all_to_all | solution.py:353
  158.3 1.7 %shard_map.131 = f32[1,2,128,128]{3,2,1,0:T(8,128)} custom-call(s32[6]{0:T(128)S(1)} %stack.23.where, f32[8,16,128]{2,1,0:T(8,128)S(1)} %all_to_all.35.parts, f32[2,128,128]{2,1,0:T(8,128)S(1)} %get-tuple-element.34.plain, bf16[1,2,128,128]{3,2,1,0:T(8,128)(2,1)S(1)} %copy-done, bf16[1,2,128,128]{3,2,1,0:T(8,128)(2,1)S(1)} %copy-done.1), custom_call_target="tpu_custom_call" | custom-call | tf_op jit(solution)/shard_map/pallas_call | solution.py:283
  (11 shorter events, 0.1 us)
Async XLA Ops:
  3.9 3.7 %collective-permute-start = (f32[448,256]{1,0:T(8,128)S(1)}, f32[448,256]{1,0:T(8,128)S(1)}, u32[]{:S(2)}, u32[]{:S(2)}) collective-permute-start(f32[448,256]{1,0:T(8,128)S(1)} %get-tuple-element.21), channel_id=1, source_target_pairs={{0,4},{4,0},{1,5},{5,1},{2,6},{6,2},{3,7},{7,3},{8,12},{12,8},{9,1... | collective-permute-start | bytes 1376264 | tf_op jit(solution)/shard_map/ppermute | solution.py:319
  92.3 20.9 %copy-start = (bf16[1,2,128,128]{3,2,1,0:T(8,128)(2,1)S(1)}, bf16[1,2,128,128]{3,2,1,0:T(8,128)(2,1)}, u32[]{:S(2)}) copy-start(bf16[1,2,128,128]{3,2,1,0:T(8,128)(2,1)} %uinv.3) | copy-start | bytes 196612
  92.3 20.9 %copy-start.1 = (bf16[1,2,128,128]{3,2,1,0:T(8,128)(2,1)S(1)}, bf16[1,2,128,128]{3,2,1,0:T(8,128)(2,1)}, u32[]{:S(2)}) copy-start(bf16[1,2,128,128]{3,2,1,0:T(8,128)(2,1)} %ulink.3) | copy-start | bytes 196612
  92.3 20.9 %copy-start.2 = (bf16[512,512]{1,0:T(8,128)(2,1)S(1)}, bf16[512,512]{1,0:T(8,128)(2,1)}, u32[]{:S(2)}) copy-start(bf16[512,512]{1,0:T(8,128)(2,1)} %root_lower.1) | copy-start | bytes 1572868
  92.3 20.9 %copy-start.3 = (bf16[512,512]{1,0:T(8,128)(2,1)S(1)}, bf16[512,512]{1,0:T(8,128)(2,1)}, u32[]{:S(2)}) copy-start(bf16[512,512]{1,0:T(8,128)(2,1)} %root_upper.1) | copy-start | bytes 1572868
  92.3 20.9 %copy-start.4 = (bf16[1,2,128,128]{3,2,1,0:T(8,128)(2,1)S(1)}, bf16[1,2,128,128]{3,2,1,0:T(8,128)(2,1)}, u32[]{:S(2)}) copy-start(bf16[1,2,128,128]{3,2,1,0:T(8,128)(2,1)} %linv.1) | copy-start | bytes 196612
  92.3 20.9 %copy-start.5 = (bf16[1,2,128,128]{3,2,1,0:T(8,128)(2,1)S(1)}, bf16[1,2,128,128]{3,2,1,0:T(8,128)(2,1)}, u32[]{:S(2)}) copy-start(bf16[1,2,128,128]{3,2,1,0:T(8,128)(2,1)} %llink.1) | copy-start | bytes 196612
  92.3 20.9 %copy-start.6 = (bf16[1,2,128,128]{3,2,1,0:T(8,128)(2,1)S(1)}, bf16[1,2,128,128]{3,2,1,0:T(8,128)(2,1)}, u32[]{:S(2)}) copy-start(bf16[1,2,128,128]{3,2,1,0:T(8,128)(2,1)} %rhs.1) | copy-start | bytes 196612
  92.4 20.9 %copy-start.7 = (bf16[1,2,128,512]{3,2,1,0:T(8,128)(2,1)S(1)}, bf16[1,2,128,512]{3,2,1,0:T(8,128)(2,1)}, u32[]{:S(2)}) copy-start(bf16[1,2,128,512]{3,2,1,0:T(8,128)(2,1)} %uroot.1) | copy-start | bytes 786436
  92.4 20.9 %copy-start.8 = (bf16[512,128]{1,0:T(8,128)(2,1)S(1)}, bf16[512,128]{1,0:T(8,128)(2,1)}, u32[]{:S(2)}) copy-start(bf16[512,128]{1,0:T(8,128)(2,1)} %rhs_root.1) | copy-start | bytes 393220

commit v4 on v3

--- a/solution.py
+++ b/solution.py
@@ -1,3 +1,5 @@
+from functools import partial
+
 import jax
 import jax.numpy as jnp
 from jax import lax
@@ -53,61 +55,63 @@
     return jnp.where(rows == cols, F32(1), F32(0))
 
 
-def copy_all(pairs, sems):
+def slots_kernel(
+    where, linv_in, llink_in, rhs_in, uinv_in, ulink_in, lroot_in, keep, send,
+    linv, llink, rhs, uinv, ulink, lroot, sems,
+):
+    sources = (linv_in, llink_in, rhs_in, uinv_in, ulink_in, lroot_in)
+    targets = (linv, llink, rhs, uinv, ulink, lroot)
     copies = [
         pltpu.make_async_copy(source, target, sems.at[k])
-        for k, (source, target) in enumerate(pairs)
+        for k, (source, target) in enumerate(zip(sources, targets))
     ]
     for copy in copies:
         copy.start()
-    for copy in copies:
+    core, both = where[3], where[5] == 2
+    for copy in copies[:3]:
         copy.wait()
-
-
-def slots_kernel(
-    where, linv_in, llink_in, rhs_in, uinv_in, ulink_in, lroot_in, own, keep, send,
-    linv, llink, rhs, uinv, ulink, lroot, sems,
-):
-    sources = (linv_in, llink_in, rhs_in, uinv_in, ulink_in, lroot_in)
-    copy_all(list(zip(sources, (linv, llink, rhs, uinv, ulink, lroot))), sems)
-    core, both = where[3], where[5] == 2
     maps = []
     for slot in range(2):
         made = dot(linv[0, slot], jnp.concatenate([llink[0, slot], rhs[0, slot]], 1))
         maps.append(jnp.concatenate([-made[:, :W], made[:, W:]], 1))
     chain = mul3(maps[1][:, :W], maps[0]) + shift(maps[1][:, W:])
     chain = jnp.where(both, chain, maps[0])
+    send[:W] = chain
+    for copy in copies[3:]:
+        copy.wait()
     back = [-dot(uinv[0, slot], ulink[0, slot]) for slot in range(2)]
     back = pack(jnp.where(both, mul3(back[0], back[1]), back[0]).T)
-    own[:W] = chain
-    own[W:] = back
-    send[:W] = chain
     send[W : W + W // 2] = back
-    for half, target, at in ((core, keep, 0), (1 - core, send, W + W // 2)):
-        rows = pl.ds(pl.multiple_of(half * 256, 256), 256)
+    for part, target, at in ((core, keep, 0), (1 - core, send, W + W // 2)):
+        rows = pl.ds(pl.multiple_of(part * 256, 256), 256)
         second = jnp.where(both, mul2(lroot[0, 1, rows], chain), F32(0))
         target[at : at + 256] = mul2(lroot[0, 0, rows], maps[0]) + second
 
 
-def chip_kernel(where, own, keep, send, out, early):
-    first = where[3] == 0
-    mine, theirs = own[:W], send[:W]
-    head = jnp.where(first, mine, theirs)
-    tail = jnp.where(first, theirs, mine)
+def half(core, rows):
+    middle = rows.shape[0] // 2
+    return jnp.where(core == 0, rows[:middle], rows[middle:])
+
+
+def chip_kernel(where, keep, pair, out, early, ends):
+    core = where[3]
+    first = core == 0
+    head, tail = pair[0, :W], pair[1, :W]
     chain = mul3(tail[:, :W], head) + shift(tail[:, W:])
-    back_mine, back_theirs = own[W:], send[W : W + W // 2]
-    back_head = jnp.where(first, back_mine, back_theirs)
-    back_tail = jnp.where(first, back_theirs, back_mine)
-    root_mine, root_theirs = keep[...], send[W + W // 2 :]
-    root_head = jnp.where(first, root_mine, root_theirs)
-    root_tail = jnp.where(first, root_theirs, root_mine)
+    back_head, back_tail = [unpack(pair[k, W : W + W // 2]) for k in range(2)]
+    root_mine = keep[...]
+    root_head = jnp.where(first, root_mine, pair[0, W + W // 2 :])
+    root_tail = jnp.where(first, pair[1, W + W // 2 :], root_mine)
     root = root_head + mul3(root_tail[:, :W], head) + shift(root_tail[:, W:])
     early[...] = head
+    ends[0] = back_head
+    ends[1] = back_tail
+    chain_half = half(core, chain)
+    back_half = half(core, pack(mul3(back_tail, back_head)))
     for other in range(4):
-        out[other, :128] = chain
-        out[other, 128:192] = back_head
-        out[other, 192:256] = back_tail
-        out[other, 256:] = root[64 * other : 64 * other + 64]
+        out[other, :64] = chain_half
+        out[other, 64:96] = back_half
+        out[other, 96:] = root[64 * other : 64 * other + 64]
 
 
 def compose(place, maps, roots):
@@ -128,38 +132,15 @@
     return prefix, root, before
 
 
-def half(core, rows):
-    middle = rows.shape[0] // 2
-    return jnp.where(core == 0, rows[:middle], rows[middle:])
-
-
-def plane_kernel(where, parts, out, before, backs):
-    maps = [parts[k, :128] for k in range(4)]
-    roots = [parts[k, 256:] for k in range(4)]
-    chain, root, prefix = compose(where[2], maps, roots)
-    before[...] = prefix
-    every = []
-    for k in range(4):
-        every += [unpack(parts[k, 128:192]), unpack(parts[k, 192:256])]
-    for k in range(8):
-        backs[k] = every[k]
-    while len(every) > 1:
-        every = [mul3(every[k + 1], every[k]) for k in range(0, len(every), 2)]
-    out[:64] = half(where[3], chain)
-    out[64:96] = half(where[3], pack(every[0]))
-    out[96:] = root
-
-
 def joined(pieces):
     maps = [jnp.concatenate([pieces[0, k, :64], pieces[1, k, :64]], 0) for k in range(4)]
     backs = [jnp.concatenate([pieces[0, k, 64:], pieces[1, k, 64:]], 0) for k in range(4)]
     return maps, [unpack(packed) for packed in backs]
 
 
-def group_kernel(where, parts, pieces, out, before, backs):
+def level_kernel(axis, where, parts, pieces, out, before, backs):
     maps, every = joined(pieces)
-    roots = [parts[k, 96:] for k in range(4)]
-    chain, root, prefix = compose(where[1], maps, roots)
+    chain, root, prefix = compose(where[axis], maps, [parts[k, 96:] for k in range(4)])
     before[...] = prefix
     for k in range(4):
         backs[k] = every[k]
@@ -186,9 +167,10 @@
         states[0],
         jnp.where(place == 1, states[1], jnp.where(place == 2, states[2], states[3])),
     )
+    for k in range(4):
+        backs[k] = every[k]
     for other in range(4):
         root[other] = total
-        backs[other] = every[other]
 
 
 def sum_kernel(parts, out):
@@ -198,15 +180,13 @@
 
 
 def root_kernel(
-    where, sums, rhs_root, root_lower, root_upper, carry, before_low, before_x, early,
+    where, sums, rhs_root, root_lower, root_upper, carry, before_low, before_x, early, ends,
     linv, llink, rhs, uinv, ulink, uroot, own_root, plain, offset,
 ):
     core, both = where[3], where[5] == 2
     summed = jnp.concatenate([sums[2 * (k % 4) + k // 4] for k in range(8)], 0)
     inner = mul2(root_lower[...], rhs_root[...].astype(F32) - summed)
     root = mul2(root_upper[...], inner)
-    columns = lax.broadcasted_iota(jnp.int32, (W, 512), 0)
-    own_root[...] = jnp.sum(jnp.where(columns == where[4], root.T, F32(0)), 0, keepdims=True)
     state = carry[...]
     for ref in (before_low, before_x):
         state = mul3(ref[:, :W], state) + ref[:, W:]
@@ -223,15 +203,21 @@
     plain[0] = offsets[0]
     plain[1] = offsets[1]
     turned = jnp.where(both, offsets[0] + mul3(link, offsets[1]), offsets[0]).T
+    carried = jnp.where(core == 0, turned, mul3(turned, ends[0]))
     for other in range(8):
-        offset[other] = turned[16 * other : 16 * other + 16]
+        rows = slice(16 * other, 16 * other + 16)
+        offset[other, :16] = carried[rows]
+        offset[other, 16:] = turned[rows]
+    columns = lax.broadcasted_iota(jnp.int32, (W, 512), 0)
+    own_root[...] = jnp.sum(jnp.where(columns == where[4], root.T, F32(0)), 0, keepdims=True)
 
 
 def offset_kernel(where, parts, backs, plane_backs, group_backs, out):
     group, place = where[0], where[1]
-    state = parts[7]
-    for k in reversed(range(7)):
-        state = parts[k] + mul3(state, backs[k])
+    chips = [parts[2 * k, :16] + parts[2 * k + 1, :16] for k in range(4)]
+    state = chips[3]
+    for k in reversed(range(3)):
+        state = chips[k] + mul3(state, backs[k])
     sent = state
     for k in reversed(range(3)):
         sent = jnp.where(place > k, mul3(sent, plane_backs[k]), sent)
@@ -251,15 +237,20 @@
         state = jnp.where(
             place < k, planes[4 * group + k] + mul3(state, plane_backs[k]), state
         )
-    for k in reversed(range(8)):
-        out[k] = state
+    for k in reversed(range(4)):
+        for core in range(2):
+            out[2 * k + core, :16] = state
+            out[2 * k + core, 16:] = parts[2 * k + 1, 16:]
         if k:
-            state = parts[k] + mul3(state, backs[k])
-
-
-def answer_kernel(where, parts, plain, uinv, ulink, out):
+            chip = parts[2 * k, :16] + parts[2 * k + 1, :16]
+            state = chip + mul3(state, backs[k])
+
+
+def answer_kernel(where, parts, ends, plain, uinv, ulink, out):
     both = where[5] == 2
-    state = jnp.concatenate([parts[k] for k in range(8)], 0).T
+    state = jnp.concatenate([parts[k, :16] for k in range(8)], 0)
+    other = jnp.concatenate([parts[k, 16:] for k in range(8)], 0)
+    state = jnp.where(where[3] == 0, mul3(state, ends[1]) + other, state).T
     links = [-dot(uinv[0, slot], ulink[0, slot]) for slot in range(2)]
     last = mul3(links[1], state) + plain[1]
     state = jnp.where(both, last, state)
@@ -310,23 +301,29 @@
     where = jnp.stack(places + [column, live_counts[0, 0]]).astype(jnp.int32)
     square, wide = (W, W), (W, 2 * W)
 
-    own, keep, send = call(
+    keep, send = call(
         slots_kernel,
         [where, lower_inverse, lower_link, rhs_blocks, upper_inverse, upper_link, lower_root],
-        [(192, 256), (256, 256), (448, 256)],
+        [(256, 256), (448, 256)],
         fetched=True,
     )
-    send = lax.ppermute(send, "c", [(0, 1), (1, 0)])
-    out, early = call(chip_kernel, [where, own, keep, send], [(4, 320, 256), wide])
+    pair = lax.all_gather(send, "c")
+    out, early, ends = call(
+        chip_kernel, [where, keep, pair], [(4, 160, 256), wide, (2,) + square]
+    )
+
+    def level(axis, parts):
+        pieces = lax.all_gather(parts[:, :96], "c")
+        return call(
+            partial(level_kernel, axis),
+            [where, parts, pieces],
+            [(160, 256), wide, (4,) + square],
+        )
+
     parts = lax.all_to_all(out, "x", 0, 0, tiled=True)
-    out, before_x, backs = call(
-        plane_kernel, [where, parts], [(160, 256), wide, (8,) + square]
-    )
+    out, before_x, chip_backs = level(2, parts)
     parts = lax.all_gather(out, "zl")
-    pieces = lax.all_gather(parts[:, :96], "c")
-    out, before_low, low_backs = call(
-        group_kernel, [where, parts, pieces], [(160, 256), wide, (4,) + square]
-    )
+    out, before_low, low_backs = level(1, parts)
     parts = lax.all_gather(out, "zh")
     pieces = lax.all_gather(parts[:, :96], "c")
     root, carry, high_backs = call(
@@ -339,20 +336,22 @@
         root_kernel,
         [
             where, sums, rhs_root, root_lower_inverse, root_upper_inverse, carry, before_low,
-            before_x, early, lower_inverse, lower_link, rhs_blocks, upper_inverse, upper_link,
-            upper_root,
+            before_x, early, ends, lower_inverse, lower_link, rhs_blocks, upper_inverse,
+            upper_link, upper_root,
         ],
-        [(1, 512), (2,) + square, (8, 16, W)],
+        [(1, 512), (2,) + square, (8, 32, W)],
     )
     parts = lax.all_to_all(offset, ("x", "c"), 0, 0, tiled=True)
     (offset,) = call(
-        offset_kernel, [where, parts, backs, low_backs, high_backs], [(16, 16, W)]
+        offset_kernel, [where, parts, chip_backs, low_backs, high_backs], [(16, 16, W)]
     )
     planes = lax.all_to_all(offset, ("zh", "zl"), 0, 0, tiled=True)
-    (states,) = call(carry_kernel, [where, planes, low_backs, parts, backs], [(8, 16, W)])
+    (states,) = call(
+        carry_kernel, [where, planes, low_backs, parts, chip_backs], [(8, 32, W)]
+    )
     states = lax.all_to_all(states, ("x", "c"), 0, 0, tiled=True)
     (answers,) = call(
-        answer_kernel, [where, states, plain, upper_inverse, upper_link], [(1, 2, W, W)]
+        answer_kernel, [where, states, ends, plain, upper_inverse, upper_link], [(1, 2, W, W)]
     )
     return answers, own_root.reshape(512, 1)
 

time: 163 us -> 157 us (0.963)
  starting transfers between devices: 1.92 us -> 0 us
  waiting for transfers between devices: 1.78 us -> 0 us
    all_gather x0 -> x3, blocking collectives: none -> 7.2 us  [the longest x2 4.74 us: level(): pieces = lax.all_gather(parts[:, :96], 'c')]
    all_to_all x1, blocking collectives: 24.7 us -> 17.6 us  [on_device(): parts = lax.all_to_all(out, 'x', 0, 0, tiled=True)]
    all_gather x2 -> x1, blocking collectives: 4.74 us -> 2.37 us  [on_device(): pieces = lax.all_gather(parts[:, :96], 'c')]
    ppermute x1 -> x0, starting transfers between devices: 1.92 us -> none  [on_device(): send = lax.ppermute(send, 'c', [(0, 1), (1, 0)])]
    ppermute x1 -> x0, waiting for transfers between devices: 1.78 us -> none  [on_device(): send = lax.ppermute(send, 'c', [(0, 1), (1, 0)])]
  transfers between devices with their start and end apart: 1 -> 0, of which waited for: 1 -> 0; matrix products, arithmetic and copies ran while one was open for 0% -> 0% of each run, Pallas kernels for 0% -> 0%
where the time goes in v4:
time: 157 us; the launch traced here: 154 us
  blocking collectives  137 us (87%)
  Pallas kernels  15.6 us (10%)
    all_gather x1, blocking collectives, on_device(): parts = lax.all_gather(out, 'zh')  34.8 us
    all_to_all x1, blocking collectives, on_device(): planes = lax.all_to_all(offset, ('zh', 'zl'), 0, 0, tiled=True)  20.9 us
    all_to_all x1, blocking collectives, on_device(): parts = lax.all_to_all(out, 'x', 0, 0, tiled=True)  17.6 us
    all_gather x1, blocking collectives, on_device(): parts = lax.all_gather(out, 'zl')  16.8 us
    pallas_call x10, Pallas kernels, call(): pl.pallas_call(kernel, out_shape=[jax.ShapeDtypeStruct(shape, F32) for sh...  15.6 us
    all_to_all x1, blocking collectives, on_device(): parts = lax.all_to_all(root, 'y', 0, 0, tiled=True)  10.3 us
    all_to_all x1, blocking collectives, on_device(): sums = lax.all_to_all(root, ('x', 'c'), 0, 0, tiled=True)  10.1 us
    all_to_all x1, blocking collectives, on_device(): states = lax.all_to_all(states, ('x', 'c'), 0, 0, tiled=True)  8.53 us

profile of v4, /device:TPU:6, one launch (start us, length us, event | category | flops | bytes accessed | tf_op | source)
XLA Modules:
  0.0 154.4 jit_solution(11497156512218698130)
XLA Ops:
  1.3 0.1 stack.23.where
  1.4 2.4 %shard_map.122 = (f32[256,256]{1,0:T(8,128)S(1)}, f32[448,256]{1,0:T(8,128)S(1)}) custom-call(s32[6]{0:T(128)S(1)} %stack.23.where, bf16[1,2,128,128]{3,2,1,0:T(8,128)(2,1)} %linv.1, bf16[1,2,128,128]{3,2,1,0:T(8,128)(2,1)} %llink.1, bf16[1,2,128,128]{3,2,1,0:T(8,128)(2,1)} %rhs.1, bf16[1,2,128,128]{3,2,1,0:T(8,128)(2,1)} %uinv.3, ...), custom_call_target="tpu_custom_call" | custom-call | tf_op jit(solution)/shard_map/pallas_call | solution.py:274
  3.8 2.5 %all-gather = f32[896,256]{1,0:T(8,128)S(1)} all-gather(f32[448,256]{1,0:T(8,128)S(1)} %get-tuple-element.20), channel_id=2, replica_groups=mesh['zh'=4,'zl'=4,'x'=4,'c'=2,'y'=4] {'c'}, dimensions={0}, use_global_device_ids=true | all-gather | bytes 1376256 | tf_op jit(solution)/shard_map/all_gather | solution.py:310
  6.3 0.8 shard_map.123
  7.1 17.6 %all_to_all.30.parts = f32[4,160,256]{2,1,0:T(8,128)S(1)} all-to-all(f32[4,160,256]{2,1,0:T(8,128)S(1)} %get-tuple-element.21), channel_id=1, replica_groups=mesh['zh'=4,'zl'=4,'x'=4,'c'=2,'y'=4] {'x'}, dimensions={0} | all-to-all | bytes 1310720 | tf_op jit(solution)/shard_map/all_to_all | solution.py:323
  24.8 2.4 %all-gather.1 = f32[8,96,256]{2,1,0:T(8,128)S(1)} all-gather(f32[4,96,256]{2,1,0:T(8,128)S(1)} %slice.12), channel_id=3, replica_groups=mesh['zh'=4,'zl'=4,'x'=4,'c'=2,'y'=4] {'c'}, dimensions={0}, use_global_device_ids=true | all-gather | bytes 1179648 | tf_op jit(solution)/shard_map/all_gather | solution.py:316
  27.2 1.3 shard_map.124
  28.4 16.8 %all-gather.2 = f32[640,256]{1,0:T(8,128)S(1)} all-gather(f32[160,256]{1,0:T(8,128)S(1)} %get-tuple-element.22), channel_id=4, replica_groups=mesh['zh'=4,'zl'=4,'x'=4,'c'=2,'y'=4] {'zl'}, dimensions={0}, use_global_device_ids=true | all-gather | bytes 819200 | tf_op jit(solution)/shard_map/all_gather | solution.py:325
  45.3 2.4 %all-gather.3 = f32[8,96,256]{2,1,0:T(8,128)S(1)} all-gather(f32[4,96,256]{2,1,0:T(8,128)S(1)} %slice.13), channel_id=5, replica_groups=mesh['zh'=4,'zl'=4,'x'=4,'c'=2,'y'=4] {'c'}, dimensions={0}, use_global_device_ids=true | all-gather | bytes 1179648 | tf_op jit(solution)/shard_map/all_gather | solution.py:316
  47.6 1.3 shard_map.125
  48.9 34.8 %all-gather.4 = f32[640,256]{1,0:T(8,128)S(1)} all-gather(f32[160,256]{1,0:T(8,128)S(1)} %get-tuple-element.23), channel_id=6, replica_groups=mesh['zh'=4,'zl'=4,'x'=4,'c'=2,'y'=4] {'zh'}, dimensions={0}, use_global_device_ids=true | all-gather | bytes 819200 | tf_op jit(solution)/shard_map/all_gather | solution.py:327
  83.7 2.4 %all-gather.5 = f32[8,96,256]{2,1,0:T(8,128)S(1)} all-gather(f32[4,96,256]{2,1,0:T(8,128)S(1)} %slice.14), channel_id=7, replica_groups=mesh['zh'=4,'zl'=4,'x'=4,'c'=2,'y'=4] {'c'}, dimensions={0}, use_global_device_ids=true | all-gather | bytes 1179648 | tf_op jit(solution)/shard_map/all_gather | solution.py:328
  86.1 0.0 copy-start.8
  86.1 1.1 shard_map.126
  87.2 0.0 copy-start.3
  87.3 10.3 %all_to_all.31.parts = f32[4,64,128]{2,1,0:T(8,128)S(1)} all-to-all(f32[4,64,128]{2,1,0:T(8,128)S(1)} %get-tuple-element.24), channel_id=1, replica_groups=mesh['zh'=4,'zl'=4,'x'=4,'c'=2,'y'=4] {'y'}, dimensions={0} | all-to-all | bytes 262144 | tf_op jit(solution)/shard_map/all_to_all | solution.py:332
  97.6 0.0 copy-start
  97.6 0.0 copy-start.1
  97.6 10.1 %all_to_all.32.sums = f32[8,64,128]{2,1,0:T(8,128)S(1)} all-to-all(f32[8,64,128]{2,1,0:T(8,128)S(1)} %shard_map.127), channel_id=1, replica_groups=mesh['zh'=4,'zl'=4,'x'=4,'c'=2,'y'=4] {'x','c'}, dimensions={0} | all-to-all | bytes 524288 | tf_op jit(solution)/shard_map/all_to_all | solution.py:334
  107.8 0.0 copy-done.4
  107.8 0.0 copy-done.5
  107.8 0.0 copy-done.6
  107.8 0.0 copy-done.7
  107.8 0.0 copy-done.8
  107.8 0.0 copy-done.3
  107.8 3.9 %shard_map.128 = (f32[1,512]{1,0:T(1,128)}, f32[2,128,128]{2,1,0:T(8,128)S(1)}, f32[8,32,128]{2,1,0:T(8,128)S(1)}) custom-call(s32[6]{0:T(128)S(1)} %stack.23.where, f32[8,64,128]{2,1,0:T(8,128)S(1)} %all_to_all.32.sums, bf16[512,128]{1,0:T(8,128)(2,1)S(1)} %copy-done.8, bf16[512,512]{1,0:T(8,128)(2,1)S(1)} %copy-done.2, bf16[512,512]{1,0:T(8,128)(2,1)S(1)} %copy-done.3, ...), custom_call_target="tpu_custom_call" | custom-call | tf_op jit(solution)/shard_map/pallas_call | solution.py:274
  111.8 8.5 %all_to_all.33.parts = f32[8,32,128]{2,1,0:T(8,128)S(1)} all-to-all(f32[8,32,128]{2,1,0:T(8,128)S(1)} %get-tuple-element.30), channel_id=1, replica_groups=mesh['zh'=4,'zl'=4,'x'=4,'c'=2,'y'=4] {'x','c'}, dimensions={0} | all-to-all | bytes 262144 | tf_op jit(solution)/shard_map/all_to_all | solution.py:344
  120.3 1.6 %shard_map.129 = f32[16,16,128]{2,1,0:T(8,128)S(1)} custom-call(s32[6]{0:T(128)S(1)} %stack.23.where, f32[8,32,128]{2,1,0:T(8,128)S(1)} %all_to_all.33.parts, f32[4,128,128]{2,1,0:T(8,128)S(1)} %get-tuple-element.31.backs, f32[4,128,128]{2,1,0:T(8,128)S(1)} %get-tuple-element.32.plane_backs, f32[4,128,128]{2,1,0:T(8,128)S(1)} %get-tuple-element.33.group_backs), custom_call_target="tpu_custom_call" | custom-call | tf_op jit(solution)/shard_map/pallas_call | solution.py:274
  121.9 20.9 %all_to_all.34.planes = f32[16,16,128]{2,1,0:T(8,128)S(1)} all-to-all(f32[16,16,128]{2,1,0:T(8,128)S(1)} %shard_map.129), channel_id=1, replica_groups=mesh['zh'=4,'zl'=4,'x'=4,'c'=2,'y'=4] {'zh','zl'}, dimensions={0} | all-to-all | bytes 262144 | tf_op jit(solution)/shard_map/all_to_all | solution.py:348
  142.9 1.3 shard_map.130
  144.1 8.5 %all_to_all.35.parts = f32[8,32,128]{2,1,0:T(8,128)S(1)} all-to-all(f32[8,32,128]{2,1,0:T(8,128)S(1)} %shard_map.130), channel_id=1, replica_groups=mesh['zh'=4,'zl'=4,'x'=4,'c'=2,'y'=4] {'x','c'}, dimensions={0} | all-to-all | bytes 262144 | tf_op jit(solution)/shard_map/all_to_all | solution.py:352
  152.7 1.8 %shard_map.131 = f32[1,2,128,128]{3,2,1,0:T(8,128)} custom-call(s32[6]{0:T(128)S(1)} %stack.23.where, f32[8,32,128]{2,1,0:T(8,128)S(1)} %all_to_all.35.parts, f32[2,128,128]{2,1,0:T(8,128)S(1)} %get-tuple-element.29.ends, f32[2,128,128]{2,1,0:T(8,128)S(1)} %get-tuple-element.34.plain, bf16[1,2,128,128]{3,2,1,0:T(8,128)(2,1)S(1)} %copy-done, ...), custom_call_target="tpu_custom_call" | custom-call | tf_op jit(solution)/shard_map/pallas_call | solution.py:274
  (12 shorter events, 0.1 us)
Async XLA Ops:
  86.1 21.6 %copy-start.4 = (bf16[1,2,128,128]{3,2,1,0:T(8,128)(2,1)S(1)}, bf16[1,2,128,128]{3,2,1,0:T(8,128)(2,1)}, u32[]{:S(2)}) copy-start(bf16[1,2,128,128]{3,2,1,0:T(8,128)(2,1)} %linv.1) | copy-start | bytes 196612
  86.1 21.6 %copy-start.5 = (bf16[1,2,128,128]{3,2,1,0:T(8,128)(2,1)S(1)}, bf16[1,2,128,128]{3,2,1,0:T(8,128)(2,1)}, u32[]{:S(2)}) copy-start(bf16[1,2,128,128]{3,2,1,0:T(8,128)(2,1)} %llink.1) | copy-start | bytes 196612
  86.1 21.6 %copy-start.6 = (bf16[1,2,128,128]{3,2,1,0:T(8,128)(2,1)S(1)}, bf16[1,2,128,128]{3,2,1,0:T(8,128)(2,1)}, u32[]{:S(2)}) copy-start(bf16[1,2,128,128]{3,2,1,0:T(8,128)(2,1)} %rhs.1) | copy-start | bytes 196612
  86.1 21.7 %copy-start.7 = (bf16[1,2,128,512]{3,2,1,0:T(8,128)(2,1)S(1)}, bf16[1,2,128,512]{3,2,1,0:T(8,128)(2,1)}, u32[]{:S(2)}) copy-start(bf16[1,2,128,512]{3,2,1,0:T(8,128)(2,1)} %uroot.1) | copy-start | bytes 786436
  86.1 21.7 %copy-start.8 = (bf16[512,128]{1,0:T(8,128)(2,1)S(1)}, bf16[512,128]{1,0:T(8,128)(2,1)}, u32[]{:S(2)}) copy-start(bf16[512,128]{1,0:T(8,128)(2,1)} %rhs_root.1) | copy-start | bytes 393220
  87.2 20.5 %copy-start.3 = (bf16[512,512]{1,0:T(8,128)(2,1)S(1)}, bf16[512,512]{1,0:T(8,128)(2,1)}, u32[]{:S(2)}) copy-start(bf16[512,512]{1,0:T(8,128)(2,1)} %root_upper.1) | copy-start | bytes 1572868
  97.6 10.2 %copy-start.2 = (bf16[512,512]{1,0:T(8,128)(2,1)S(1)}, bf16[512,512]{1,0:T(8,128)(2,1)}, u32[]{:S(2)}) copy-start(bf16[512,512]{1,0:T(8,128)(2,1)} %root_lower.1) | copy-start | bytes 1572868
  97.6 10.2 %copy-start = (bf16[1,2,128,128]{3,2,1,0:T(8,128)(2,1)S(1)}, bf16[1,2,128,128]{3,2,1,0:T(8,128)(2,1)}, u32[]{:S(2)}) copy-start(bf16[1,2,128,128]{3,2,1,0:T(8,128)(2,1)} %uinv.3) | copy-start | bytes 196612
  97.6 10.2 %copy-start.1 = (bf16[1,2,128,128]{3,2,1,0:T(8,128)(2,1)S(1)}, bf16[1,2,128,128]{3,2,1,0:T(8,128)(2,1)}, u32[]{:S(2)}) copy-start(bf16[1,2,128,128]{3,2,1,0:T(8,128)(2,1)} %ulink.3) | copy-start | bytes 196612

commit v5 on v4

v5 whole, which is shorter than its diff:
```python
import jax
import jax.numpy as jnp
from jax import lax
from jax.experimental import pallas as pl
from jax.experimental.pallas import tpu as pltpu
from jax.sharding import Mesh
from jax.sharding import PartitionSpec as P

W = 128
F32 = jnp.float32
BF16 = jnp.bfloat16
CHAIN = ("zh", "zl", "x", "c")


def dot(left, right):
    return jnp.dot(left, right, preferred_element_type=F32)


def halves(value):
    high = value.astype(BF16)
    return high, (value - high.astype(F32)).astype(BF16)


def mul2(exact, right):
    high, low = halves(right)
    return dot(exact, high) + dot(exact, low)


def mul3(left, right):
    left_high, left_low = halves(left)
    right_high, right_low = halves(right)
    return dot(
        jnp.concatenate([left_high, left_low, left_high], 1),
        jnp.concatenate([right_high, right_high, right_low], 0),
    )


def shift(offset):
    return jnp.concatenate([jnp.zeros_like(offset), offset], 1)


def pack(square):
    return jnp.concatenate([square[: W // 2], square[W // 2 :]], 1)


def unpack(packed):
    return jnp.concatenate([packed[:, :W], packed[:, W:]], 0)


def eye():
    rows = lax.broadcasted_iota(jnp.int32, (W, W), 0)
    cols = lax.broadcasted_iota(jnp.int32, (W, W), 1)
    return jnp.where(rows == cols, F32(1), F32(0))


def slots_kernel(
    where, linv_in, llink_in, rhs_in, uinv_in, ulink_in, lroot_in, keep, send, ahead,
    linv, llink, rhs, uinv, ulink, lroot, sems,
):
    sources = (linv_in, llink_in, rhs_in, uinv_in, ulink_in, lroot_in)
    targets = (linv, llink, rhs, uinv, ulink, lroot)
    copies = [
        pltpu.make_async_copy(source, target, sems.at[k])
        for k, (source, target) in enumerate(zip(sources, targets))
    ]
    for copy in copies:
        copy.start()
    core, both = where[3], where[5] == 2
    for copy in copies[:3]:
        copy.wait()
    maps = []
    for slot in range(2):
        made = dot(linv[0, slot], jnp.concatenate([llink[0, slot], rhs[0, slot]], 1))
        maps.append(jnp.concatenate([-made[:, :W], made[:, W:]], 1))
    chain = mul3(maps[1][:, :W], maps[0]) + shift(maps[1][:, W:])
    chain = jnp.where(both, chain, maps[0])
    send[:W] = chain
    for copy in copies[3:]:
        copy.wait()
    links = [-dot(uinv[0, slot], ulink[0, slot]) for slot in range(2)]
    back = jnp.where(both, mul3(links[0], links[1]), links[0])
    send[W : W + W // 2] = pack(back.T)
    ahead[:W] = maps[0]
    ahead[W:] = jnp.concatenate([back, links[1]], 1)
    for part, target, at in ((core, keep, 0), (1 - core, send, W + W // 2)):
        rows = pl.ds(pl.multiple_of(part * 256, 256), 256)
        second = jnp.where(both, mul2(lroot[0, 1, rows], chain), F32(0))
        target[at : at + 256] = mul2(lroot[0, 0, rows], maps[0]) + second


def half(core, rows):
    middle = rows.shape[0] // 2
    return jnp.where(core == 0, rows[:middle], rows[middle:])


def after(map_rows, ahead):
    return mul3(map_rows[:, :W], ahead) + shift(map_rows[:, W:])


def chip_kernel(where, keep, pair, ahead, out, solve, ends, last):
    core = where[3]
    first = core == 0
    head, tail = pair[0, :W], pair[1, :W]
    root_mine = keep[...]
    root_head = jnp.where(first, root_mine, pair[0, W + W // 2 :])
    root_tail = jnp.where(first, pair[1, W + W // 2 :], root_mine)
    slot = ahead[:W]
    made = after(jnp.concatenate([tail, slot, root_tail], 0), head)
    chain, root = made[:W], root_head + made[2 * W :]
    solve[:W] = jnp.where(first, slot, made[W : 2 * W])
    solve[W:] = jnp.where(first, head, chain)
    back_head, back_tail = [unpack(pair[k, W : W + W // 2]) for k in range(2)]
    chain_half = half(core, chain)
    back_half = half(core, pack(mul3(back_tail, back_head)))
    for other in range(4):
        out[other, :64] = chain_half
        out[other, 64:96] = back_half
        out[other, 96:] = root[64 * other : 64 * other + 64]
    ends[...] = back_head.T
    answer = jnp.concatenate([ahead[W:, :W], ahead[W:, W:]], 0)
    last[:, :W] = jnp.where(first, mul3(answer, back_tail.T), answer)
    last[:, W:] = jnp.where(first, answer, F32(0))


def compose(place, maps, roots):
    one = after(jnp.concatenate([maps[1], roots[1]], 0), maps[0])
    two = after(jnp.concatenate([maps[3], roots[3]], 0), maps[2])
    root_one, root_two = roots[0] + one[W:], roots[2] + two[W:]
    one, two = one[:W], two[:W]
    made = after(jnp.concatenate([maps[2], two, root_two], 0), one)
    start = jnp.concatenate([eye(), jnp.zeros((W, W), F32)], 1)
    before = jnp.where(
        place == 0,
        start,
        jnp.where(place == 1, maps[0], jnp.where(place == 2, one, made[:W])),
    )
    return made[W : 2 * W], root_one + made[2 * W :], before


def products(backs):
    p10, p21, p32 = [mul3(backs[k + 1], backs[k]) for k in range(3)]
    return p10, p21, p32, mul3(backs[2], p10), mul3(backs[3], p21), mul3(p32, p10)


def joined(pieces):
    maps = [jnp.concatenate([pieces[0, k, :64], pieces[1, k, :64]], 0) for k in range(4)]
    backs = [jnp.concatenate([pieces[0, k, 64:], pieces[1, k, 64:]], 0) for k in range(4)]
    return maps, [unpack(packed) for packed in backs]


def plane_kernel(where, parts, pieces, out, before, gather, spread):
    core = where[3]
    maps, backs = joined(pieces)
    chain, root, prefix = compose(where[2], maps, [parts[k, 96:] for k in range(4)])
    before[...] = prefix
    p10, p21, p32, p210, p321, total = products(backs)
    out[:64] = half(core, chain)
    out[64:96] = half(core, pack(total))
    out[96:] = root
    for k, value in enumerate((eye(), backs[0], p10, p210)):
        gather[W * k : W * k + W] = value
    for k, value in enumerate((p321, p32, backs[3], p21, backs[2], backs[1])):
        spread[:, W * k : W * k + W] = value


def pick(place, *values):
    chosen = values[-1]
    for k in reversed(range(len(values) - 1)):
        chosen = jnp.where(place == k, values[k], chosen)
    return chosen


def group_kernel(
    where, parts, pieces, solve, before_x, out, before, solve_out, ahead, within,
    chain_ref, back_ref, root_ref,
):
    core, place = where[3], where[1]
    maps, backs = joined(pieces)
    chain, root, prefix = compose(place, maps, [parts[k, 96:] for k in range(4)])
    before[...] = prefix
    p10, p21, p32, p210, p321, total = products(backs)
    at = 0
    for ref, value, rows, start in (
        (chain_ref, chain, 16, 64 * core + 16 * place),
        (back_ref, pack(total), 8, 32 * core + 8 * place),
        (root_ref, root, 16, 16 * place),
    ):
        ref[...] = value
        out[at : at + rows] = ref[pl.ds(pl.multiple_of(start, rows), rows)]
        at += rows
    solve_out[...] = after(solve[...], before_x[...])
    one, none = eye(), jnp.zeros((W, W), F32)
    ahead[...] = pick(place, one, backs[0], p10, p210)
    within[:W] = pick(place, p321, p32, backs[3], one)
    within[W : 2 * W] = pick(place, one, none)
    within[2 * W : 3 * W] = pick(place, backs[1], one, none)
    within[3 * W :] = pick(place, p21, backs[2], one, none)


def top_kernel(where, parts, pieces, solve, before_low, ahead, root, carry, solve_out, sent):
    place = where[0]
    maps, backs, roots = [], [], []
    for k in range(4):
        mine = [(core, 4 * k + low) for core in range(2) for low in range(4)]
        maps.append(jnp.concatenate([pieces[core, z, :16] for core, z in mine], 0))
        backs.append(unpack(jnp.concatenate([pieces[core, z, 16:] for core, z in mine], 0)))
        roots.append(jnp.concatenate([parts[4 * k + low, 24:] for low in range(4)], 0))
    total = roots[0][:, W:]
    state = maps[0][:, W:]
    states = [jnp.zeros((W, W), F32), state]
    for k in range(1, 4):
        stacked = mul3(jnp.concatenate([maps[k][:, :W], roots[k][:, :W]], 0), state)
        total = total + stacked[W:] + roots[k][:, W:]
        state = stacked[:W] + maps[k][:, W:]
        states.append(state)
    carry[...] = pick(place, *states[:4])
    for other in range(4):
        root[other] = total
    solve_out[...] = after(solve[...], before_low[...])
    one = mul3(ahead[...], pick(place, backs[0], backs[0], backs[1], backs[2]))
    sent[:, :W] = ahead[...]
    sent[:, W : 2 * W] = one
    sent[:, 2 * W :] = mul3(one, pick(place, backs[0], backs[0], backs[0], backs[1]))


def sum_kernel(parts, out):
    total = (parts[0] + parts[1]) + (parts[2] + parts[3])
    for other in range(8):
        out[other] = total


def root_kernel(
    where, sums, rhs_root, root_lower, root_upper, carry, solve, ends, uinv, ulink, uroot,
    own_root, plain, offset,
):
    core, both = where[3], where[5] == 2
    summed = jnp.concatenate([sums[2 * (k % 4) + k // 4] for k in range(8)], 0)
    inner = mul2(root_lower[...], rhs_root[...].astype(F32) - summed)
    root = mul2(root_upper[...], inner)
    solved = mul3(solve[:, :W], carry[...]) + solve[:, W:]
    first, second = uinv[0, 0].astype(F32), uinv[0, 1].astype(F32)
    link = jnp.where(both, -dot(uinv[0, 0], ulink[0, 0]), F32(0))
    over = mul3(link, second)
    moved = mul3(ends[...], jnp.concatenate([first, over], 1))
    root_high, root_low = halves(root)
    inner = [
        solved[W * slot : W * slot + W]
        - (dot(uroot[0, slot], root_high) + dot(uroot[0, slot], root_low))
        for slot in range(2)
    ]
    on_first = mul3(jnp.concatenate([first, moved[:, :W]], 0), inner[0])
    on_second = mul3(jnp.concatenate([over, moved[:, W:], second], 0), inner[1])
    whole = on_first + on_second[: 2 * W]
    plain[:W] = whole[:W]
    plain[W:] = on_second[2 * W :]
    turned = whole[:W].T
    carried = jnp.where(core == 0, whole[:W], whole[W:]).T
    for other in range(8):
        rows = slice(16 * other, 16 * other + 16)
        offset[other, :16] = carried[rows]
        offset[other, 16:] = turned[rows]
    columns = lax.broadcasted_iota(jnp.int32, (W, 512), 0)
    own_root[...] = jnp.sum(jnp.where(columns == where[4], root.T, F32(0)), 0, keepdims=True)


def chip_offsets(parts):
    return [parts[2 * k, :16] + parts[2 * k + 1, :16] for k in range(4)]


def offset_kernel(where, parts, gather, sent, out):
    state = mul3(jnp.concatenate(chip_offsets(parts), 1), gather[...])
    moved = mul3(state, sent[...])
    values = [state, moved[:, :W], moved[:, W : 2 * W], moved[:, 2 * W :]]
    for other in range(4):
        value = pick(where[0] - other, *values)
        for k in range(4):
            out[4 * other + k] = value


def carry_kernel(where, planes, within, parts, spread, out):
    group = where[0]
    state = jnp.zeros((16, W), F32)
    for k in range(4, 16):
        state = state + jnp.where(k // 4 > group, planes[k], F32(0))
    offsets = [planes[4 * group + k] for k in range(1, 4)]
    state = mul3(jnp.concatenate([state] + offsets, 1), within[...])
    chips = chip_offsets(parts)
    moved = mul3(chips[3], spread[:, 3 * W : 5 * W])
    plain = [
        chips[1] + mul3(chips[2], spread[:, 5 * W :]) + moved[:, :W],
        chips[2] + moved[:, W:],
        chips[3],
    ]
    moved = mul3(state, spread[:, : 3 * W])
    states = [plain[k] + moved[:, W * k : W * k + W] for k in range(3)] + [state]
    for k in range(4):
        for core in range(2):
            out[2 * k + core, :16] = states[k]
            out[2 * k + core, 16:] = parts[2 * k + 1, 16:]


def answer_kernel(where, parts, last, plain, out):
    state = jnp.concatenate([parts[k, :16] for k in range(8)], 0).T
    other = jnp.concatenate([parts[k, 16:] for k in range(8)], 0).T
    made = mul3(last[...], jnp.concatenate([state, other], 0)) + plain[...]
    out[0, 0] = made[:W]
    out[0, 1] = jnp.where(where[5] == 2, made[W:], F32(0))


def call(kernel, inputs, shapes, fetched=False, scratch=()):
    vmem = pl.BlockSpec(memory_space=pltpu.VMEM)
    smem = pl.BlockSpec(memory_space=pltpu.SMEM)
    block = pl.BlockSpec(memory_space=pltpu.HBM) if fetched else vmem
    scratch = [pltpu.VMEM(shape, F32) for shape in scratch]
    if fetched:
        scratch = [pltpu.VMEM(a.shape, a.dtype) for a in inputs if a.dtype == BF16]
        scratch.append(pltpu.SemaphoreType.DMA((len(scratch),)))
    if fetched:
        inputs = [
            pltpu.with_memory_space_constraint(a, pltpu.HBM) if a.dtype == BF16 else a
            for a in inputs
        ]
    return pl.pallas_call(
        kernel,
        out_shape=[jax.ShapeDtypeStruct(shape, F32) for shape in shapes],
        in_specs=[
            smem if a.dtype == jnp.int32 else block if a.dtype == BF16 else vmem for a in inputs
        ],
        out_specs=[vmem] * len(shapes),
        scratch_shapes=scratch,
        compiler_params=pltpu.CompilerParams(vmem_limit_bytes=32 * 1024 * 1024),
    )(*inputs)


def on_device(
    lower_inverse,
    upper_inverse,
    lower_link,
    upper_link,
    lower_root,
    upper_root,
    rhs_blocks,
    rhs_root,
    root_lower_inverse,
    root_upper_inverse,
    live_counts,
):
    places = [lax.axis_index(name) for name in CHAIN]
    column = ((places[0] * 4 + places[1]) * 4 + places[2]) * 2 + places[3]
    where = jnp.stack(places + [column, live_counts[0, 0]]).astype(jnp.int32)
    square, wide = (W, W), (W, 2 * W)

    keep, send, ahead = call(
        slots_kernel,
        [where, lower_inverse, lower_link, rhs_blocks, upper_inverse, upper_link, lower_root],
        [(256, 256), (448, 256), (256, 256)],
        fetched=True,
    )
    pair = lax.all_gather(send, "c")
    out, solve, ends, last = call(
        chip_kernel,
        [where, keep, pair, ahead],
        [(4, 160, 256), (256, 256), square, (256, 256)],
    )
    parts = lax.all_to_all(out, "x", 0, 0, tiled=True)
    pieces = lax.all_gather(parts[:, :96], "c")
    out, before_x, gather, spread = call(
        plane_kernel, [where, parts, pieces], [(160, 256), wide, (4 * W, W), (W, 6 * W)]
    )
    parts = lax.all_gather(out, "zl")
    pieces = lax.all_gather(parts[:, :96], "c")
    out, before_low, solve, ahead, within = call(
        group_kernel,
        [where, parts, pieces, solve, before_x],
        [(40, 256), wide, (256, 256), square, (4 * W, W)],
        scratch=[wide, (64, 256), (64, 256)],
    )
    parts = lax.all_gather(out, ("zh", "zl"))
    pieces = lax.all_gather(parts[:, :24], "c")
    root, carry, solve, sent = call(
        top_kernel,
        [where, parts, pieces, solve, before_low, ahead],
        [(4, 64, W), square, (256, 256), (W, 3 * W)],
    )
    parts = lax.all_to_all(root, "y", 0, 0, tiled=True)
    (root,) = call(sum_kernel, [parts], [(8, 64, W)])
    sums = lax.all_to_all(root, ("x", "c"), 0, 0, tiled=True)
    own_root, plain, offset = call(
        root_kernel,
        [
            where, sums, rhs_root, root_lower_inverse, root_upper_inverse, carry, solve, ends,
            upper_inverse, upper_link, upper_root,
        ],
        [(1, 512), (256, W), (8, 32, W)],
    )
    parts = lax.all_to_all(offset, ("x", "c"), 0, 0, tiled=True)
    (offset,) = call(offset_kernel, [where, parts, gather, sent], [(16, 16, W)])
    planes = lax.all_to_all(offset, ("zh", "zl"), 0, 0, tiled=True)
    (states,) = call(carry_kernel, [where, planes, within, parts, spread], [(8, 32, W)])
    states = lax.all_to_all(states, ("x", "c"), 0, 0, tiled=True)
    (answers,) = call(answer_kernel, [where, states, last, plain], [(1, 2, W, W)])
    return answers, own_root.reshape(512, 1)


def solution(mesh):
    fine = Mesh(mesh.devices.reshape(4, 4, 4, 2, 4), CHAIN + ("y",))
    split = P("y", CHAIN)
    return jax.shard_map(
        on_device,
        mesh=fine,
        in_specs=(split,) * 7 + (P(), P(), P(), split),
        out_specs=(split, P(None, CHAIN)),
        check_vma=False,
    )
```

time: 157 us -> 155 us (0.987)
  Pallas kernels: 15.6 us -> 13.8 us
    all_gather x1 -> x2, blocking collectives: 2.37 us -> 4.74 us  [on_device(): pieces = lax.all_gather(parts[:, :96], 'c')]
    all_gather x3 -> x2, blocking collectives: 39.5 us -> 37.6 us  [the longest x1 35.3 us: on_device(): parts = lax.all_gather(out, ('zh', 'zl'))]
    pallas_call x10, Pallas kernels: 15.6 us -> 13.8 us  [call(): pl.pallas_call(kernel, out_shape=[jax.ShapeDtypeStruct(shape, F32) for sh...]
where the time goes in v5:
time: 155 us; the launch traced here: 153 us
  blocking collectives  137 us (88%)
  Pallas kernels  13.8 us (9%)
    all_gather x1, blocking collectives, on_device(): parts = lax.all_gather(out, ('zh', 'zl'))  35.3 us
    all_to_all x1, blocking collectives, on_device(): planes = lax.all_to_all(offset, ('zh', 'zl'), 0, 0, tiled=True)  20.5 us
    all_to_all x1, blocking collectives, on_device(): parts = lax.all_to_all(out, 'x', 0, 0, tiled=True)  17.6 us
    all_gather x1, blocking collectives, on_device(): parts = lax.all_gather(out, 'zl')  16.8 us
    pallas_call x10, Pallas kernels, call(): pl.pallas_call(kernel, out_shape=[jax.ShapeDtypeStruct(shape, F32) for sh...  13.8 us
    all_to_all x1, blocking collectives, on_device(): parts = lax.all_to_all(root, 'y', 0, 0, tiled=True)  10.4 us
    all_to_all x1, blocking collectives, on_device(): sums = lax.all_to_all(root, ('x', 'c'), 0, 0, tiled=True)  10.1 us
    all_to_all x1, blocking collectives, on_device(): states = lax.all_to_all(states, ('x', 'c'), 0, 0, tiled=True)  8.52 us

profile of v5, /device:TPU:6, one launch (start us, length us, event | category | flops | bytes accessed | tf_op | source)
XLA Modules:
  0.0 152.7 jit_solution(17323257974224958994)
XLA Ops:
  1.3 0.1 stack.23.where
  1.4 2.4 %shard_map.122 = (f32[256,256]{1,0:T(8,128)S(1)}, f32[448,256]{1,0:T(8,128)S(1)}, f32[256,256]{1,0:T(8,128)S(1)}) custom-call(s32[6]{0:T(128)S(1)} %stack.23.where, bf16[1,2,128,128]{3,2,1,0:T(8,128)(2,1)} %linv_in.1, bf16[1,2,128,128]{3,2,1,0:T(8,128)(2,1)} %llink_in.1, bf16[1,2,128,128]{3,2,1,0:T(8,128)(2,1)} %rhs_in.1, bf16[1,2,128,128]{3,2,1,0:T(8,128)(2,1)} %uinv.1, ...), custom_call_target="tpu_custom_call" | custom-call | tf_op jit(solution)/shard_map/pallas_call | solution.py:323
  3.8 2.5 %all-gather = f32[896,256]{1,0:T(8,128)S(1)} all-gather(f32[448,256]{1,0:T(8,128)S(1)} %get-tuple-element.26), channel_id=2, replica_groups=mesh['zh'=4,'zl'=4,'x'=4,'c'=2,'y'=4] {'c'}, dimensions={0}, use_global_device_ids=true | all-gather | bytes 1376256 | tf_op jit(solution)/shard_map/all_gather | solution.py:359
  6.3 0.9 shard_map.123
  7.2 17.6 %all_to_all.30.parts = f32[4,160,256]{2,1,0:T(8,128)S(1)} all-to-all(f32[4,160,256]{2,1,0:T(8,128)S(1)} %get-tuple-element.28), channel_id=1, replica_groups=mesh['zh'=4,'zl'=4,'x'=4,'c'=2,'y'=4] {'x'}, dimensions={0} | all-to-all | bytes 1310720 | tf_op jit(solution)/shard_map/all_to_all | solution.py:365
  24.9 2.4 %all-gather.1 = f32[8,96,256]{2,1,0:T(8,128)S(1)} all-gather(f32[4,96,256]{2,1,0:T(8,128)S(1)} %slice.12), channel_id=3, replica_groups=mesh['zh'=4,'zl'=4,'x'=4,'c'=2,'y'=4] {'c'}, dimensions={0}, use_global_device_ids=true | all-gather | bytes 1179648 | tf_op jit(solution)/shard_map/all_gather | solution.py:366
  27.2 1.2 shard_map.124
  28.5 16.8 %all-gather.2 = f32[640,256]{1,0:T(8,128)S(1)} all-gather(f32[160,256]{1,0:T(8,128)S(1)} %get-tuple-element.29), channel_id=4, replica_groups=mesh['zh'=4,'zl'=4,'x'=4,'c'=2,'y'=4] {'zl'}, dimensions={0}, use_global_device_ids=true | all-gather | bytes 819200 | tf_op jit(solution)/shard_map/all_gather | solution.py:370
  45.3 2.4 %all-gather.3 = f32[8,96,256]{2,1,0:T(8,128)S(1)} all-gather(f32[4,96,256]{2,1,0:T(8,128)S(1)} %slice.13), channel_id=5, replica_groups=mesh['zh'=4,'zl'=4,'x'=4,'c'=2,'y'=4] {'c'}, dimensions={0}, use_global_device_ids=true | all-gather | bytes 1179648 | tf_op jit(solution)/shard_map/all_gather | solution.py:371
  47.7 1.3 shard_map.125
  49.0 35.3 %all-gather.4 = f32[640,256]{1,0:T(8,128)S(1)} all-gather(f32[40,256]{1,0:T(8,128)S(1)} %get-tuple-element.32), channel_id=6, replica_groups=mesh['zh'=4,'zl'=4,'x'=4,'c'=2,'y'=4] {'zh','zl'}, dimensions={0}, use_global_device_ids=true | all-gather | bytes 696320 | tf_op jit(solution)/shard_map/all_gather | solution.py:378
  84.3 2.4 %all-gather.5 = f32[32,24,256]{2,1,0:T(8,128)S(1)} all-gather(f32[16,24,256]{2,1,0:T(8,128)S(1)} %slice.14), channel_id=7, replica_groups=mesh['zh'=4,'zl'=4,'x'=4,'c'=2,'y'=4] {'c'}, dimensions={0}, use_global_device_ids=true | all-gather | bytes 1179648 | tf_op jit(solution)/shard_map/all_gather | solution.py:379
  86.7 0.0 copy-start.2
  86.7 1.3 shard_map.126
  88.0 0.0 copy-start.1
  88.0 10.4 %all_to_all.31.parts = f32[4,64,128]{2,1,0:T(8,128)S(1)} all-to-all(f32[4,64,128]{2,1,0:T(8,128)S(1)} %get-tuple-element.36), channel_id=1, replica_groups=mesh['zh'=4,'zl'=4,'x'=4,'c'=2,'y'=4] {'y'}, dimensions={0} | all-to-all | bytes 262144 | tf_op jit(solution)/shard_map/all_to_all | solution.py:385
  98.4 0.0 copy-start.3
  98.4 0.0 copy-start.4
  98.4 10.1 %all_to_all.32.sums = f32[8,64,128]{2,1,0:T(8,128)S(1)} all-to-all(f32[8,64,128]{2,1,0:T(8,128)S(1)} %shard_map.127), channel_id=1, replica_groups=mesh['zh'=4,'zl'=4,'x'=4,'c'=2,'y'=4] {'x','c'}, dimensions={0} | all-to-all | bytes 524288 | tf_op jit(solution)/shard_map/all_to_all | solution.py:387
  108.5 0.0 copy-done.2
  108.5 0.0 copy-done.5
  108.5 0.0 copy-done.1
  108.5 0.0 copy-done
  108.5 0.0 copy-done.3
  108.5 0.0 copy-done.4
  108.6 3.3 %shard_map.128 = (f32[1,512]{1,0:T(1,128)}, f32[256,128]{1,0:T(8,128)S(1)}, f32[8,32,128]{2,1,0:T(8,128)S(1)}) custom-call(s32[6]{0:T(128)S(1)} %stack.23.where, f32[8,64,128]{2,1,0:T(8,128)S(1)} %all_to_all.32.sums, bf16[512,128]{1,0:T(8,128)(2,1)S(1)} %copy-done.5, bf16[512,512]{1,0:T(8,128)(2,1)S(1)} %copy-done, bf16[512,512]{1,0:T(8,128)(2,1)S(1)} %copy-done.1, ...), custom_call_target="tpu_custom_call" | custom-call | tf_op jit(solution)/shard_map/pallas_call | solution.py:323
  111.9 8.5 %all_to_all.33.parts = f32[8,32,128]{2,1,0:T(8,128)S(1)} all-to-all(f32[8,32,128]{2,1,0:T(8,128)S(1)} %get-tuple-element.40), channel_id=1, replica_groups=mesh['zh'=4,'zl'=4,'x'=4,'c'=2,'y'=4] {'x','c'}, dimensions={0} | all-to-all | bytes 262144 | tf_op jit(solution)/shard_map/all_to_all | solution.py:396
  120.4 0.9 shard_map.129
  121.3 20.5 %all_to_all.34.planes = f32[16,16,128]{2,1,0:T(8,128)S(1)} all-to-all(f32[16,16,128]{2,1,0:T(8,128)S(1)} %shard_map.129), channel_id=1, replica_groups=mesh['zh'=4,'zl'=4,'x'=4,'c'=2,'y'=4] {'zh','zl'}, dimensions={0} | all-to-all | bytes 262144 | tf_op jit(solution)/shard_map/all_to_all | solution.py:398
  141.8 0.9 shard_map.130
  142.6 8.5 %all_to_all.35.parts = f32[8,32,128]{2,1,0:T(8,128)S(1)} all-to-all(f32[8,32,128]{2,1,0:T(8,128)S(1)} %shard_map.130), channel_id=1, replica_groups=mesh['zh'=4,'zl'=4,'x'=4,'c'=2,'y'=4] {'x','c'}, dimensions={0} | all-to-all | bytes 262144 | tf_op jit(solution)/shard_map/all_to_all | solution.py:400
  151.2 1.6 %shard_map.131 = f32[1,2,128,128]{3,2,1,0:T(8,128)} custom-call(s32[6]{0:T(128)S(1)} %stack.23.where, f32[8,32,128]{2,1,0:T(8,128)S(1)} %all_to_all.35.parts, f32[256,256]{1,0:T(8,128)S(1)} %get-tuple-element.45.last, f32[256,128]{1,0:T(8,128)S(1)} %get-tuple-element.46.plain), custom_call_target="tpu_custom_call" | custom-call | tf_op jit(solution)/shard_map/pallas_call | solution.py:323
  (6 shorter events, 0.1 us)
Async XLA Ops:
  86.7 21.8 %copy-start.2 = (bf16[1,2,128,512]{3,2,1,0:T(8,128)(2,1)S(1)}, bf16[1,2,128,512]{3,2,1,0:T(8,128)(2,1)}, u32[]{:S(2)}) copy-start(bf16[1,2,128,512]{3,2,1,0:T(8,128)(2,1)} %uroot.1) | copy-start | bytes 786436
  86.7 21.8 %copy-start.5 = (bf16[512,128]{1,0:T(8,128)(2,1)S(1)}, bf16[512,128]{1,0:T(8,128)(2,1)}, u32[]{:S(2)}) copy-start(bf16[512,128]{1,0:T(8,128)(2,1)} %rhs_root.1) | copy-start | bytes 393220
  88.0 20.5 %copy-start.1 = (bf16[512,512]{1,0:T(8,128)(2,1)S(1)}, bf16[512,512]{1,0:T(8,128)(2,1)}, u32[]{:S(2)}) copy-start(bf16[512,512]{1,0:T(8,128)(2,1)} %root_upper.1) | copy-start | bytes 1572868
  98.4 10.1 %copy-start = (bf16[512,512]{1,0:T(8,128)(2,1)S(1)}, bf16[512,512]{1,0:T(8,128)(2,1)}, u32[]{:S(2)}) copy-start(bf16[512,512]{1,0:T(8,128)(2,1)} %root_lower.1) | copy-start | bytes 1572868
  98.4 10.1 %copy-start.3 = (bf16[1,2,128,128]{3,2,1,0:T(8,128)(2,1)S(1)}, bf16[1,2,128,128]{3,2,1,0:T(8,128)(2,1)}, u32[]{:S(2)}) copy-start(bf16[1,2,128,128]{3,2,1,0:T(8,128)(2,1)} %uinv.1) | copy-start | bytes 196612
  98.4 10.1 %copy-start.4 = (bf16[1,2,128,128]{3,2,1,0:T(8,128)(2,1)S(1)}, bf16[1,2,128,128]{3,2,1,0:T(8,128)(2,1)}, u32[]{:S(2)}) copy-start(bf16[1,2,128,128]{3,2,1,0:T(8,128)(2,1)} %ulink.1) | copy-start | bytes 196612

commit v6 on v5

--- a/solution.py
+++ b/solution.py
@@ -9,7 +9,11 @@
 W = 128
 F32 = jnp.float32
 BF16 = jnp.bfloat16
-CHAIN = ("zh", "zl", "x", "c")
+CHAIN = ("zh", "za", "zb", "x", "c")
+LOW = ("za", "zb")
+SHARE = ("zb",)
+SHARES = 2
+ROWS = 64 // SHARES
 
 
 def dot(left, right):
@@ -172,22 +176,16 @@
 
 def group_kernel(
     where, parts, pieces, solve, before_x, out, before, solve_out, ahead, within,
-    chain_ref, back_ref, root_ref,
 ):
     core, place = where[3], where[1]
+    share = pl.ds(pl.multiple_of(96 + lax.rem(place, SHARES) * ROWS, ROWS), ROWS)
     maps, backs = joined(pieces)
-    chain, root, prefix = compose(place, maps, [parts[k, 96:] for k in range(4)])
+    chain, root, prefix = compose(place, maps, [parts[k, share] for k in range(4)])
     before[...] = prefix
     p10, p21, p32, p210, p321, total = products(backs)
-    at = 0
-    for ref, value, rows, start in (
-        (chain_ref, chain, 16, 64 * core + 16 * place),
-        (back_ref, pack(total), 8, 32 * core + 8 * place),
-        (root_ref, root, 16, 16 * place),
-    ):
-        ref[...] = value
-        out[at : at + rows] = ref[pl.ds(pl.multiple_of(start, rows), rows)]
-        at += rows
+    out[:64] = half(core, chain)
+    out[64:96] = half(core, pack(total))
+    out[96:] = root
     solve_out[...] = after(solve[...], before_x[...])
     one, none = eye(), jnp.zeros((W, W), F32)
     ahead[...] = pick(place, one, backs[0], p10, p210)
@@ -199,12 +197,8 @@
 
 def top_kernel(where, parts, pieces, solve, before_low, ahead, root, carry, solve_out, sent):
     place = where[0]
-    maps, backs, roots = [], [], []
-    for k in range(4):
-        mine = [(core, 4 * k + low) for core in range(2) for low in range(4)]
-        maps.append(jnp.concatenate([pieces[core, z, :16] for core, z in mine], 0))
-        backs.append(unpack(jnp.concatenate([pieces[core, z, 16:] for core, z in mine], 0)))
-        roots.append(jnp.concatenate([parts[4 * k + low, 24:] for low in range(4)], 0))
+    maps, backs = joined(pieces)
+    roots = [parts[k, 96:] for k in range(4)]
     total = roots[0][:, W:]
     state = maps[0][:, W:]
     states = [jnp.zeros((W, W), F32), state]
@@ -225,7 +219,7 @@
 
 def sum_kernel(parts, out):
     total = (parts[0] + parts[1]) + (parts[2] + parts[3])
-    for other in range(8):
+    for other in range(8 * SHARES):
         out[other] = total
 
 
@@ -234,7 +228,8 @@
     own_root, plain, offset,
 ):
     core, both = where[3], where[5] == 2
-    summed = jnp.concatenate([sums[2 * (k % 4) + k // 4] for k in range(8)], 0)
+    order = [(k * 4 + x) * 2 + c for c in range(2) for x in range(4) for k in range(SHARES)]
+    summed = jnp.concatenate([sums[k] for k in order], 0)
     inner = mul2(root_lower[...], rhs_root[...].astype(F32) - summed)
     root = mul2(root_upper[...], inner)
     solved = mul3(solve[:, :W], carry[...]) + solve[:, W:]
@@ -307,15 +302,14 @@
     out[0, 1] = jnp.where(where[5] == 2, made[W:], F32(0))
 
 
-def call(kernel, inputs, shapes, fetched=False, scratch=()):
+def call(kernel, inputs, shapes, fetched=False):
     vmem = pl.BlockSpec(memory_space=pltpu.VMEM)
     smem = pl.BlockSpec(memory_space=pltpu.SMEM)
     block = pl.BlockSpec(memory_space=pltpu.HBM) if fetched else vmem
-    scratch = [pltpu.VMEM(shape, F32) for shape in scratch]
+    scratch = []
     if fetched:
         scratch = [pltpu.VMEM(a.shape, a.dtype) for a in inputs if a.dtype == BF16]
         scratch.append(pltpu.SemaphoreType.DMA((len(scratch),)))
-    if fetched:
         inputs = [
             pltpu.with_memory_space_constraint(a, pltpu.HBM) if a.dtype == BF16 else a
             for a in inputs
@@ -345,7 +339,7 @@
     root_upper_inverse,
     live_counts,
 ):
-    places = [lax.axis_index(name) for name in CHAIN]
+    places = [lax.axis_index(axes) for axes in ("zh", LOW, "x", "c")]
     column = ((places[0] * 4 + places[1]) * 4 + places[2]) * 2 + places[3]
     where = jnp.stack(places + [column, live_counts[0, 0]]).astype(jnp.int32)
     square, wide = (W, W), (W, 2 * W)
@@ -367,24 +361,23 @@
     out, before_x, gather, spread = call(
         plane_kernel, [where, parts, pieces], [(160, 256), wide, (4 * W, W), (W, 6 * W)]
     )
-    parts = lax.all_gather(out, "zl")
+    parts = lax.all_gather(out, LOW)
     pieces = lax.all_gather(parts[:, :96], "c")
     out, before_low, solve, ahead, within = call(
         group_kernel,
         [where, parts, pieces, solve, before_x],
-        [(40, 256), wide, (256, 256), square, (4 * W, W)],
-        scratch=[wide, (64, 256), (64, 256)],
-    )
-    parts = lax.all_gather(out, ("zh", "zl"))
-    pieces = lax.all_gather(parts[:, :24], "c")
+        [(96 + ROWS, 256), wide, (256, 256), square, (4 * W, W)],
+    )
+    parts = lax.all_gather(out, "zh")
+    pieces = lax.all_gather(parts[:, :96], "c")
     root, carry, solve, sent = call(
         top_kernel,
         [where, parts, pieces, solve, before_low, ahead],
-        [(4, 64, W), square, (256, 256), (W, 3 * W)],
+        [(4, ROWS, W), square, (256, 256), (W, 3 * W)],
     )
     parts = lax.all_to_all(root, "y", 0, 0, tiled=True)
-    (root,) = call(sum_kernel, [parts], [(8, 64, W)])
-    sums = lax.all_to_all(root, ("x", "c"), 0, 0, tiled=True)
+    (root,) = call(sum_kernel, [parts], [(8 * SHARES, ROWS, W)])
+    sums = lax.all_to_all(root, SHARE + ("x", "c"), 0, 0, tiled=True)
     own_root, plain, offset = call(
         root_kernel,
         [
@@ -395,7 +388,7 @@
     )
     parts = lax.all_to_all(offset, ("x", "c"), 0, 0, tiled=True)
     (offset,) = call(offset_kernel, [where, parts, gather, sent], [(16, 16, W)])
-    planes = lax.all_to_all(offset, ("zh", "zl"), 0, 0, tiled=True)
+    planes = lax.all_to_all(offset, ("zh",) + LOW, 0, 0, tiled=True)
     (states,) = call(carry_kernel, [where, planes, within, parts, spread], [(8, 32, W)])
     states = lax.all_to_all(states, ("x", "c"), 0, 0, tiled=True)
     (answers,) = call(answer_kernel, [where, states, last, plain], [(1, 2, W, W)])
@@ -403,7 +396,7 @@
 
 
 def solution(mesh):
-    fine = Mesh(mesh.devices.reshape(4, 4, 4, 2, 4), CHAIN + ("y",))
+    fine = Mesh(mesh.devices.reshape(4, 2, 2, 4, 2, 4), CHAIN + ("y",))
     split = P("y", CHAIN)
     return jax.shard_map(
         on_device,

time: 155 us -> 153 us (0.987)
  blocking collectives: 137 us -> 135 us
    all_gather x3 -> x2, blocking collectives: 54.5 us -> 46.5 us  [the longest x1 29.6 us: on_device(): parts = lax.all_gather(out, 'zh')]
    all_to_all x2, blocking collectives: 30.6 us -> 34.3 us  [the longest x1 23.7 us: on_device(): planes = lax.all_to_all(offset, ('zh',) + LOW, 0, 0, tiled=True)]
    all_gather x2 -> x3, blocking collectives: 4.74 us -> 7.11 us  [on_device(): pieces = lax.all_gather(parts[:, :96], 'c')]
where the time goes in v6:
time: 153 us; the launch traced here: 150 us
  blocking collectives  135 us (88%)
  Pallas kernels  13.8 us (9%)
    all_gather x1, blocking collectives, on_device(): parts = lax.all_gather(out, 'zh')  29.6 us
    all_to_all x1, blocking collectives, on_device(): planes = lax.all_to_all(offset, ('zh',) + LOW, 0, 0, tiled=True)  23.7 us
    all_to_all x1, blocking collectives, on_device(): parts = lax.all_to_all(out, 'x', 0, 0, tiled=True)  17.7 us
    all_gather x1, blocking collectives, on_device(): parts = lax.all_gather(out, LOW)  16.8 us
    pallas_call x10, Pallas kernels, call(): pl.pallas_call(kernel, out_shape=[jax.ShapeDtypeStruct(shape, F32) for sh...  13.8 us
    all_to_all x1, blocking collectives, on_device(): sums = lax.all_to_all(root, SHARE + ('x', 'c'), 0, 0, tiled=True)  10.6 us
    all_to_all x1, blocking collectives, on_device(): parts = lax.all_to_all(root, 'y', 0, 0, tiled=True)  9.86 us
    all_to_all x1, blocking collectives, on_device(): parts = lax.all_to_all(offset, ('x', 'c'), 0, 0, tiled=True)  8.71 us

profile of v6, /device:TPU:6, one launch (start us, length us, event | category | flops | bytes accessed | tf_op | source)
XLA Modules:
  0.0 150.4 jit_solution(1535969664233249876)
XLA Ops:
  1.3 0.1 stack.23.where
  1.4 2.4 %shard_map.122 = (f32[256,256]{1,0:T(8,128)S(1)}, f32[448,256]{1,0:T(8,128)S(1)}, f32[256,256]{1,0:T(8,128)S(1)}) custom-call(s32[6]{0:T(128)S(1)} %stack.23.where, bf16[1,2,128,128]{3,2,1,0:T(8,128)(2,1)} %linv_in.1, bf16[1,2,128,128]{3,2,1,0:T(8,128)(2,1)} %llink_in.1, bf16[1,2,128,128]{3,2,1,0:T(8,128)(2,1)} %rhs_in.1, bf16[1,2,128,128]{3,2,1,0:T(8,128)(2,1)} %uinv.1, ...), custom_call_target="tpu_custom_call" | custom-call | tf_op jit(solution)/shard_map/pallas_call | solution.py:317
  3.8 2.5 %all-gather = f32[896,256]{1,0:T(8,128)S(1)} all-gather(f32[448,256]{1,0:T(8,128)S(1)} %get-tuple-element.26), channel_id=2, replica_groups=mesh['zh'=4,'za'=2,'zb'=2,'x'=4,'c'=2,'y'=4] {'c'}, dimensions={0}, use_global_device_ids=true | all-gather | bytes 1376256 | tf_op jit(solution)/shard_map/all_gather | solution.py:353
  6.3 0.9 shard_map.123
  7.2 17.7 %all_to_all.30.parts = f32[4,160,256]{2,1,0:T(8,128)S(1)} all-to-all(f32[4,160,256]{2,1,0:T(8,128)S(1)} %get-tuple-element.28), channel_id=1, replica_groups=mesh['zh'=4,'za'=2,'zb'=2,'x'=4,'c'=2,'y'=4] {'x'}, dimensions={0} | all-to-all | bytes 1310720 | tf_op jit(solution)/shard_map/all_to_all | solution.py:359
  24.9 2.4 %all-gather.1 = f32[8,96,256]{2,1,0:T(8,128)S(1)} all-gather(f32[4,96,256]{2,1,0:T(8,128)S(1)} %slice.12), channel_id=3, replica_groups=mesh['zh'=4,'za'=2,'zb'=2,'x'=4,'c'=2,'y'=4] {'c'}, dimensions={0}, use_global_device_ids=true | all-gather | bytes 1179648 | tf_op jit(solution)/shard_map/all_gather | solution.py:360
  27.3 1.2 shard_map.124
  28.5 16.8 %all-gather.2 = f32[640,256]{1,0:T(8,128)S(1)} all-gather(f32[160,256]{1,0:T(8,128)S(1)} %get-tuple-element.29), channel_id=4, replica_groups=mesh['zh'=4,'za'=2,'zb'=2,'x'=4,'c'=2,'y'=4] {'za','zb'}, dimensions={0}, use_global_device_ids=true | all-gather | bytes 819200 | tf_op jit(solution)/shard_map/all_gather | solution.py:364
  45.3 2.4 %all-gather.3 = f32[8,96,256]{2,1,0:T(8,128)S(1)} all-gather(f32[4,96,256]{2,1,0:T(8,128)S(1)} %slice.13), channel_id=5, replica_groups=mesh['zh'=4,'za'=2,'zb'=2,'x'=4,'c'=2,'y'=4] {'c'}, dimensions={0}, use_global_device_ids=true | all-gather | bytes 1179648 | tf_op jit(solution)/shard_map/all_gather | solution.py:365
  47.7 1.3 shard_map.125
  49.0 29.6 %all-gather.4 = f32[512,256]{1,0:T(8,128)S(1)} all-gather(f32[128,256]{1,0:T(8,128)S(1)} %get-tuple-element.32), channel_id=6, replica_groups=mesh['zh'=4,'za'=2,'zb'=2,'x'=4,'c'=2,'y'=4] {'zh'}, dimensions={0}, use_global_device_ids=true | all-gather | bytes 655360 | tf_op jit(solution)/shard_map/all_gather | solution.py:371
  78.7 2.4 %all-gather.5 = f32[8,96,256]{2,1,0:T(8,128)S(1)} all-gather(f32[4,96,256]{2,1,0:T(8,128)S(1)} %slice.14), channel_id=7, replica_groups=mesh['zh'=4,'za'=2,'zb'=2,'x'=4,'c'=2,'y'=4] {'c'}, dimensions={0}, use_global_device_ids=true | all-gather | bytes 1179648 | tf_op jit(solution)/shard_map/all_gather | solution.py:372
  81.0 1.3 shard_map.126
  82.4 0.0 copy-start
  82.4 9.9 %all_to_all.31.parts = f32[4,32,128]{2,1,0:T(8,128)S(1)} all-to-all(f32[4,32,128]{2,1,0:T(8,128)S(1)} %get-tuple-element.36), channel_id=1, replica_groups=mesh['zh'=4,'za'=2,'zb'=2,'x'=4,'c'=2,'y'=4] {'y'}, dimensions={0} | all-to-all | bytes 131072 | tf_op jit(solution)/shard_map/all_to_all | solution.py:378
  92.3 0.0 copy-start.2
  92.3 0.0 copy-start.3
  92.3 0.0 copy-start.4
  92.3 10.6 %all_to_all.32.sums = f32[16,32,128]{2,1,0:T(8,128)S(1)} all-to-all(f32[16,32,128]{2,1,0:T(8,128)S(1)} %shard_map.127), channel_id=1, replica_groups=mesh['zh'=4,'za'=2,'zb'=2,'x'=4,'c'=2,'y'=4] {'zb','x','c'}, dimensions={0} | all-to-all | bytes 524288 | tf_op jit(solution)/shard_map/all_to_all | solution.py:380
  102.9 0.0 copy-done.1
  102.9 0.0 copy-done.5
  102.9 0.0 copy-done
  102.9 0.0 copy-done.2
  102.9 0.0 copy-done.3
  102.9 0.0 copy-done.4
  102.9 3.3 %shard_map.128 = (f32[1,512]{1,0:T(1,128)}, f32[256,128]{1,0:T(8,128)S(1)}, f32[8,32,128]{2,1,0:T(8,128)S(1)}) custom-call(s32[6]{0:T(128)S(1)} %stack.23.where, f32[16,32,128]{2,1,0:T(8,128)S(1)} %all_to_all.32.sums, bf16[512,128]{1,0:T(8,128)(2,1)S(1)} %copy-done.5, bf16[512,512]{1,0:T(8,128)(2,1)S(1)} %copy-done, bf16[512,512]{1,0:T(8,128)(2,1)S(1)} %copy-done.1, ...), custom_call_target="tpu_custom_call" | custom-call | tf_op jit(solution)/shard_map/pallas_call | solution.py:317
  106.2 8.7 %all_to_all.33.parts = f32[8,32,128]{2,1,0:T(8,128)S(1)} all-to-all(f32[8,32,128]{2,1,0:T(8,128)S(1)} %get-tuple-element.40), channel_id=1, replica_groups=mesh['zh'=4,'za'=2,'zb'=2,'x'=4,'c'=2,'y'=4] {'x','c'}, dimensions={0} | all-to-all | bytes 262144 | tf_op jit(solution)/shard_map/all_to_all | solution.py:389
  115.0 0.9 shard_map.129
  115.8 23.7 %all_to_all.34.planes = f32[16,16,128]{2,1,0:T(8,128)S(1)} all-to-all(f32[16,16,128]{2,1,0:T(8,128)S(1)} %shard_map.129), channel_id=1, replica_groups=mesh['zh'=4,'za'=2,'zb'=2,'x'=4,'c'=2,'y'=4] {'zh','za','zb'}, dimensions={0} | all-to-all | bytes 262144 | tf_op jit(solution)/shard_map/all_to_all | solution.py:391
  139.5 0.9 shard_map.130
  140.4 8.5 %all_to_all.35.parts = f32[8,32,128]{2,1,0:T(8,128)S(1)} all-to-all(f32[8,32,128]{2,1,0:T(8,128)S(1)} %shard_map.130), channel_id=1, replica_groups=mesh['zh'=4,'za'=2,'zb'=2,'x'=4,'c'=2,'y'=4] {'x','c'}, dimensions={0} | all-to-all | bytes 262144 | tf_op jit(solution)/shard_map/all_to_all | solution.py:393
  148.9 1.5 %shard_map.131 = f32[1,2,128,128]{3,2,1,0:T(8,128)} custom-call(s32[6]{0:T(128)S(1)} %stack.23.where, f32[8,32,128]{2,1,0:T(8,128)S(1)} %all_to_all.35.parts, f32[256,256]{1,0:T(8,128)S(1)} %get-tuple-element.45.last, f32[256,128]{1,0:T(8,128)S(1)} %get-tuple-element.46.plain), custom_call_target="tpu_custom_call" | custom-call | tf_op jit(solution)/shard_map/pallas_call | solution.py:317
  (6 shorter events, 0.1 us)
Async XLA Ops:
  81.0 21.8 %copy-start.1 = (bf16[512,512]{1,0:T(8,128)(2,1)S(1)}, bf16[512,512]{1,0:T(8,128)(2,1)}, u32[]{:S(2)}) copy-start(bf16[512,512]{1,0:T(8,128)(2,1)} %root_upper.1) | copy-start | bytes 1572868
  81.0 21.8 %copy-start.5 = (bf16[512,128]{1,0:T(8,128)(2,1)S(1)}, bf16[512,128]{1,0:T(8,128)(2,1)}, u32[]{:S(2)}) copy-start(bf16[512,128]{1,0:T(8,128)(2,1)} %rhs_root.1) | copy-start | bytes 393220
  82.4 20.5 %copy-start = (bf16[512,512]{1,0:T(8,128)(2,1)S(1)}, bf16[512,512]{1,0:T(8,128)(2,1)}, u32[]{:S(2)}) copy-start(bf16[512,512]{1,0:T(8,128)(2,1)} %root_lower.1) | copy-start | bytes 1572868
  92.3 10.6 %copy-start.2 = (bf16[1,2,128,512]{3,2,1,0:T(8,128)(2,1)S(1)}, bf16[1,2,128,512]{3,2,1,0:T(8,128)(2,1)}, u32[]{:S(2)}) copy-start(bf16[1,2,128,512]{3,2,1,0:T(8,128)(2,1)} %uroot.1) | copy-start | bytes 786436
  92.3 10.6 %copy-start.3 = (bf16[1,2,128,128]{3,2,1,0:T(8,128)(2,1)S(1)}, bf16[1,2,128,128]{3,2,1,0:T(8,128)(2,1)}, u32[]{:S(2)}) copy-start(bf16[1,2,128,128]{3,2,1,0:T(8,128)(2,1)} %uinv.1) | copy-start | bytes 196612
  92.3 10.6 %copy-start.4 = (bf16[1,2,128,128]{3,2,1,0:T(8,128)(2,1)S(1)}, bf16[1,2,128,128]{3,2,1,0:T(8,128)(2,1)}, u32[]{:S(2)}) copy-start(bf16[1,2,128,128]{3,2,1,0:T(8,128)(2,1)} %ulink.1) | copy-start | bytes 196612

commit v7 on v6

--- a/solution.py
+++ b/solution.py
@@ -27,16 +27,22 @@
 
 def mul2(exact, right):
     high, low = halves(right)
-    return dot(exact, high) + dot(exact, low)
+    if right.shape[1] == W:
+        made = dot(exact, jnp.concatenate([high, low], 1))
+        return made[:, :W] + made[:, W:]
+    return dot(jnp.concatenate([exact, exact], 1), jnp.concatenate([high, low], 0))
 
 
 def mul3(left, right):
     left_high, left_low = halves(left)
     right_high, right_low = halves(right)
-    return dot(
-        jnp.concatenate([left_high, left_low, left_high], 1),
-        jnp.concatenate([right_high, right_high, right_low], 0),
-    )
+    both = jnp.concatenate([left_high, left_low], 1)
+    if right.shape[1] == W:
+        upper = jnp.concatenate([right_high, right_low], 1)
+        lower = jnp.concatenate([right_high, jnp.zeros_like(right_low)], 1)
+        made = dot(both, jnp.concatenate([upper, lower], 0))
+        return made[:, :W] + made[:, W:]
+    return dot(both, jnp.concatenate([right_high, right_high], 0)) + dot(left_high, right_low)
 
 
 def shift(offset):
@@ -86,10 +92,12 @@
     send[W : W + W // 2] = pack(back.T)
     ahead[:W] = maps[0]
     ahead[W:] = jnp.concatenate([back, links[1]], 1)
+    second = jnp.where(both, chain, F32(0))
+    ahead_high, ahead_low = halves(jnp.concatenate([maps[0], second], 0))
     for part, target, at in ((core, keep, 0), (1 - core, send, W + W // 2)):
         rows = pl.ds(pl.multiple_of(part * 256, 256), 256)
-        second = jnp.where(both, mul2(lroot[0, 1, rows], chain), F32(0))
-        target[at : at + 256] = mul2(lroot[0, 0, rows], maps[0]) + second
+        blocks = jnp.concatenate([lroot[0, 0, rows], lroot[0, 1, rows]], 1)
+        target[at : at + 256] = dot(blocks, ahead_high) + dot(blocks, ahead_low)
 
 
 def half(core, rows):
@@ -237,12 +245,8 @@
     link = jnp.where(both, -dot(uinv[0, 0], ulink[0, 0]), F32(0))
     over = mul3(link, second)
     moved = mul3(ends[...], jnp.concatenate([first, over], 1))
-    root_high, root_low = halves(root)
-    inner = [
-        solved[W * slot : W * slot + W]
-        - (dot(uroot[0, slot], root_high) + dot(uroot[0, slot], root_low))
-        for slot in range(2)
-    ]
+    parts = mul2(jnp.concatenate([uroot[0, 0], uroot[0, 1]], 0), root)
+    inner = [(solved - parts)[W * slot : W * slot + W] for slot in range(2)]
     on_first = mul3(jnp.concatenate([first, moved[:, :W]], 0), inner[0])
     on_second = mul3(jnp.concatenate([over, moved[:, W:], second], 0), inner[1])
     whole = on_first + on_second[: 2 * W]

time: 153 us -> 151 us (0.987)
  no operation moved by 1% of the time
where the time goes in v7:
time: 151 us; the launch traced here: 149 us
  blocking collectives  135 us (89%)
  Pallas kernels  12.5 us (8%)
    all_gather x1, blocking collectives, on_device(): parts = lax.all_gather(out, 'zh')  29.4 us
    all_to_all x1, blocking collectives, on_device(): planes = lax.all_to_all(offset, ('zh',) + LOW, 0, 0, tiled=True)  23.4 us
    all_to_all x1, blocking collectives, on_device(): parts = lax.all_to_all(out, 'x', 0, 0, tiled=True)  17.7 us
    all_gather x1, blocking collectives, on_device(): parts = lax.all_gather(out, LOW)  16.8 us
    pallas_call x10, Pallas kernels, call(): pl.pallas_call(kernel, out_shape=[jax.ShapeDtypeStruct(shape, F32) for sh...  12.5 us
    all_to_all x1, blocking collectives, on_device(): sums = lax.all_to_all(root, SHARE + ('x', 'c'), 0, 0, tiled=True)  10.6 us
    all_to_all x1, blocking collectives, on_device(): parts = lax.all_to_all(root, 'y', 0, 0, tiled=True)  9.87 us
    all_to_all x1, blocking collectives, on_device(): parts = lax.all_to_all(offset, ('x', 'c'), 0, 0, tiled=True)  8.71 us

profile of v7, /device:TPU:6, one launch (start us, length us, event | category | flops | bytes accessed | tf_op | source)
XLA Modules:
  0.0 148.7 jit_solution(12237737578963830928)
XLA Ops:
  1.3 0.1 stack.23.where
  1.4 2.3 %shard_map.122 = (f32[256,256]{1,0:T(8,128)S(1)}, f32[448,256]{1,0:T(8,128)S(1)}, f32[256,256]{1,0:T(8,128)S(1)}) custom-call(s32[6]{0:T(128)S(1)} %stack.23.where, bf16[1,2,128,128]{3,2,1,0:T(8,128)(2,1)} %linv_in.1, bf16[1,2,128,128]{3,2,1,0:T(8,128)(2,1)} %llink_in.1, bf16[1,2,128,128]{3,2,1,0:T(8,128)(2,1)} %rhs_in.1, bf16[1,2,128,128]{3,2,1,0:T(8,128)(2,1)} %uinv.1, ...), custom_call_target="tpu_custom_call" | custom-call | tf_op jit(solution)/shard_map/pallas_call | solution.py:321
  3.7 2.5 %all-gather = f32[896,256]{1,0:T(8,128)S(1)} all-gather(f32[448,256]{1,0:T(8,128)S(1)} %get-tuple-element.26), channel_id=2, replica_groups=mesh['zh'=4,'za'=2,'zb'=2,'x'=4,'c'=2,'y'=4] {'c'}, dimensions={0}, use_global_device_ids=true | all-gather | bytes 1376256 | tf_op jit(solution)/shard_map/all_gather | solution.py:357
  6.2 0.9 shard_map.123
  7.1 17.7 %all_to_all.30.parts = f32[4,160,256]{2,1,0:T(8,128)S(1)} all-to-all(f32[4,160,256]{2,1,0:T(8,128)S(1)} %get-tuple-element.28), channel_id=1, replica_groups=mesh['zh'=4,'za'=2,'zb'=2,'x'=4,'c'=2,'y'=4] {'x'}, dimensions={0} | all-to-all | bytes 1310720 | tf_op jit(solution)/shard_map/all_to_all | solution.py:363
  24.8 2.4 %all-gather.1 = f32[8,96,256]{2,1,0:T(8,128)S(1)} all-gather(f32[4,96,256]{2,1,0:T(8,128)S(1)} %slice.12), channel_id=3, replica_groups=mesh['zh'=4,'za'=2,'zb'=2,'x'=4,'c'=2,'y'=4] {'c'}, dimensions={0}, use_global_device_ids=true | all-gather | bytes 1179648 | tf_op jit(solution)/shard_map/all_gather | solution.py:364
  27.1 1.1 shard_map.124
  28.2 16.8 %all-gather.2 = f32[640,256]{1,0:T(8,128)S(1)} all-gather(f32[160,256]{1,0:T(8,128)S(1)} %get-tuple-element.29), channel_id=4, replica_groups=mesh['zh'=4,'za'=2,'zb'=2,'x'=4,'c'=2,'y'=4] {'za','zb'}, dimensions={0}, use_global_device_ids=true | all-gather | bytes 819200 | tf_op jit(solution)/shard_map/all_gather | solution.py:368
  45.1 2.4 %all-gather.3 = f32[8,96,256]{2,1,0:T(8,128)S(1)} all-gather(f32[4,96,256]{2,1,0:T(8,128)S(1)} %slice.13), channel_id=5, replica_groups=mesh['zh'=4,'za'=2,'zb'=2,'x'=4,'c'=2,'y'=4] {'c'}, dimensions={0}, use_global_device_ids=true | all-gather | bytes 1179648 | tf_op jit(solution)/shard_map/all_gather | solution.py:369
  47.5 1.2 shard_map.125
  48.6 29.4 %all-gather.4 = f32[512,256]{1,0:T(8,128)S(1)} all-gather(f32[128,256]{1,0:T(8,128)S(1)} %get-tuple-element.32), channel_id=6, replica_groups=mesh['zh'=4,'za'=2,'zb'=2,'x'=4,'c'=2,'y'=4] {'zh'}, dimensions={0}, use_global_device_ids=true | all-gather | bytes 655360 | tf_op jit(solution)/shard_map/all_gather | solution.py:375
  78.1 2.4 %all-gather.5 = f32[8,96,256]{2,1,0:T(8,128)S(1)} all-gather(f32[4,96,256]{2,1,0:T(8,128)S(1)} %slice.14), channel_id=7, replica_groups=mesh['zh'=4,'za'=2,'zb'=2,'x'=4,'c'=2,'y'=4] {'c'}, dimensions={0}, use_global_device_ids=true | all-gather | bytes 1179648 | tf_op jit(solution)/shard_map/all_gather | solution.py:376
  80.5 1.2 shard_map.126
  81.7 0.0 copy-start
  81.7 9.9 %all_to_all.31.parts = f32[4,32,128]{2,1,0:T(8,128)S(1)} all-to-all(f32[4,32,128]{2,1,0:T(8,128)S(1)} %get-tuple-element.36), channel_id=1, replica_groups=mesh['zh'=4,'za'=2,'zb'=2,'x'=4,'c'=2,'y'=4] {'y'}, dimensions={0} | all-to-all | bytes 131072 | tf_op jit(solution)/shard_map/all_to_all | solution.py:382
  91.6 0.0 copy-start.2
  91.6 0.0 copy-start.3
  91.6 0.0 copy-start.4
  91.6 10.6 %all_to_all.32.sums = f32[16,32,128]{2,1,0:T(8,128)S(1)} all-to-all(f32[16,32,128]{2,1,0:T(8,128)S(1)} %shard_map.127), channel_id=1, replica_groups=mesh['zh'=4,'za'=2,'zb'=2,'x'=4,'c'=2,'y'=4] {'zb','x','c'}, dimensions={0} | all-to-all | bytes 524288 | tf_op jit(solution)/shard_map/all_to_all | solution.py:384
  102.2 0.0 copy-done.1
  102.2 0.0 copy-done.5
  102.2 0.0 copy-done
  102.2 0.0 copy-done.2
  102.2 0.0 copy-done.3
  102.3 0.0 copy-done.4
  102.3 2.5 %shard_map.128 = (f32[1,512]{1,0:T(1,128)}, f32[256,128]{1,0:T(8,128)S(1)}, f32[8,32,128]{2,1,0:T(8,128)S(1)}) custom-call(s32[6]{0:T(128)S(1)} %stack.23.where, f32[16,32,128]{2,1,0:T(8,128)S(1)} %all_to_all.32.sums, bf16[512,128]{1,0:T(8,128)(2,1)S(1)} %copy-done.5, bf16[512,512]{1,0:T(8,128)(2,1)S(1)} %copy-done, bf16[512,512]{1,0:T(8,128)(2,1)S(1)} %copy-done.1, ...), custom_call_target="tpu_custom_call" | custom-call | tf_op jit(solution)/shard_map/pallas_call | solution.py:321
  104.8 8.7 %all_to_all.33.parts = f32[8,32,128]{2,1,0:T(8,128)S(1)} all-to-all(f32[8,32,128]{2,1,0:T(8,128)S(1)} %get-tuple-element.40), channel_id=1, replica_groups=mesh['zh'=4,'za'=2,'zb'=2,'x'=4,'c'=2,'y'=4] {'x','c'}, dimensions={0} | all-to-all | bytes 262144 | tf_op jit(solution)/shard_map/all_to_all | solution.py:393
  113.5 0.9 shard_map.129
  114.4 23.4 %all_to_all.34.planes = f32[16,16,128]{2,1,0:T(8,128)S(1)} all-to-all(f32[16,16,128]{2,1,0:T(8,128)S(1)} %shard_map.129), channel_id=1, replica_groups=mesh['zh'=4,'za'=2,'zb'=2,'x'=4,'c'=2,'y'=4] {'zh','za','zb'}, dimensions={0} | all-to-all | bytes 262144 | tf_op jit(solution)/shard_map/all_to_all | solution.py:395
  137.8 0.9 shard_map.130
  138.7 8.5 %all_to_all.35.parts = f32[8,32,128]{2,1,0:T(8,128)S(1)} all-to-all(f32[8,32,128]{2,1,0:T(8,128)S(1)} %shard_map.130), channel_id=1, replica_groups=mesh['zh'=4,'za'=2,'zb'=2,'x'=4,'c'=2,'y'=4] {'x','c'}, dimensions={0} | all-to-all | bytes 262144 | tf_op jit(solution)/shard_map/all_to_all | solution.py:397
  147.2 1.5 %shard_map.131 = f32[1,2,128,128]{3,2,1,0:T(8,128)} custom-call(s32[6]{0:T(128)S(1)} %stack.23.where, f32[8,32,128]{2,1,0:T(8,128)S(1)} %all_to_all.35.parts, f32[256,256]{1,0:T(8,128)S(1)} %get-tuple-element.45.last, f32[256,128]{1,0:T(8,128)S(1)} %get-tuple-element.46.plain), custom_call_target="tpu_custom_call" | custom-call | tf_op jit(solution)/shard_map/pallas_call | solution.py:321
  (6 shorter events, 0.1 us)
Async XLA Ops:
  80.4 21.8 %copy-start.1 = (bf16[512,512]{1,0:T(8,128)(2,1)S(1)}, bf16[512,512]{1,0:T(8,128)(2,1)}, u32[]{:S(2)}) copy-start(bf16[512,512]{1,0:T(8,128)(2,1)} %root_upper.1) | copy-start | bytes 1572868
  80.5 21.8 %copy-start.5 = (bf16[512,128]{1,0:T(8,128)(2,1)S(1)}, bf16[512,128]{1,0:T(8,128)(2,1)}, u32[]{:S(2)}) copy-start(bf16[512,128]{1,0:T(8,128)(2,1)} %rhs_root.1) | copy-start | bytes 393220
  81.7 20.5 %copy-start = (bf16[512,512]{1,0:T(8,128)(2,1)S(1)}, bf16[512,512]{1,0:T(8,128)(2,1)}, u32[]{:S(2)}) copy-start(bf16[512,512]{1,0:T(8,128)(2,1)} %root_lower.1) | copy-start | bytes 1572868
  91.6 10.6 %copy-start.2 = (bf16[1,2,128,512]{3,2,1,0:T(8,128)(2,1)S(1)}, bf16[1,2,128,512]{3,2,1,0:T(8,128)(2,1)}, u32[]{:S(2)}) copy-start(bf16[1,2,128,512]{3,2,1,0:T(8,128)(2,1)} %uroot.1) | copy-start | bytes 786436
  91.6 10.6 %copy-start.3 = (bf16[1,2,128,128]{3,2,1,0:T(8,128)(2,1)S(1)}, bf16[1,2,128,128]{3,2,1,0:T(8,128)(2,1)}, u32[]{:S(2)}) copy-start(bf16[1,2,128,128]{3,2,1,0:T(8,128)(2,1)} %uinv.1) | copy-start | bytes 196612
  91.6 10.6 %copy-start.4 = (bf16[1,2,128,128]{3,2,1,0:T(8,128)(2,1)S(1)}, bf16[1,2,128,128]{3,2,1,0:T(8,128)(2,1)}, u32[]{:S(2)}) copy-start(bf16[1,2,128,128]{3,2,1,0:T(8,128)(2,1)} %ulink.1) | copy-start | bytes 196612

commit v8 on v7

--- a/solution.py
+++ b/solution.py
@@ -183,7 +183,7 @@
 
 
 def group_kernel(
-    where, parts, pieces, solve, before_x, out, before, solve_out, ahead, within,
+    where, parts, pieces, solve, before_x, out, before, solve_out, ahead, within, back_ref,
 ):
     core, place = where[3], where[1]
     share = pl.ds(pl.multiple_of(96 + lax.rem(place, SHARES) * ROWS, ROWS), ROWS)
@@ -192,8 +192,9 @@
     before[...] = prefix
     p10, p21, p32, p210, p321, total = products(backs)
     out[:64] = half(core, chain)
-    out[64:96] = half(core, pack(total))
-    out[96:] = root
+    back_ref[...] = pack(total)
+    out[64:72] = back_ref[pl.ds(pl.multiple_of(32 * core + 8 * where[2], 8), 8)]
+    out[72:] = root
     solve_out[...] = after(solve[...], before_x[...])
     one, none = eye(), jnp.zeros((W, W), F32)
     ahead[...] = pick(place, one, backs[0], p10, p210)
@@ -203,10 +204,10 @@
     within[3 * W :] = pick(place, p21, backs[2], one, none)
 
 
-def top_kernel(where, parts, pieces, solve, before_low, ahead, root, carry, solve_out, sent):
+def top_kernel(where, parts, pieces, solve, before_low, root, carry, solve_out):
     place = where[0]
-    maps, backs = joined(pieces)
-    roots = [parts[k, 96:] for k in range(4)]
+    maps = [jnp.concatenate([pieces[0, k], pieces[1, k]], 0) for k in range(4)]
+    roots = [parts[k, 72:] for k in range(4)]
     total = roots[0][:, W:]
     state = maps[0][:, W:]
     states = [jnp.zeros((W, W), F32), state]
@@ -219,10 +220,6 @@
     for other in range(4):
         root[other] = total
     solve_out[...] = after(solve[...], before_low[...])
-    one = mul3(ahead[...], pick(place, backs[0], backs[0], backs[1], backs[2]))
-    sent[:, :W] = ahead[...]
-    sent[:, W : 2 * W] = one
-    sent[:, 2 * W :] = mul3(one, pick(place, backs[0], backs[0], backs[0], backs[1]))
 
 
 def sum_kernel(parts, out):
@@ -232,8 +229,8 @@
 
 
 def root_kernel(
-    where, sums, rhs_root, root_lower, root_upper, carry, solve, ends, uinv, ulink, uroot,
-    own_root, plain, offset,
+    where, sums, rhs_root, root_lower, root_upper, carry, solve, ends, groups, uinv, ulink,
+    uroot, own_root, plain, offset,
 ):
     core, both = where[3], where[5] == 2
     order = [(k * 4 + x) * 2 + c for c in range(2) for x in range(4) for k in range(SHARES)]
@@ -257,7 +254,11 @@
     for other in range(8):
         rows = slice(16 * other, 16 * other + 16)
         offset[other, :16] = carried[rows]
-        offset[other, 16:] = turned[rows]
+        offset[other, 16:32] = turned[rows]
+        for k in range(2):
+            at = 32 + 16 * k
+            offset[other, at : at + 8] = groups[k + 1, 64:72, :W]
+            offset[other, at + 8 : at + 16] = groups[k + 1, 64:72, W:]
     columns = lax.broadcasted_iota(jnp.int32, (W, 512), 0)
     own_root[...] = jnp.sum(jnp.where(columns == where[4], root.T, F32(0)), 0, keepdims=True)
 
@@ -266,10 +267,17 @@
     return [parts[2 * k, :16] + parts[2 * k + 1, :16] for k in range(4)]
 
 
-def offset_kernel(where, parts, gather, sent, out):
+def offset_kernel(where, parts, gather, ahead, out):
+    backs = []
+    for at in (32, 48):
+        order = [2 * x + core for core in range(2) for x in range(4)]
+        sides = [parts[k, at : at + 8] for k in order]
+        sides += [parts[k, at + 8 : at + 16] for k in order]
+        backs.append(jnp.concatenate(sides, 0))
     state = mul3(jnp.concatenate(chip_offsets(parts), 1), gather[...])
-    moved = mul3(state, sent[...])
-    values = [state, moved[:, :W], moved[:, W : 2 * W], moved[:, 2 * W :]]
+    one = mul3(state, ahead[...])
+    two = mul3(one, jnp.where(where[0] == 3, backs[1], backs[0]))
+    values = [state, one, two, mul3(two, backs[0])]
     for other in range(4):
         value = pick(where[0] - other, *values)
         for k in range(4):
@@ -295,7 +303,7 @@
     for k in range(4):
         for core in range(2):
             out[2 * k + core, :16] = states[k]
-            out[2 * k + core, 16:] = parts[2 * k + 1, 16:]
+            out[2 * k + core, 16:] = parts[2 * k + 1, 16:32]
 
 
 def answer_kernel(where, parts, last, plain, out):
@@ -306,11 +314,11 @@
     out[0, 1] = jnp.where(where[5] == 2, made[W:], F32(0))
 
 
-def call(kernel, inputs, shapes, fetched=False):
+def call(kernel, inputs, shapes, fetched=False, scratch=()):
     vmem = pl.BlockSpec(memory_space=pltpu.VMEM)
     smem = pl.BlockSpec(memory_space=pltpu.SMEM)
     block = pl.BlockSpec(memory_space=pltpu.HBM) if fetched else vmem
-    scratch = []
+    scratch = [pltpu.VMEM(shape, F32) for shape in scratch]
     if fetched:
         scratch = [pltpu.VMEM(a.shape, a.dtype) for a in inputs if a.dtype == BF16]
         scratch.append(pltpu.SemaphoreType.DMA((len(scratch),)))
@@ -370,14 +378,15 @@
     out, before_low, solve, ahead, within = call(
         group_kernel,
         [where, parts, pieces, solve, before_x],
-        [(96 + ROWS, 256), wide, (256, 256), square, (4 * W, W)],
-    )
-    parts = lax.all_gather(out, "zh")
-    pieces = lax.all_gather(parts[:, :96], "c")
-    root, carry, solve, sent = call(
+        [(72 + ROWS, 256), wide, (256, 256), square, (4 * W, W)],
+        scratch=[(64, 256)],
+    )
+    groups = lax.all_gather(out, "zh")
+    pieces = lax.all_gather(groups[:, :64], "c")
+    root, carry, solve = call(
         top_kernel,
-        [where, parts, pieces, solve, before_low, ahead],
-        [(4, ROWS, W), square, (256, 256), (W, 3 * W)],
+        [where, groups, pieces, solve, before_low],
+        [(4, ROWS, W), square, (256, 256)],
     )
     parts = lax.all_to_all(root, "y", 0, 0, tiled=True)
     (root,) = call(sum_kernel, [parts], [(8 * SHARES, ROWS, W)])
@@ -386,12 +395,12 @@
         root_kernel,
         [
             where, sums, rhs_root, root_lower_inverse, root_upper_inverse, carry, solve, ends,
-            upper_inverse, upper_link, upper_root,
+            groups, upper_inverse, upper_link, upper_root,
         ],
-        [(1, 512), (256, W), (8, 32, W)],
+        [(1, 512), (256, W), (8, 64, W)],
     )
     parts = lax.all_to_all(offset, ("x", "c"), 0, 0, tiled=True)
-    (offset,) = call(offset_kernel, [where, parts, gather, sent], [(16, 16, W)])
+    (offset,) = call(offset_kernel, [where, parts, gather, ahead], [(16, 16, W)])
     planes = lax.all_to_all(offset, ("zh",) + LOW, 0, 0, tiled=True)
     (states,) = call(carry_kernel, [where, planes, within, parts, spread], [(8, 32, W)])
     states = lax.all_to_all(states, ("x", "c"), 0, 0, tiled=True)

time: 151 us -> 148 us (0.980)
  blocking collectives: 135 us -> 132 us
    all_gather x3 -> x2, blocking collectives: 7.11 us -> 4.74 us  [on_device(): pieces = lax.all_gather(parts[:, :96], 'c')]
    all_to_all x1, blocking collectives: 23.4 us -> 21.3 us  [on_device(): planes = lax.all_to_all(offset, ('zh',) + LOW, 0, 0, tiled=True)]
    all_gather x1 -> x2, blocking collectives: 29.4 us -> 29.7 us  [the longest x1 27.5 us: on_device(): groups = lax.all_gather(out, 'zh')]
where the time goes in v8:
time: 148 us; the launch traced here: 146 us
  blocking collectives  132 us (89%)
  Pallas kernels  12.5 us (8%)
    all_gather x1, blocking collectives, on_device(): groups = lax.all_gather(out, 'zh')  27.5 us
    all_to_all x1, blocking collectives, on_device(): planes = lax.all_to_all(offset, ('zh',) + LOW, 0, 0, tiled=True)  21.3 us
    all_to_all x1, blocking collectives, on_device(): parts = lax.all_to_all(out, 'x', 0, 0, tiled=True)  17.7 us
    all_gather x1, blocking collectives, on_device(): parts = lax.all_gather(out, LOW)  16.8 us
    pallas_call x10, Pallas kernels, call(): pl.pallas_call(kernel, out_shape=[jax.ShapeDtypeStruct(shape, F32) for sh...  12.5 us
    all_to_all x1, blocking collectives, on_device(): sums = lax.all_to_all(root, SHARE + ('x', 'c'), 0, 0, tiled=True)  10.3 us
    all_to_all x1, blocking collectives, on_device(): parts = lax.all_to_all(offset, ('x', 'c'), 0, 0, tiled=True)  10.1 us
    all_to_all x1, blocking collectives, on_device(): parts = lax.all_to_all(root, 'y', 0, 0, tiled=True)  10 us

profile of v8, /device:TPU:6, one launch (start us, length us, event | category | flops | bytes accessed | tf_op | source)
XLA Modules:
  0.0 145.8 jit_solution(11519673586296527784)
XLA Ops:
  1.3 0.1 stack.23.where
  1.4 2.3 %shard_map.122 = (f32[256,256]{1,0:T(8,128)S(1)}, f32[448,256]{1,0:T(8,128)S(1)}, f32[256,256]{1,0:T(8,128)S(1)}) custom-call(s32[6]{0:T(128)S(1)} %stack.23.where, bf16[1,2,128,128]{3,2,1,0:T(8,128)(2,1)} %linv_in.1, bf16[1,2,128,128]{3,2,1,0:T(8,128)(2,1)} %llink_in.1, bf16[1,2,128,128]{3,2,1,0:T(8,128)(2,1)} %rhs_in.1, bf16[1,2,128,128]{3,2,1,0:T(8,128)(2,1)} %uinv.1, ...), custom_call_target="tpu_custom_call" | custom-call | tf_op jit(solution)/shard_map/pallas_call | solution.py:329
  3.7 2.5 %all-gather = f32[896,256]{1,0:T(8,128)S(1)} all-gather(f32[448,256]{1,0:T(8,128)S(1)} %get-tuple-element.25), channel_id=2, replica_groups=mesh['zh'=4,'za'=2,'zb'=2,'x'=4,'c'=2,'y'=4] {'c'}, dimensions={0}, use_global_device_ids=true | all-gather | bytes 1376256 | tf_op jit(solution)/shard_map/all_gather | solution.py:365
  6.2 0.9 shard_map.123
  7.1 17.7 %all_to_all.30.parts = f32[4,160,256]{2,1,0:T(8,128)S(1)} all-to-all(f32[4,160,256]{2,1,0:T(8,128)S(1)} %get-tuple-element.27), channel_id=1, replica_groups=mesh['zh'=4,'za'=2,'zb'=2,'x'=4,'c'=2,'y'=4] {'x'}, dimensions={0} | all-to-all | bytes 1310720 | tf_op jit(solution)/shard_map/all_to_all | solution.py:371
  24.8 2.4 %all-gather.1 = f32[8,96,256]{2,1,0:T(8,128)S(1)} all-gather(f32[4,96,256]{2,1,0:T(8,128)S(1)} %slice.12), channel_id=3, replica_groups=mesh['zh'=4,'za'=2,'zb'=2,'x'=4,'c'=2,'y'=4] {'c'}, dimensions={0}, use_global_device_ids=true | all-gather | bytes 1179648 | tf_op jit(solution)/shard_map/all_gather | solution.py:372
  27.1 1.1 shard_map.124
  28.2 16.8 %all-gather.2 = f32[640,256]{1,0:T(8,128)S(1)} all-gather(f32[160,256]{1,0:T(8,128)S(1)} %get-tuple-element.28), channel_id=4, replica_groups=mesh['zh'=4,'za'=2,'zb'=2,'x'=4,'c'=2,'y'=4] {'za','zb'}, dimensions={0}, use_global_device_ids=true | all-gather | bytes 819200 | tf_op jit(solution)/shard_map/all_gather | solution.py:376
  45.1 2.4 %all-gather.3 = f32[8,96,256]{2,1,0:T(8,128)S(1)} all-gather(f32[4,96,256]{2,1,0:T(8,128)S(1)} %slice.13), channel_id=5, replica_groups=mesh['zh'=4,'za'=2,'zb'=2,'x'=4,'c'=2,'y'=4] {'c'}, dimensions={0}, use_global_device_ids=true | all-gather | bytes 1179648 | tf_op jit(solution)/shard_map/all_gather | solution.py:377
  47.5 1.2 shard_map.125
  48.6 27.5 %all-gather.4 = f32[416,256]{1,0:T(8,128)S(1)} all-gather(f32[104,256]{1,0:T(8,128)S(1)} %get-tuple-element.31), channel_id=6, replica_groups=mesh['zh'=4,'za'=2,'zb'=2,'x'=4,'c'=2,'y'=4] {'zh'}, dimensions={0}, use_global_device_ids=true | all-gather | bytes 532480 | tf_op jit(solution)/shard_map/all_gather | solution.py:384
  76.2 2.2 %all-gather.5 = f32[8,64,256]{2,1,0:T(8,128)S(1)} all-gather(f32[4,64,256]{2,1,0:T(8,128)S(1)} %slice.14), channel_id=7, replica_groups=mesh['zh'=4,'za'=2,'zb'=2,'x'=4,'c'=2,'y'=4] {'c'}, dimensions={0}, use_global_device_ids=true | all-gather | bytes 786432 | tf_op jit(solution)/shard_map/all_gather | solution.py:385
  78.4 1.1 shard_map.126
  79.4 0.0 copy-start
  79.5 10.0 %all_to_all.31.parts = f32[4,32,128]{2,1,0:T(8,128)S(1)} all-to-all(f32[4,32,128]{2,1,0:T(8,128)S(1)} %get-tuple-element.34), channel_id=1, replica_groups=mesh['zh'=4,'za'=2,'zb'=2,'x'=4,'c'=2,'y'=4] {'y'}, dimensions={0} | all-to-all | bytes 131072 | tf_op jit(solution)/shard_map/all_to_all | solution.py:391
  89.5 0.0 copy-start.2
  89.5 0.0 copy-start.3
  89.5 0.0 copy-start.4
  89.6 10.3 %all_to_all.32.sums = f32[16,32,128]{2,1,0:T(8,128)S(1)} all-to-all(f32[16,32,128]{2,1,0:T(8,128)S(1)} %shard_map.127), channel_id=1, replica_groups=mesh['zh'=4,'za'=2,'zb'=2,'x'=4,'c'=2,'y'=4] {'zb','x','c'}, dimensions={0} | all-to-all | bytes 524288 | tf_op jit(solution)/shard_map/all_to_all | solution.py:393
  99.9 0.0 copy-done.1
  99.9 0.0 copy-done.5
  99.9 0.0 copy-done
  99.9 0.0 copy-done.2
  99.9 0.0 copy-done.3
  99.9 0.0 copy-done.4
  99.9 2.5 %shard_map.128 = (f32[1,512]{1,0:T(1,128)}, f32[256,128]{1,0:T(8,128)S(1)}, f32[8,64,128]{2,1,0:T(8,128)S(1)}) custom-call(s32[6]{0:T(128)S(1)} %stack.23.where, f32[16,32,128]{2,1,0:T(8,128)S(1)} %all_to_all.32.sums, bf16[512,128]{1,0:T(8,128)(2,1)S(1)} %copy-done.5, bf16[512,512]{1,0:T(8,128)(2,1)S(1)} %copy-done, bf16[512,512]{1,0:T(8,128)(2,1)S(1)} %copy-done.1, ...), custom_call_target="tpu_custom_call" | custom-call | tf_op jit(solution)/shard_map/pallas_call | solution.py:329
  102.4 10.1 %all_to_all.33.parts = f32[8,64,128]{2,1,0:T(8,128)S(1)} all-to-all(f32[8,64,128]{2,1,0:T(8,128)S(1)} %get-tuple-element.38), channel_id=1, replica_groups=mesh['zh'=4,'za'=2,'zb'=2,'x'=4,'c'=2,'y'=4] {'x','c'}, dimensions={0} | all-to-all | bytes 524288 | tf_op jit(solution)/shard_map/all_to_all | solution.py:402
  112.5 1.1 shard_map.129
  113.7 21.3 %all_to_all.34.planes = f32[16,16,128]{2,1,0:T(8,128)S(1)} all-to-all(f32[16,16,128]{2,1,0:T(8,128)S(1)} %shard_map.129), channel_id=1, replica_groups=mesh['zh'=4,'za'=2,'zb'=2,'x'=4,'c'=2,'y'=4] {'zh','za','zb'}, dimensions={0} | all-to-all | bytes 262144 | tf_op jit(solution)/shard_map/all_to_all | solution.py:404
  134.9 0.9 shard_map.130
  135.8 8.5 %all_to_all.35.parts = f32[8,32,128]{2,1,0:T(8,128)S(1)} all-to-all(f32[8,32,128]{2,1,0:T(8,128)S(1)} %shard_map.130), channel_id=1, replica_groups=mesh['zh'=4,'za'=2,'zb'=2,'x'=4,'c'=2,'y'=4] {'x','c'}, dimensions={0} | all-to-all | bytes 262144 | tf_op jit(solution)/shard_map/all_to_all | solution.py:406
  144.3 1.5 %shard_map.131 = f32[1,2,128,128]{3,2,1,0:T(8,128)} custom-call(s32[6]{0:T(128)S(1)} %stack.23.where, f32[8,32,128]{2,1,0:T(8,128)S(1)} %all_to_all.35.parts, f32[256,256]{1,0:T(8,128)S(1)} %get-tuple-element.43.last, f32[256,128]{1,0:T(8,128)S(1)} %get-tuple-element.44.plain), custom_call_target="tpu_custom_call" | custom-call | tf_op jit(solution)/shard_map/pallas_call | solution.py:329
  (6 shorter events, 0.1 us)
Async XLA Ops:
  78.4 21.6 %copy-start.1 = (bf16[512,512]{1,0:T(8,128)(2,1)S(1)}, bf16[512,512]{1,0:T(8,128)(2,1)}, u32[]{:S(2)}) copy-start(bf16[512,512]{1,0:T(8,128)(2,1)} %root_upper.1) | copy-start | bytes 1572868
  78.4 21.6 %copy-start.5 = (bf16[512,128]{1,0:T(8,128)(2,1)S(1)}, bf16[512,128]{1,0:T(8,128)(2,1)}, u32[]{:S(2)}) copy-start(bf16[512,128]{1,0:T(8,128)(2,1)} %rhs_root.1) | copy-start | bytes 393220
  79.4 20.5 %copy-start = (bf16[512,512]{1,0:T(8,128)(2,1)S(1)}, bf16[512,512]{1,0:T(8,128)(2,1)}, u32[]{:S(2)}) copy-start(bf16[512,512]{1,0:T(8,128)(2,1)} %root_lower.1) | copy-start | bytes 1572868
  89.5 10.4 %copy-start.2 = (bf16[1,2,128,512]{3,2,1,0:T(8,128)(2,1)S(1)}, bf16[1,2,128,512]{3,2,1,0:T(8,128)(2,1)}, u32[]{:S(2)}) copy-start(bf16[1,2,128,512]{3,2,1,0:T(8,128)(2,1)} %uroot.1) | copy-start | bytes 786436
  89.5 10.4 %copy-start.3 = (bf16[1,2,128,128]{3,2,1,0:T(8,128)(2,1)S(1)}, bf16[1,2,128,128]{3,2,1,0:T(8,128)(2,1)}, u32[]{:S(2)}) copy-start(bf16[1,2,128,128]{3,2,1,0:T(8,128)(2,1)} %uinv.1) | copy-start | bytes 196612
  89.5 10.4 %copy-start.4 = (bf16[1,2,128,128]{3,2,1,0:T(8,128)(2,1)S(1)}, bf16[1,2,128,128]{3,2,1,0:T(8,128)(2,1)}, u32[]{:S(2)}) copy-start(bf16[1,2,128,128]{3,2,1,0:T(8,128)(2,1)} %ulink.1) | copy-start | bytes 196612

commit v9 on v8

--- a/solution.py
+++ b/solution.py
@@ -14,6 +14,8 @@
 SHARE = ("zb",)
 SHARES = 2
 ROWS = 64 // SHARES
+HIGH, PLANE, CHIP, CORE, COLUMN, LIVE, ODD, PIECE = range(8)
+MARKS = (8, 512)
 
 
 def dot(left, right):
@@ -57,6 +59,17 @@
     return jnp.concatenate([packed[:, :W], packed[:, W:]], 0)
 
 
+def choose(mark, value, one, other):
+    return jnp.where(jnp.broadcast_to(mark[:, : one.shape[1]], one.shape) == value, one, other)
+
+
+def pick(mark, *values):
+    chosen = values[-1]
+    for k in reversed(range(len(values) - 1)):
+        chosen = choose(mark, k, values[k], chosen)
+    return chosen
+
+
 def eye():
     rows = lax.broadcasted_iota(jnp.int32, (W, W), 0)
     cols = lax.broadcasted_iota(jnp.int32, (W, W), 1)
@@ -64,7 +77,7 @@
 
 
 def slots_kernel(
-    where, linv_in, llink_in, rhs_in, uinv_in, ulink_in, lroot_in, keep, send, ahead,
+    where, linv_in, llink_in, rhs_in, uinv_in, ulink_in, lroot_in, keep, send, ahead, marks,
     linv, llink, rhs, uinv, ulink, lroot, sems,
 ):
     sources = (linv_in, llink_in, rhs_in, uinv_in, ulink_in, lroot_in)
@@ -76,6 +89,11 @@
     for copy in copies:
         copy.start()
     core, both = where[3], where[5] == 2
+    rows = lax.broadcasted_iota(jnp.int32, MARKS, 0)
+    made = jnp.zeros(MARKS, jnp.int32)
+    for k in range(8):
+        made = jnp.where(rows == k, where[k], made)
+    marks[...] = made
     for copy in copies[:3]:
         copy.wait()
     maps = []
@@ -102,25 +120,24 @@
 
 def half(core, rows):
     middle = rows.shape[0] // 2
-    return jnp.where(core == 0, rows[:middle], rows[middle:])
+    return choose(core, 0, rows[:middle], rows[middle:])
 
 
 def after(map_rows, ahead):
     return mul3(map_rows[:, :W], ahead) + shift(map_rows[:, W:])
 
 
-def chip_kernel(where, keep, pair, ahead, out, solve, ends, last):
-    core = where[3]
-    first = core == 0
+def chip_kernel(marks, keep, pair, ahead, out, solve, ends, last):
+    core = marks[CORE : CORE + 1]
     head, tail = pair[0, :W], pair[1, :W]
     root_mine = keep[...]
-    root_head = jnp.where(first, root_mine, pair[0, W + W // 2 :])
-    root_tail = jnp.where(first, pair[1, W + W // 2 :], root_mine)
+    root_head = choose(core, 0, root_mine, pair[0, W + W // 2 :])
+    root_tail = choose(core, 0, pair[1, W + W // 2 :], root_mine)
     slot = ahead[:W]
     made = after(jnp.concatenate([tail, slot, root_tail], 0), head)
     chain, root = made[:W], root_head + made[2 * W :]
-    solve[:W] = jnp.where(first, slot, made[W : 2 * W])
-    solve[W:] = jnp.where(first, head, chain)
+    solve[:W] = choose(core, 0, slot, made[W : 2 * W])
+    solve[W:] = choose(core, 0, head, chain)
     back_head, back_tail = [unpack(pair[k, W : W + W // 2]) for k in range(2)]
     chain_half = half(core, chain)
     back_half = half(core, pack(mul3(back_tail, back_head)))
@@ -130,8 +147,8 @@
         out[other, 96:] = root[64 * other : 64 * other + 64]
     ends[...] = back_head.T
     answer = jnp.concatenate([ahead[W:, :W], ahead[W:, W:]], 0)
-    last[:, :W] = jnp.where(first, mul3(answer, back_tail.T), answer)
-    last[:, W:] = jnp.where(first, answer, F32(0))
+    last[:, :W] = choose(core, 0, mul3(answer, back_tail.T), answer)
+    last[:, W:] = choose(core, 0, answer, jnp.zeros_like(answer))
 
 
 def compose(place, maps, roots):
@@ -141,11 +158,7 @@
     one, two = one[:W], two[:W]
     made = after(jnp.concatenate([maps[2], two, root_two], 0), one)
     start = jnp.concatenate([eye(), jnp.zeros((W, W), F32)], 1)
-    before = jnp.where(
-        place == 0,
-        start,
-        jnp.where(place == 1, maps[0], jnp.where(place == 2, one, made[:W])),
-    )
+    before = pick(place, start, maps[0], one, made[:W])
     return made[W : 2 * W], root_one + made[2 * W :], before
 
 
@@ -160,10 +173,10 @@
     return maps, [unpack(packed) for packed in backs]
 
 
-def plane_kernel(where, parts, pieces, out, before, gather, spread):
-    core = where[3]
+def plane_kernel(marks, parts, pieces, out, before, gather, spread):
+    core = marks[CORE : CORE + 1]
     maps, backs = joined(pieces)
-    chain, root, prefix = compose(where[2], maps, [parts[k, 96:] for k in range(4)])
+    chain, root, prefix = compose(marks[CHIP : CHIP + 1], maps, [parts[k, 96:] for k in range(4)])
     before[...] = prefix
     p10, p21, p32, p210, p321, total = products(backs)
     out[:64] = half(core, chain)
@@ -175,25 +188,19 @@
         spread[:, W * k : W * k + W] = value
 
 
-def pick(place, *values):
-    chosen = values[-1]
-    for k in reversed(range(len(values) - 1)):
-        chosen = jnp.where(place == k, values[k], chosen)
-    return chosen
-
-
 def group_kernel(
-    where, parts, pieces, solve, before_x, out, before, solve_out, ahead, within, back_ref,
+    marks, parts, pieces, solve, before_x, out, before, solve_out, ahead, within,
 ):
-    core, place = where[3], where[1]
-    share = pl.ds(pl.multiple_of(96 + lax.rem(place, SHARES) * ROWS, ROWS), ROWS)
+    core, place = marks[CORE : CORE + 1], marks[PLANE : PLANE + 1]
+    odd = marks[ODD : ODD + 1]
     maps, backs = joined(pieces)
-    chain, root, prefix = compose(place, maps, [parts[k, share] for k in range(4)])
+    roots = [choose(odd, 0, parts[k, 96 : 96 + ROWS], parts[k, 96 + ROWS :]) for k in range(4)]
+    chain, root, prefix = compose(place, maps, roots)
     before[...] = prefix
     p10, p21, p32, p210, p321, total = products(backs)
     out[:64] = half(core, chain)
-    back_ref[...] = pack(total)
-    out[64:72] = back_ref[pl.ds(pl.multiple_of(32 * core + 8 * where[2], 8), 8)]
+    packed = pack(total)
+    out[64:72] = pick(marks[PIECE : PIECE + 1], *[packed[8 * k : 8 * k + 8] for k in range(8)])
     out[72:] = root
     solve_out[...] = after(solve[...], before_x[...])
     one, none = eye(), jnp.zeros((W, W), F32)
@@ -204,8 +211,8 @@
     within[3 * W :] = pick(place, p21, backs[2], one, none)
 
 
-def top_kernel(where, parts, pieces, solve, before_low, root, carry, solve_out):
-    place = where[0]
+def top_kernel(marks, parts, pieces, solve, before_low, root, carry, solve_out):
+    place = marks[HIGH : HIGH + 1]
     maps = [jnp.concatenate([pieces[0, k], pieces[1, k]], 0) for k in range(4)]
     roots = [parts[k, 72:] for k in range(4)]
     total = roots[0][:, W:]
@@ -229,17 +236,17 @@
 
 
 def root_kernel(
-    where, sums, rhs_root, root_lower, root_upper, carry, solve, ends, groups, uinv, ulink,
+    marks, sums, rhs_root, root_lower, root_upper, carry, solve, ends, groups, uinv, ulink,
     uroot, own_root, plain, offset,
 ):
-    core, both = where[3], where[5] == 2
     order = [(k * 4 + x) * 2 + c for c in range(2) for x in range(4) for k in range(SHARES)]
     summed = jnp.concatenate([sums[k] for k in order], 0)
     inner = mul2(root_lower[...], rhs_root[...].astype(F32) - summed)
     root = mul2(root_upper[...], inner)
     solved = mul3(solve[:, :W], carry[...]) + solve[:, W:]
     first, second = uinv[0, 0].astype(F32), uinv[0, 1].astype(F32)
-    link = jnp.where(both, -dot(uinv[0, 0], ulink[0, 0]), F32(0))
+    link = -dot(uinv[0, 0], ulink[0, 0])
+    link = choose(marks[LIVE : LIVE + 1], 2, link, jnp.zeros_like(link))
     over = mul3(link, second)
     moved = mul3(ends[...], jnp.concatenate([first, over], 1))
     parts = mul2(jnp.concatenate([uroot[0, 0], uroot[0, 1]], 0), root)
@@ -250,7 +257,7 @@
     plain[:W] = whole[:W]
     plain[W:] = on_second[2 * W :]
     turned = whole[:W].T
-    carried = jnp.where(core == 0, whole[:W], whole[W:]).T
+    carried = choose(marks[CORE : CORE + 1], 0, whole[:W], whole[W:]).T
     for other in range(8):
         rows = slice(16 * other, 16 * other + 16)
         offset[other, :16] = carried[rows]
@@ -260,14 +267,16 @@
             offset[other, at : at + 8] = groups[k + 1, 64:72, :W]
             offset[other, at + 8 : at + 16] = groups[k + 1, 64:72, W:]
     columns = lax.broadcasted_iota(jnp.int32, (W, 512), 0)
-    own_root[...] = jnp.sum(jnp.where(columns == where[4], root.T, F32(0)), 0, keepdims=True)
+    own = jnp.broadcast_to(marks[COLUMN : COLUMN + 1], (W, 512)) == columns
+    own_root[...] = jnp.sum(jnp.where(own, root.T, F32(0)), 0, keepdims=True)
 
 
 def chip_offsets(parts):
     return [parts[2 * k, :16] + parts[2 * k + 1, :16] for k in range(4)]
 
 
-def offset_kernel(where, parts, gather, ahead, out):
+def offset_kernel(marks, parts, gather, ahead, out):
+    group = marks[HIGH : HIGH + 1]
     backs = []
     for at in (32, 48):
         order = [2 * x + core for core in range(2) for x in range(4)]
@@ -276,20 +285,21 @@
         backs.append(jnp.concatenate(sides, 0))
     state = mul3(jnp.concatenate(chip_offsets(parts), 1), gather[...])
     one = mul3(state, ahead[...])
-    two = mul3(one, jnp.where(where[0] == 3, backs[1], backs[0]))
+    two = mul3(one, choose(group, 3, backs[1], backs[0]))
     values = [state, one, two, mul3(two, backs[0])]
     for other in range(4):
-        value = pick(where[0] - other, *values)
+        value = pick(group - other, *values)
         for k in range(4):
             out[4 * other + k] = value
 
 
-def carry_kernel(where, planes, within, parts, spread, out):
-    group = where[0]
+def carry_kernel(marks, planes, within, parts, spread, out):
+    group = marks[HIGH : HIGH + 1]
+    apart = jnp.broadcast_to(group[:, :W], (16, W))
     state = jnp.zeros((16, W), F32)
     for k in range(4, 16):
-        state = state + jnp.where(k // 4 > group, planes[k], F32(0))
-    offsets = [planes[4 * group + k] for k in range(1, 4)]
+        state = state + jnp.where(apart < k // 4, planes[k], F32(0))
+    offsets = [pick(group, *[planes[4 * g + k] for g in range(4)]) for k in range(1, 4)]
     state = mul3(jnp.concatenate([state] + offsets, 1), within[...])
     chips = chip_offsets(parts)
     moved = mul3(chips[3], spread[:, 3 * W : 5 * W])
@@ -306,19 +316,20 @@
             out[2 * k + core, 16:] = parts[2 * k + 1, 16:32]
 
 
-def answer_kernel(where, parts, last, plain, out):
+def answer_kernel(marks, parts, last, plain, column, out, own_root):
     state = jnp.concatenate([parts[k, :16] for k in range(8)], 0).T
     other = jnp.concatenate([parts[k, 16:] for k in range(8)], 0).T
     made = mul3(last[...], jnp.concatenate([state, other], 0)) + plain[...]
     out[0, 0] = made[:W]
-    out[0, 1] = jnp.where(where[5] == 2, made[W:], F32(0))
-
-
-def call(kernel, inputs, shapes, fetched=False, scratch=()):
+    out[0, 1] = choose(marks[LIVE : LIVE + 1], 2, made[W:], jnp.zeros_like(made[W:]))
+    own_root[...] = column[...]
+
+
+def call(kernel, inputs, shapes, fetched=False):
     vmem = pl.BlockSpec(memory_space=pltpu.VMEM)
     smem = pl.BlockSpec(memory_space=pltpu.SMEM)
     block = pl.BlockSpec(memory_space=pltpu.HBM) if fetched else vmem
-    scratch = [pltpu.VMEM(shape, F32) for shape in scratch]
+    scratch = []
     if fetched:
         scratch = [pltpu.VMEM(a.shape, a.dtype) for a in inputs if a.dtype == BF16]
         scratch.append(pltpu.SemaphoreType.DMA((len(scratch),)))
@@ -328,9 +339,11 @@
         ]
     return pl.pallas_call(
         kernel,
-        out_shape=[jax.ShapeDtypeStruct(shape, F32) for shape in shapes],
+        out_shape=[
+            jax.ShapeDtypeStruct(shape, jnp.int32 if shape == MARKS else F32) for shape in shapes
+        ],
         in_specs=[
-            smem if a.dtype == jnp.int32 else block if a.dtype == BF16 else vmem for a in inputs
+            smem if a.ndim == 1 else block if a.dtype == BF16 else vmem for a in inputs
         ],
         out_specs=[vmem] * len(shapes),
         scratch_shapes=scratch,
@@ -353,58 +366,60 @@
 ):
     places = [lax.axis_index(axes) for axes in ("zh", LOW, "x", "c")]
     column = ((places[0] * 4 + places[1]) * 4 + places[2]) * 2 + places[3]
-    where = jnp.stack(places + [column, live_counts[0, 0]]).astype(jnp.int32)
+    odd, piece = lax.axis_index("zb"), 4 * places[3] + places[2]
+    where = jnp.stack(places + [column, live_counts[0, 0], odd, piece]).astype(jnp.int32)
     square, wide = (W, W), (W, 2 * W)
 
-    keep, send, ahead = call(
+    keep, send, ahead, marks = call(
         slots_kernel,
         [where, lower_inverse, lower_link, rhs_blocks, upper_inverse, upper_link, lower_root],
-        [(256, 256), (448, 256), (256, 256)],
+        [(256, 256), (448, 256), (256, 256), MARKS],
         fetched=True,
     )
     pair = lax.all_gather(send, "c")
     out, solve, ends, last = call(
         chip_kernel,
-        [where, keep, pair, ahead],
+        [marks, keep, pair, ahead],
         [(4, 160, 256), (256, 256), square, (256, 256)],
     )
     parts = lax.all_to_all(out, "x", 0, 0, tiled=True)
     pieces = lax.all_gather(parts[:, :96], "c")
     out, before_x, gather, spread = call(
-        plane_kernel, [where, parts, pieces], [(160, 256), wide, (4 * W, W), (W, 6 * W)]
+        plane_kernel, [marks, parts, pieces], [(160, 256), wide, (4 * W, W), (W, 6 * W)]
     )
     parts = lax.all_gather(out, LOW)
     pieces = lax.all_gather(parts[:, :96], "c")
     out, before_low, solve, ahead, within = call(
         group_kernel,
-        [where, parts, pieces, solve, before_x],
+        [marks, parts, pieces, solve, before_x],
         [(72 + ROWS, 256), wide, (256, 256), square, (4 * W, W)],
-        scratch=[(64, 256)],
     )
     groups = lax.all_gather(out, "zh")
     pieces = lax.all_gather(groups[:, :64], "c")
     root, carry, solve = call(
         top_kernel,
-        [where, groups, pieces, solve, before_low],
+        [marks, groups, pieces, solve, before_low],
         [(4, ROWS, W), square, (256, 256)],
     )
     parts = lax.all_to_all(root, "y", 0, 0, tiled=True)
     (root,) = call(sum_kernel, [parts], [(8 * SHARES, ROWS, W)])
     sums = lax.all_to_all(root, SHARE + ("x", "c"), 0, 0, tiled=True)
-    own_root, plain, offset = call(
+    column, plain, offset = call(
         root_kernel,
         [
-            where, sums, rhs_root, root_lower_inverse, root_upper_inverse, carry, solve, ends,
+            marks, sums, rhs_root, root_lower_inverse, root_upper_inverse, carry, solve, ends,
             groups, upper_inverse, upper_link, upper_root,
         ],
         [(1, 512), (256, W), (8, 64, W)],
     )
     parts = lax.all_to_all(offset, ("x", "c"), 0, 0, tiled=True)
-    (offset,) = call(offset_kernel, [where, parts, gather, ahead], [(16, 16, W)])
+    (offset,) = call(offset_kernel, [marks, parts, gather, ahead], [(16, 16, W)])
     planes = lax.all_to_all(offset, ("zh",) + LOW, 0, 0, tiled=True)
-    (states,) = call(carry_kernel, [where, planes, within, parts, spread], [(8, 32, W)])
+    (states,) = call(carry_kernel, [marks, planes, within, parts, spread], [(8, 32, W)])
     states = lax.all_to_all(states, ("x", "c"), 0, 0, tiled=True)
-    (answers,) = call(answer_kernel, [where, states, last, plain], [(1, 2, W, W)])
+    answers, own_root = call(
+        answer_kernel, [marks, states, last, plain, column], [(1, 2, W, W), (1, 512)]
+    )
     return answers, own_root.reshape(512, 1)
 
 

time: 148 us -> 144 us (0.973)
  Pallas kernels: 12.5 us -> 7.64 us
    pallas_call x10, Pallas kernels: 12.5 us -> 7.64 us  [call(): pl.pallas_call(kernel, out_shape=[jax.ShapeDtypeStruct(shape, jnp.int32 i...]
where the time goes in v9:
time: 144 us; the launch traced here: 141 us
  blocking collectives  132 us (92%)
  Pallas kernels  7.64 us (5%)
  between operations  1.44 us (1%)
    all_gather x1, blocking collectives, on_device(): groups = lax.all_gather(out, 'zh')  27.2 us
    all_to_all x1, blocking collectives, on_device(): planes = lax.all_to_all(offset, ('zh',) + LOW, 0, 0, tiled=True)  22.1 us
    all_to_all x1, blocking collectives, on_device(): parts = lax.all_to_all(out, 'x', 0, 0, tiled=True)  17.7 us
    all_gather x1, blocking collectives, on_device(): parts = lax.all_gather(out, LOW)  16.8 us
    all_to_all x1, blocking collectives, on_device(): sums = lax.all_to_all(root, SHARE + ('x', 'c'), 0, 0, tiled=True)  10.5 us
    all_to_all x1, blocking collectives, on_device(): parts = lax.all_to_all(offset, ('x', 'c'), 0, 0, tiled=True)  10.2 us
    all_to_all x1, blocking collectives, on_device(): parts = lax.all_to_all(root, 'y', 0, 0, tiled=True)  9.44 us
    all_to_all x1, blocking collectives, on_device(): states = lax.all_to_all(states, ('x', 'c'), 0, 0, tiled=True)  8.52 us

profile of v9, /device:TPU:6, one launch (start us, length us, event | category | flops | bytes accessed | tf_op | source)
XLA Modules:
  0.0 141.0 jit_solution(9768738080129255810)
XLA Ops:
  1.3 0.1 stack.31.where
  1.4 2.3 %shard_map.122 = (f32[256,256]{1,0:T(8,128)S(1)}, f32[448,256]{1,0:T(8,128)S(1)}, f32[256,256]{1,0:T(8,128)S(1)}, s32[8,512]{1,0:T(8,128)S(1)}) custom-call(s32[8]{0:T(128)S(1)} %stack.31.where, bf16[1,2,128,128]{3,2,1,0:T(8,128)(2,1)} %linv_in.1, bf16[1,2,128,128]{3,2,1,0:T(8,128)(2,1)} %llink_in.1, bf16[1,2,128,128]{3,2,1,0:T(8,128)(2,1)} %rhs_in.1, ...), custom_call_target="tpu_custom_call" | custom-call | tf_op jit(solution)/shard_map/pallas_call | solution.py:340
  3.7 2.5 %all-gather = f32[896,256]{1,0:T(8,128)S(1)} all-gather(f32[448,256]{1,0:T(8,128)S(1)} %get-tuple-element.29), channel_id=2, replica_groups=mesh['zh'=4,'za'=2,'zb'=2,'x'=4,'c'=2,'y'=4] {'c'}, dimensions={0}, use_global_device_ids=true | all-gather | bytes 1376256 | tf_op jit(solution)/shard_map/all_gather | solution.py:379
  6.2 0.4 shard_map.123
  6.6 17.7 %all_to_all.30.parts = f32[4,160,256]{2,1,0:T(8,128)S(1)} all-to-all(f32[4,160,256]{2,1,0:T(8,128)S(1)} %get-tuple-element.31), channel_id=1, replica_groups=mesh['zh'=4,'za'=2,'zb'=2,'x'=4,'c'=2,'y'=4] {'x'}, dimensions={0} | all-to-all | bytes 1310720 | tf_op jit(solution)/shard_map/all_to_all | solution.py:385
  24.2 2.4 %all-gather.1 = f32[8,96,256]{2,1,0:T(8,128)S(1)} all-gather(f32[4,96,256]{2,1,0:T(8,128)S(1)} %slice.12), channel_id=3, replica_groups=mesh['zh'=4,'za'=2,'zb'=2,'x'=4,'c'=2,'y'=4] {'c'}, dimensions={0}, use_global_device_ids=true | all-gather | bytes 1179648 | tf_op jit(solution)/shard_map/all_gather | solution.py:386
  26.6 0.6 shard_map.124
  27.2 16.8 %all-gather.2 = f32[640,256]{1,0:T(8,128)S(1)} all-gather(f32[160,256]{1,0:T(8,128)S(1)} %get-tuple-element.32), channel_id=4, replica_groups=mesh['zh'=4,'za'=2,'zb'=2,'x'=4,'c'=2,'y'=4] {'za','zb'}, dimensions={0}, use_global_device_ids=true | all-gather | bytes 819200 | tf_op jit(solution)/shard_map/all_gather | solution.py:390
  44.0 2.4 %all-gather.3 = f32[8,96,256]{2,1,0:T(8,128)S(1)} all-gather(f32[4,96,256]{2,1,0:T(8,128)S(1)} %slice.13), channel_id=5, replica_groups=mesh['zh'=4,'za'=2,'zb'=2,'x'=4,'c'=2,'y'=4] {'c'}, dimensions={0}, use_global_device_ids=true | all-gather | bytes 1179648 | tf_op jit(solution)/shard_map/all_gather | solution.py:391
  46.4 0.6 shard_map.125
  47.0 27.2 %all-gather.4 = f32[416,256]{1,0:T(8,128)S(1)} all-gather(f32[104,256]{1,0:T(8,128)S(1)} %get-tuple-element.35), channel_id=6, replica_groups=mesh['zh'=4,'za'=2,'zb'=2,'x'=4,'c'=2,'y'=4] {'zh'}, dimensions={0}, use_global_device_ids=true | all-gather | bytes 532480 | tf_op jit(solution)/shard_map/all_gather | solution.py:397
  74.2 2.2 %all-gather.5 = f32[8,64,256]{2,1,0:T(8,128)S(1)} all-gather(f32[4,64,256]{2,1,0:T(8,128)S(1)} %slice.14), channel_id=7, replica_groups=mesh['zh'=4,'za'=2,'zb'=2,'x'=4,'c'=2,'y'=4] {'c'}, dimensions={0}, use_global_device_ids=true | all-gather | bytes 786432 | tf_op jit(solution)/shard_map/all_gather | solution.py:398
  76.4 0.5 shard_map.126
  76.9 0.0 copy-start
  77.0 9.4 %all_to_all.31.parts = f32[4,32,128]{2,1,0:T(8,128)S(1)} all-to-all(f32[4,32,128]{2,1,0:T(8,128)S(1)} %get-tuple-element.38), channel_id=1, replica_groups=mesh['zh'=4,'za'=2,'zb'=2,'x'=4,'c'=2,'y'=4] {'y'}, dimensions={0} | all-to-all | bytes 131072 | tf_op jit(solution)/shard_map/all_to_all | solution.py:404
  86.4 0.0 copy-start.2
  86.4 0.0 copy-start.3
  86.5 0.0 copy-start.4
  86.5 10.5 %all_to_all.32.sums = f32[16,32,128]{2,1,0:T(8,128)S(1)} all-to-all(f32[16,32,128]{2,1,0:T(8,128)S(1)} %shard_map.127), channel_id=1, replica_groups=mesh['zh'=4,'za'=2,'zb'=2,'x'=4,'c'=2,'y'=4] {'zb','x','c'}, dimensions={0} | all-to-all | bytes 524288 | tf_op jit(solution)/shard_map/all_to_all | solution.py:406
  96.9 0.0 copy-done.1
  96.9 0.0 copy-done.5
  96.9 0.0 copy-done
  96.9 0.0 copy-done.2
  97.0 0.0 copy-done.3
  97.0 0.0 copy-done.4
  97.0 1.4 shard_map.128
  98.3 10.2 %all_to_all.33.parts = f32[8,64,128]{2,1,0:T(8,128)S(1)} all-to-all(f32[8,64,128]{2,1,0:T(8,128)S(1)} %get-tuple-element.42), channel_id=1, replica_groups=mesh['zh'=4,'za'=2,'zb'=2,'x'=4,'c'=2,'y'=4] {'x','c'}, dimensions={0} | all-to-all | bytes 524288 | tf_op jit(solution)/shard_map/all_to_all | solution.py:415
  108.5 0.6 shard_map.129
  109.1 22.1 %all_to_all.34.planes = f32[16,16,128]{2,1,0:T(8,128)S(1)} all-to-all(f32[16,16,128]{2,1,0:T(8,128)S(1)} %shard_map.129), channel_id=1, replica_groups=mesh['zh'=4,'za'=2,'zb'=2,'x'=4,'c'=2,'y'=4] {'zh','za','zb'}, dimensions={0} | all-to-all | bytes 262144 | tf_op jit(solution)/shard_map/all_to_all | solution.py:417
  131.2 0.3 shard_map.130
  131.5 8.5 %all_to_all.35.parts = f32[8,32,128]{2,1,0:T(8,128)S(1)} all-to-all(f32[8,32,128]{2,1,0:T(8,128)S(1)} %shard_map.130), channel_id=1, replica_groups=mesh['zh'=4,'za'=2,'zb'=2,'x'=4,'c'=2,'y'=4] {'x','c'}, dimensions={0} | all-to-all | bytes 262144 | tf_op jit(solution)/shard_map/all_to_all | solution.py:419
  140.1 1.0 shard_map.131
  (6 shorter events, 0.1 us)
Async XLA Ops:
  76.4 20.5 %copy-start.1 = (bf16[512,512]{1,0:T(8,128)(2,1)S(1)}, bf16[512,512]{1,0:T(8,128)(2,1)}, u32[]{:S(2)}) copy-start(bf16[512,512]{1,0:T(8,128)(2,1)} %root_upper.1) | copy-start | bytes 1572868
  76.4 20.5 %copy-start.5 = (bf16[512,128]{1,0:T(8,128)(2,1)S(1)}, bf16[512,128]{1,0:T(8,128)(2,1)}, u32[]{:S(2)}) copy-start(bf16[512,128]{1,0:T(8,128)(2,1)} %rhs_root.1) | copy-start | bytes 393220
  76.9 20.0 %copy-start = (bf16[512,512]{1,0:T(8,128)(2,1)S(1)}, bf16[512,512]{1,0:T(8,128)(2,1)}, u32[]{:S(2)}) copy-start(bf16[512,512]{1,0:T(8,128)(2,1)} %root_lower.1) | copy-start | bytes 1572868
  86.4 10.5 %copy-start.2 = (bf16[1,2,128,512]{3,2,1,0:T(8,128)(2,1)S(1)}, bf16[1,2,128,512]{3,2,1,0:T(8,128)(2,1)}, u32[]{:S(2)}) copy-start(bf16[1,2,128,512]{3,2,1,0:T(8,128)(2,1)} %uroot.1) | copy-start | bytes 786436
  86.4 10.5 %copy-start.3 = (bf16[1,2,128,128]{3,2,1,0:T(8,128)(2,1)S(1)}, bf16[1,2,128,128]{3,2,1,0:T(8,128)(2,1)}, u32[]{:S(2)}) copy-start(bf16[1,2,128,128]{3,2,1,0:T(8,128)(2,1)} %uinv.1) | copy-start | bytes 196612
  86.5 10.5 %copy-start.4 = (bf16[1,2,128,128]{3,2,1,0:T(8,128)(2,1)S(1)}, bf16[1,2,128,128]{3,2,1,0:T(8,128)(2,1)}, u32[]{:S(2)}) copy-start(bf16[1,2,128,128]{3,2,1,0:T(8,128)(2,1)} %ulink.1) | copy-start | bytes 196612

commit v10 on v9

--- a/solution.py
+++ b/solution.py
@@ -77,7 +77,7 @@
 
 
 def slots_kernel(
-    where, linv_in, llink_in, rhs_in, uinv_in, ulink_in, lroot_in, keep, send, ahead, marks,
+    marks, linv_in, llink_in, rhs_in, uinv_in, ulink_in, lroot_in, keep, send, ahead,
     linv, llink, rhs, uinv, ulink, lroot, sems,
 ):
     sources = (linv_in, llink_in, rhs_in, uinv_in, ulink_in, lroot_in)
@@ -88,12 +88,7 @@
     ]
     for copy in copies:
         copy.start()
-    core, both = where[3], where[5] == 2
-    rows = lax.broadcasted_iota(jnp.int32, MARKS, 0)
-    made = jnp.zeros(MARKS, jnp.int32)
-    for k in range(8):
-        made = jnp.where(rows == k, where[k], made)
-    marks[...] = made
+    core, live = marks[CORE : CORE + 1], marks[LIVE : LIVE + 1]
     for copy in copies[:3]:
         copy.wait()
     maps = []
@@ -101,21 +96,21 @@
         made = dot(linv[0, slot], jnp.concatenate([llink[0, slot], rhs[0, slot]], 1))
         maps.append(jnp.concatenate([-made[:, :W], made[:, W:]], 1))
     chain = mul3(maps[1][:, :W], maps[0]) + shift(maps[1][:, W:])
-    chain = jnp.where(both, chain, maps[0])
+    chain = choose(live, 2, chain, maps[0])
     send[:W] = chain
     for copy in copies[3:]:
         copy.wait()
     links = [-dot(uinv[0, slot], ulink[0, slot]) for slot in range(2)]
-    back = jnp.where(both, mul3(links[0], links[1]), links[0])
+    back = choose(live, 2, mul3(links[0], links[1]), links[0])
     send[W : W + W // 2] = pack(back.T)
     ahead[:W] = maps[0]
     ahead[W:] = jnp.concatenate([back, links[1]], 1)
-    second = jnp.where(both, chain, F32(0))
+    second = choose(live, 2, chain, jnp.zeros_like(chain))
     ahead_high, ahead_low = halves(jnp.concatenate([maps[0], second], 0))
-    for part, target, at in ((core, keep, 0), (1 - core, send, W + W // 2)):
-        rows = pl.ds(pl.multiple_of(part * 256, 256), 256)
-        blocks = jnp.concatenate([lroot[0, 0, rows], lroot[0, 1, rows]], 1)
-        target[at : at + 256] = dot(blocks, ahead_high) + dot(blocks, ahead_low)
+    blocks = jnp.concatenate([lroot[0, 0], lroot[0, 1]], 1)
+    made = dot(blocks, ahead_high) + dot(blocks, ahead_low)
+    keep[...] = choose(core, 0, made[:256], made[256:])
+    send[W + W // 2 :] = choose(core, 0, made[256:], made[:256])
 
 
 def half(core, rows):
@@ -327,7 +322,6 @@
 
 def call(kernel, inputs, shapes, fetched=False):
     vmem = pl.BlockSpec(memory_space=pltpu.VMEM)
-    smem = pl.BlockSpec(memory_space=pltpu.SMEM)
     block = pl.BlockSpec(memory_space=pltpu.HBM) if fetched else vmem
     scratch = []
     if fetched:
@@ -339,12 +333,8 @@
         ]
     return pl.pallas_call(
         kernel,
-        out_shape=[
-            jax.ShapeDtypeStruct(shape, jnp.int32 if shape == MARKS else F32) for shape in shapes
-        ],
-        in_specs=[
-            smem if a.ndim == 1 else block if a.dtype == BF16 else vmem for a in inputs
-        ],
+        out_shape=[jax.ShapeDtypeStruct(shape, F32) for shape in shapes],
+        in_specs=[block if a.dtype == BF16 else vmem for a in inputs],
         out_specs=[vmem] * len(shapes),
         scratch_shapes=scratch,
         compiler_params=pltpu.CompilerParams(vmem_limit_bytes=32 * 1024 * 1024),
@@ -367,13 +357,14 @@
     places = [lax.axis_index(axes) for axes in ("zh", LOW, "x", "c")]
     column = ((places[0] * 4 + places[1]) * 4 + places[2]) * 2 + places[3]
     odd, piece = lax.axis_index("zb"), 4 * places[3] + places[2]
-    where = jnp.stack(places + [column, live_counts[0, 0], odd, piece]).astype(jnp.int32)
+    marks = jnp.stack(places + [column, live_counts[0, 0], odd, piece]).astype(jnp.int32)
+    marks = jnp.broadcast_to(marks[:, None], MARKS)
     square, wide = (W, W), (W, 2 * W)
 
-    keep, send, ahead, marks = call(
+    keep, send, ahead = call(
         slots_kernel,
-        [where, lower_inverse, lower_link, rhs_blocks, upper_inverse, upper_link, lower_root],
-        [(256, 256), (448, 256), (256, 256), MARKS],
+        [marks, lower_inverse, lower_link, rhs_blocks, upper_inverse, upper_link, lower_root],
+        [(256, 256), (448, 256), (256, 256)],
         fetched=True,
     )
     pair = lax.all_gather(send, "c")

time: 144 us -> 143 us (level)
  no operation moved by 1% of the time
where the time goes in v10:
time: 143 us; the launch traced here: 141 us
  blocking collectives  132 us (92%)
  Pallas kernels  7.11 us (5%)
  between operations  1.44 us (1%)
    all_gather x1, blocking collectives, on_device(): groups = lax.all_gather(out, 'zh')  27.6 us
    all_to_all x1, blocking collectives, on_device(): planes = lax.all_to_all(offset, ('zh',) + LOW, 0, 0, tiled=True)  21.6 us
    all_to_all x1, blocking collectives, on_device(): parts = lax.all_to_all(out, 'x', 0, 0, tiled=True)  17.6 us
    all_gather x1, blocking collectives, on_device(): parts = lax.all_gather(out, LOW)  16.8 us
    all_to_all x1, blocking collectives, on_device(): sums = lax.all_to_all(root, SHARE + ('x', 'c'), 0, 0, tiled=True)  11 us
    all_to_all x1, blocking collectives, on_device(): parts = lax.all_to_all(offset, ('x', 'c'), 0, 0, tiled=True)  10.1 us
    all_to_all x1, blocking collectives, on_device(): parts = lax.all_to_all(root, 'y', 0, 0, tiled=True)  9.17 us
    all_to_all x1, blocking collectives, on_device(): states = lax.all_to_all(states, ('x', 'c'), 0, 0, tiled=True)  8.52 us

profile of v10, /device:TPU:6, one launch (start us, length us, event | category | flops | bytes accessed | tf_op | source)
XLA Modules:
  0.0 140.6 jit_solution(16716806717083274616)
XLA Ops:
  1.3 0.1 stack.31
  1.4 0.1 broadcast_in_dim.2.marks
  1.4 1.8 %shard_map.122 = (f32[256,256]{1,0:T(8,128)S(1)}, f32[448,256]{1,0:T(8,128)S(1)}, f32[256,256]{1,0:T(8,128)S(1)}) custom-call(s32[8,512]{1,0:T(8,128)S(1)} %broadcast_in_dim.2.marks, bf16[1,2,128,128]{3,2,1,0:T(8,128)(2,1)} %linv_in.1, bf16[1,2,128,128]{3,2,1,0:T(8,128)(2,1)} %llink_in.1, bf16[1,2,128,128]{3,2,1,0:T(8,128)(2,1)} %rhs_in.1, ...), custom_call_target="tpu_custom_call" | custom-call | tf_op jit(solution)/shard_map/pallas_call | solution.py:334
  3.3 2.5 %all-gather = f32[896,256]{1,0:T(8,128)S(1)} all-gather(f32[448,256]{1,0:T(8,128)S(1)} %get-tuple-element.27), channel_id=2, replica_groups=mesh['zh'=4,'za'=2,'zb'=2,'x'=4,'c'=2,'y'=4] {'c'}, dimensions={0}, use_global_device_ids=true | all-gather | bytes 1376256 | tf_op jit(solution)/shard_map/all_gather | solution.py:370
  5.7 0.4 shard_map.123
  6.1 17.6 %all_to_all.30.parts = f32[4,160,256]{2,1,0:T(8,128)S(1)} all-to-all(f32[4,160,256]{2,1,0:T(8,128)S(1)} %get-tuple-element.29), channel_id=1, replica_groups=mesh['zh'=4,'za'=2,'zb'=2,'x'=4,'c'=2,'y'=4] {'x'}, dimensions={0} | all-to-all | bytes 1310720 | tf_op jit(solution)/shard_map/all_to_all | solution.py:376
  23.8 2.4 %all-gather.1 = f32[8,96,256]{2,1,0:T(8,128)S(1)} all-gather(f32[4,96,256]{2,1,0:T(8,128)S(1)} %slice.12), channel_id=3, replica_groups=mesh['zh'=4,'za'=2,'zb'=2,'x'=4,'c'=2,'y'=4] {'c'}, dimensions={0}, use_global_device_ids=true | all-gather | bytes 1179648 | tf_op jit(solution)/shard_map/all_gather | solution.py:377
  26.1 0.6 shard_map.124
  26.7 16.8 %all-gather.2 = f32[640,256]{1,0:T(8,128)S(1)} all-gather(f32[160,256]{1,0:T(8,128)S(1)} %get-tuple-element.30), channel_id=4, replica_groups=mesh['zh'=4,'za'=2,'zb'=2,'x'=4,'c'=2,'y'=4] {'za','zb'}, dimensions={0}, use_global_device_ids=true | all-gather | bytes 819200 | tf_op jit(solution)/shard_map/all_gather | solution.py:381
  43.5 2.4 %all-gather.3 = f32[8,96,256]{2,1,0:T(8,128)S(1)} all-gather(f32[4,96,256]{2,1,0:T(8,128)S(1)} %slice.13), channel_id=5, replica_groups=mesh['zh'=4,'za'=2,'zb'=2,'x'=4,'c'=2,'y'=4] {'c'}, dimensions={0}, use_global_device_ids=true | all-gather | bytes 1179648 | tf_op jit(solution)/shard_map/all_gather | solution.py:382
  45.9 0.6 shard_map.125
  46.5 27.6 %all-gather.4 = f32[416,256]{1,0:T(8,128)S(1)} all-gather(f32[104,256]{1,0:T(8,128)S(1)} %get-tuple-element.33), channel_id=6, replica_groups=mesh['zh'=4,'za'=2,'zb'=2,'x'=4,'c'=2,'y'=4] {'zh'}, dimensions={0}, use_global_device_ids=true | all-gather | bytes 532480 | tf_op jit(solution)/shard_map/all_gather | solution.py:388
  74.1 2.2 %all-gather.5 = f32[8,64,256]{2,1,0:T(8,128)S(1)} all-gather(f32[4,64,256]{2,1,0:T(8,128)S(1)} %slice.14), channel_id=7, replica_groups=mesh['zh'=4,'za'=2,'zb'=2,'x'=4,'c'=2,'y'=4] {'c'}, dimensions={0}, use_global_device_ids=true | all-gather | bytes 786432 | tf_op jit(solution)/shard_map/all_gather | solution.py:389
  76.3 0.5 shard_map.126
  76.8 0.0 copy-start
  76.8 9.2 %all_to_all.31.parts = f32[4,32,128]{2,1,0:T(8,128)S(1)} all-to-all(f32[4,32,128]{2,1,0:T(8,128)S(1)} %get-tuple-element.36), channel_id=1, replica_groups=mesh['zh'=4,'za'=2,'zb'=2,'x'=4,'c'=2,'y'=4] {'y'}, dimensions={0} | all-to-all | bytes 131072 | tf_op jit(solution)/shard_map/all_to_all | solution.py:395
  86.0 0.0 copy-start.2
  86.1 0.0 copy-start.3
  86.1 0.0 copy-start.4
  86.1 11.0 %all_to_all.32.sums = f32[16,32,128]{2,1,0:T(8,128)S(1)} all-to-all(f32[16,32,128]{2,1,0:T(8,128)S(1)} %shard_map.127), channel_id=1, replica_groups=mesh['zh'=4,'za'=2,'zb'=2,'x'=4,'c'=2,'y'=4] {'zb','x','c'}, dimensions={0} | all-to-all | bytes 524288 | tf_op jit(solution)/shard_map/all_to_all | solution.py:397
  97.0 0.0 copy-done.1
  97.0 0.0 copy-done.5
  97.0 0.0 copy-done
  97.0 0.0 copy-done.2
  97.1 0.0 copy-done.3
  97.1 1.4 shard_map.128
  98.5 10.1 %all_to_all.33.parts = f32[8,64,128]{2,1,0:T(8,128)S(1)} all-to-all(f32[8,64,128]{2,1,0:T(8,128)S(1)} %get-tuple-element.40), channel_id=1, replica_groups=mesh['zh'=4,'za'=2,'zb'=2,'x'=4,'c'=2,'y'=4] {'x','c'}, dimensions={0} | all-to-all | bytes 524288 | tf_op jit(solution)/shard_map/all_to_all | solution.py:406
  108.6 0.6 shard_map.129
  109.1 21.6 %all_to_all.34.planes = f32[16,16,128]{2,1,0:T(8,128)S(1)} all-to-all(f32[16,16,128]{2,1,0:T(8,128)S(1)} %shard_map.129), channel_id=1, replica_groups=mesh['zh'=4,'za'=2,'zb'=2,'x'=4,'c'=2,'y'=4] {'zh','za','zb'}, dimensions={0} | all-to-all | bytes 262144 | tf_op jit(solution)/shard_map/all_to_all | solution.py:408
  130.8 0.3 shard_map.130
  131.1 8.5 %all_to_all.35.parts = f32[8,32,128]{2,1,0:T(8,128)S(1)} all-to-all(f32[8,32,128]{2,1,0:T(8,128)S(1)} %shard_map.130), channel_id=1, replica_groups=mesh['zh'=4,'za'=2,'zb'=2,'x'=4,'c'=2,'y'=4] {'x','c'}, dimensions={0} | all-to-all | bytes 262144 | tf_op jit(solution)/shard_map/all_to_all | solution.py:410
  139.6 1.0 shard_map.131
  (7 shorter events, 0.1 us)
Async XLA Ops:
  76.3 20.8 %copy-start.1 = (bf16[512,512]{1,0:T(8,128)(2,1)S(1)}, bf16[512,512]{1,0:T(8,128)(2,1)}, u32[]{:S(2)}) copy-start(bf16[512,512]{1,0:T(8,128)(2,1)} %root_upper.1) | copy-start | bytes 1572868
  76.3 20.8 %copy-start.5 = (bf16[512,128]{1,0:T(8,128)(2,1)S(1)}, bf16[512,128]{1,0:T(8,128)(2,1)}, u32[]{:S(2)}) copy-start(bf16[512,128]{1,0:T(8,128)(2,1)} %rhs_root.1) | copy-start | bytes 393220
  76.8 20.2 %copy-start = (bf16[512,512]{1,0:T(8,128)(2,1)S(1)}, bf16[512,512]{1,0:T(8,128)(2,1)}, u32[]{:S(2)}) copy-start(bf16[512,512]{1,0:T(8,128)(2,1)} %root_lower.1) | copy-start | bytes 1572868
  86.0 11.0 %copy-start.2 = (bf16[1,2,128,512]{3,2,1,0:T(8,128)(2,1)S(1)}, bf16[1,2,128,512]{3,2,1,0:T(8,128)(2,1)}, u32[]{:S(2)}) copy-start(bf16[1,2,128,512]{3,2,1,0:T(8,128)(2,1)} %uroot.1) | copy-start | bytes 786436
  86.1 11.0 %copy-start.3 = (bf16[1,2,128,128]{3,2,1,0:T(8,128)(2,1)S(1)}, bf16[1,2,128,128]{3,2,1,0:T(8,128)(2,1)}, u32[]{:S(2)}) copy-start(bf16[1,2,128,128]{3,2,1,0:T(8,128)(2,1)} %uinv.1) | copy-start | bytes 196612
  86.1 11.0 %copy-start.4 = (bf16[1,2,128,128]{3,2,1,0:T(8,128)(2,1)S(1)}, bf16[1,2,128,128]{3,2,1,0:T(8,128)(2,1)}, u32[]{:S(2)}) copy-start(bf16[1,2,128,128]{3,2,1,0:T(8,128)(2,1)} %ulink.1) | copy-start | bytes 196612

commit v11 on v10

--- a/solution.py
+++ b/solution.py
@@ -219,14 +219,18 @@
         state = stacked[:W] + maps[k][:, W:]
         states.append(state)
     carry[...] = pick(place, *states[:4])
-    for other in range(4):
+    for other in range(8):
         root[other] = total
     solve_out[...] = after(solve[...], before_low[...])
 
 
 def sum_kernel(parts, out):
-    total = (parts[0] + parts[1]) + (parts[2] + parts[3])
-    for other in range(8 * SHARES):
+    rows = []
+    for core in range(2):
+        a, b, c, d = [parts[2 * layer + core] for layer in range(4)]
+        rows.append((a + b) + (c + d))
+    total = jnp.concatenate(rows, 0)
+    for other in range(8):
         out[other] = total
 
 
@@ -234,8 +238,8 @@
     marks, sums, rhs_root, root_lower, root_upper, carry, solve, ends, groups, uinv, ulink,
     uroot, own_root, plain, offset,
 ):
-    order = [(k * 4 + x) * 2 + c for c in range(2) for x in range(4) for k in range(SHARES)]
-    summed = jnp.concatenate([sums[k] for k in order], 0)
+    order = [(k * 4 + x, c) for c in range(2) for x in range(4) for k in range(SHARES)]
+    summed = jnp.concatenate([sums[k, ROWS * c : ROWS * c + ROWS] for k, c in order], 0)
     inner = mul2(root_lower[...], rhs_root[...].astype(F32) - summed)
     root = mul2(root_upper[...], inner)
     solved = mul3(solve[:, :W], carry[...]) + solve[:, W:]
@@ -390,11 +394,11 @@
     root, carry, solve = call(
         top_kernel,
         [marks, groups, pieces, solve, before_low],
-        [(4, ROWS, W), square, (256, 256)],
-    )
-    parts = lax.all_to_all(root, "y", 0, 0, tiled=True)
-    (root,) = call(sum_kernel, [parts], [(8 * SHARES, ROWS, W)])
-    sums = lax.all_to_all(root, SHARE + ("x", "c"), 0, 0, tiled=True)
+        [(8, ROWS, W), square, (256, 256)],
+    )
+    parts = lax.all_to_all(root, ("y", "c"), 0, 0, tiled=True)
+    (root,) = call(sum_kernel, [parts], [(8, 2 * ROWS, W)])
+    sums = lax.all_to_all(root, SHARE + ("x",), 0, 0, tiled=True)
     column, plain, offset = call(
         root_kernel,
         [

time: 143 us -> 143 us (level)
  no operation moved by 1% of the time
where the time goes in v11:
time: 143 us; the launch traced here: 140 us
  blocking collectives  131 us (92%)
  Pallas kernels  7.12 us (5%)
  between operations  1.43 us (1%)
    all_gather x1, blocking collectives, on_device(): groups = lax.all_gather(out, 'zh')  27.6 us
    all_to_all x1, blocking collectives, on_device(): planes = lax.all_to_all(offset, ('zh',) + LOW, 0, 0, tiled=True)  21.6 us
    all_to_all x1, blocking collectives, on_device(): parts = lax.all_to_all(out, 'x', 0, 0, tiled=True)  17.6 us
    all_gather x1, blocking collectives, on_device(): parts = lax.all_gather(out, LOW)  16.8 us
    all_to_all x1, blocking collectives, on_device(): parts = lax.all_to_all(offset, ('x', 'c'), 0, 0, tiled=True)  10.3 us
    all_to_all x1, blocking collectives, on_device(): sums = lax.all_to_all(root, SHARE + ('x',), 0, 0, tiled=True)  9.86 us
    all_to_all x1, blocking collectives, on_device(): parts = lax.all_to_all(root, ('y', 'c'), 0, 0, tiled=True)  9.68 us
    all_to_all x1, blocking collectives, on_device(): states = lax.all_to_all(states, ('x', 'c'), 0, 0, tiled=True)  8.52 us

profile of v11, /device:TPU:6, one launch (start us, length us, event | category | flops | bytes accessed | tf_op | source)
XLA Modules:
  0.0 140.1 jit_solution(12563091727757802909)
XLA Ops:
  1.3 0.1 stack.31
  1.4 0.1 broadcast_in_dim.2.marks
  1.4 1.8 %shard_map.122 = (f32[256,256]{1,0:T(8,128)S(1)}, f32[448,256]{1,0:T(8,128)S(1)}, f32[256,256]{1,0:T(8,128)S(1)}) custom-call(s32[8,512]{1,0:T(8,128)S(1)} %broadcast_in_dim.2.marks, bf16[1,2,128,128]{3,2,1,0:T(8,128)(2,1)} %linv_in.1, bf16[1,2,128,128]{3,2,1,0:T(8,128)(2,1)} %llink_in.1, bf16[1,2,128,128]{3,2,1,0:T(8,128)(2,1)} %rhs_in.1, ...), custom_call_target="tpu_custom_call" | custom-call | tf_op jit(solution)/shard_map/pallas_call | solution.py:338
  3.3 2.5 %all-gather = f32[896,256]{1,0:T(8,128)S(1)} all-gather(f32[448,256]{1,0:T(8,128)S(1)} %get-tuple-element.27), channel_id=2, replica_groups=mesh['zh'=4,'za'=2,'zb'=2,'x'=4,'c'=2,'y'=4] {'c'}, dimensions={0}, use_global_device_ids=true | all-gather | bytes 1376256 | tf_op jit(solution)/shard_map/all_gather | solution.py:374
  5.7 0.4 shard_map.123
  6.1 17.6 %all_to_all.30.parts = f32[4,160,256]{2,1,0:T(8,128)S(1)} all-to-all(f32[4,160,256]{2,1,0:T(8,128)S(1)} %get-tuple-element.29), channel_id=1, replica_groups=mesh['zh'=4,'za'=2,'zb'=2,'x'=4,'c'=2,'y'=4] {'x'}, dimensions={0} | all-to-all | bytes 1310720 | tf_op jit(solution)/shard_map/all_to_all | solution.py:380
  23.8 2.4 %all-gather.1 = f32[8,96,256]{2,1,0:T(8,128)S(1)} all-gather(f32[4,96,256]{2,1,0:T(8,128)S(1)} %slice.12), channel_id=3, replica_groups=mesh['zh'=4,'za'=2,'zb'=2,'x'=4,'c'=2,'y'=4] {'c'}, dimensions={0}, use_global_device_ids=true | all-gather | bytes 1179648 | tf_op jit(solution)/shard_map/all_gather | solution.py:381
  26.1 0.6 shard_map.124
  26.7 16.8 %all-gather.2 = f32[640,256]{1,0:T(8,128)S(1)} all-gather(f32[160,256]{1,0:T(8,128)S(1)} %get-tuple-element.30), channel_id=4, replica_groups=mesh['zh'=4,'za'=2,'zb'=2,'x'=4,'c'=2,'y'=4] {'za','zb'}, dimensions={0}, use_global_device_ids=true | all-gather | bytes 819200 | tf_op jit(solution)/shard_map/all_gather | solution.py:385
  43.5 2.4 %all-gather.3 = f32[8,96,256]{2,1,0:T(8,128)S(1)} all-gather(f32[4,96,256]{2,1,0:T(8,128)S(1)} %slice.13), channel_id=5, replica_groups=mesh['zh'=4,'za'=2,'zb'=2,'x'=4,'c'=2,'y'=4] {'c'}, dimensions={0}, use_global_device_ids=true | all-gather | bytes 1179648 | tf_op jit(solution)/shard_map/all_gather | solution.py:386
  45.9 0.6 shard_map.125
  46.5 27.6 %all-gather.4 = f32[416,256]{1,0:T(8,128)S(1)} all-gather(f32[104,256]{1,0:T(8,128)S(1)} %get-tuple-element.33), channel_id=6, replica_groups=mesh['zh'=4,'za'=2,'zb'=2,'x'=4,'c'=2,'y'=4] {'zh'}, dimensions={0}, use_global_device_ids=true | all-gather | bytes 532480 | tf_op jit(solution)/shard_map/all_gather | solution.py:392
  74.1 2.2 %all-gather.5 = f32[8,64,256]{2,1,0:T(8,128)S(1)} all-gather(f32[4,64,256]{2,1,0:T(8,128)S(1)} %slice.14), channel_id=7, replica_groups=mesh['zh'=4,'za'=2,'zb'=2,'x'=4,'c'=2,'y'=4] {'c'}, dimensions={0}, use_global_device_ids=true | all-gather | bytes 786432 | tf_op jit(solution)/shard_map/all_gather | solution.py:393
  76.3 0.5 shard_map.126
  76.8 0.0 copy-start.1
  76.9 9.7 %all_to_all.31.parts = f32[8,32,128]{2,1,0:T(8,128)S(1)} all-to-all(f32[8,32,128]{2,1,0:T(8,128)S(1)} %get-tuple-element.36), channel_id=1, replica_groups=mesh['zh'=4,'za'=2,'zb'=2,'x'=4,'c'=2,'y'=4] {'y','c'}, dimensions={0} | all-to-all | bytes 262144 | tf_op jit(solution)/shard_map/all_to_all | solution.py:399
  86.6 0.0 copy-start.3
  86.6 0.0 copy-start.4
  86.6 9.9 %all_to_all.32.sums = f32[8,64,128]{2,1,0:T(8,128)S(1)} all-to-all(f32[8,64,128]{2,1,0:T(8,128)S(1)} %shard_map.127), channel_id=1, replica_groups=mesh['zh'=4,'za'=2,'zb'=2,'x'=4,'c'=2,'y'=4] {'zb','x'}, dimensions={0} | all-to-all | bytes 524288 | tf_op jit(solution)/shard_map/all_to_all | solution.py:401
  96.4 0.0 copy-done.2
  96.4 0.0 copy-done.5
  96.5 0.0 copy-done.1
  96.5 0.0 copy-done
  96.5 0.0 copy-done.3
  96.5 0.0 copy-done.4
  96.5 1.4 shard_map.128
  97.9 10.3 %all_to_all.33.parts = f32[8,64,128]{2,1,0:T(8,128)S(1)} all-to-all(f32[8,64,128]{2,1,0:T(8,128)S(1)} %get-tuple-element.40), channel_id=1, replica_groups=mesh['zh'=4,'za'=2,'zb'=2,'x'=4,'c'=2,'y'=4] {'x','c'}, dimensions={0} | all-to-all | bytes 524288 | tf_op jit(solution)/shard_map/all_to_all | solution.py:410
  108.1 0.6 shard_map.129
  108.7 21.6 %all_to_all.34.planes = f32[16,16,128]{2,1,0:T(8,128)S(1)} all-to-all(f32[16,16,128]{2,1,0:T(8,128)S(1)} %shard_map.129), channel_id=1, replica_groups=mesh['zh'=4,'za'=2,'zb'=2,'x'=4,'c'=2,'y'=4] {'zh','za','zb'}, dimensions={0} | all-to-all | bytes 262144 | tf_op jit(solution)/shard_map/all_to_all | solution.py:412
  130.3 0.3 shard_map.130
  130.6 8.5 %all_to_all.35.parts = f32[8,32,128]{2,1,0:T(8,128)S(1)} all-to-all(f32[8,32,128]{2,1,0:T(8,128)S(1)} %shard_map.130), channel_id=1, replica_groups=mesh['zh'=4,'za'=2,'zb'=2,'x'=4,'c'=2,'y'=4] {'x','c'}, dimensions={0} | all-to-all | bytes 262144 | tf_op jit(solution)/shard_map/all_to_all | solution.py:414
  139.2 1.0 shard_map.131
  (7 shorter events, 0.1 us)
Async XLA Ops:
  76.3 20.2 %copy-start.2 = (bf16[1,2,128,512]{3,2,1,0:T(8,128)(2,1)S(1)}, bf16[1,2,128,512]{3,2,1,0:T(8,128)(2,1)}, u32[]{:S(2)}) copy-start(bf16[1,2,128,512]{3,2,1,0:T(8,128)(2,1)} %uroot.1) | copy-start | bytes 786436
  76.3 20.2 %copy-start.5 = (bf16[512,128]{1,0:T(8,128)(2,1)S(1)}, bf16[512,128]{1,0:T(8,128)(2,1)}, u32[]{:S(2)}) copy-start(bf16[512,128]{1,0:T(8,128)(2,1)} %rhs_root.1) | copy-start | bytes 393220
  76.8 19.6 %copy-start.1 = (bf16[512,512]{1,0:T(8,128)(2,1)S(1)}, bf16[512,512]{1,0:T(8,128)(2,1)}, u32[]{:S(2)}) copy-start(bf16[512,512]{1,0:T(8,128)(2,1)} %root_upper.1) | copy-start | bytes 1572868
  86.5 9.9 %copy-start = (bf16[512,512]{1,0:T(8,128)(2,1)S(1)}, bf16[512,512]{1,0:T(8,128)(2,1)}, u32[]{:S(2)}) copy-start(bf16[512,512]{1,0:T(8,128)(2,1)} %root_lower.1) | copy-start | bytes 1572868
  86.6 9.9 %copy-start.3 = (bf16[1,2,128,128]{3,2,1,0:T(8,128)(2,1)S(1)}, bf16[1,2,128,128]{3,2,1,0:T(8,128)(2,1)}, u32[]{:S(2)}) copy-start(bf16[1,2,128,128]{3,2,1,0:T(8,128)(2,1)} %uinv.1) | copy-start | bytes 196612
  86.6 9.9 %copy-start.4 = (bf16[1,2,128,128]{3,2,1,0:T(8,128)(2,1)S(1)}, bf16[1,2,128,128]{3,2,1,0:T(8,128)(2,1)}, u32[]{:S(2)}) copy-start(bf16[1,2,128,128]{3,2,1,0:T(8,128)(2,1)} %ulink.1) | copy-start | bytes 196612

commit v12 on v11

--- a/solution.py
+++ b/solution.py
@@ -208,17 +208,18 @@
 
 def top_kernel(marks, parts, pieces, solve, before_low, root, carry, solve_out):
     place = marks[HIGH : HIGH + 1]
-    maps = [jnp.concatenate([pieces[0, k], pieces[1, k]], 0) for k in range(4)]
+    maps = [jnp.concatenate([pieces[0, k], pieces[1, k]], 0) for k in range(3)]
     roots = [parts[k, 72:] for k in range(4)]
     total = roots[0][:, W:]
     state = maps[0][:, W:]
     states = [jnp.zeros((W, W), F32), state]
-    for k in range(1, 4):
+    for k in range(1, 3):
         stacked = mul3(jnp.concatenate([maps[k][:, :W], roots[k][:, :W]], 0), state)
         total = total + stacked[W:] + roots[k][:, W:]
         state = stacked[:W] + maps[k][:, W:]
         states.append(state)
-    carry[...] = pick(place, *states[:4])
+    total = total + mul3(roots[3][:, :W], state) + roots[3][:, W:]
+    carry[...] = pick(place, *states)
     for other in range(8):
         root[other] = total
     solve_out[...] = after(solve[...], before_low[...])
@@ -289,16 +290,17 @@
     for other in range(4):
         value = pick(group - other, *values)
         for k in range(4):
-            out[4 * other + k] = value
+            out[4 * k + other] = value
 
 
 def carry_kernel(marks, planes, within, parts, spread, out):
     group = marks[HIGH : HIGH + 1]
     apart = jnp.broadcast_to(group[:, :W], (16, W))
     state = jnp.zeros((16, W), F32)
-    for k in range(4, 16):
-        state = state + jnp.where(apart < k // 4, planes[k], F32(0))
-    offsets = [pick(group, *[planes[4 * g + k] for g in range(4)]) for k in range(1, 4)]
+    for k in range(16):
+        if k % 4:
+            state = state + jnp.where(apart < k % 4, planes[k], F32(0))
+    offsets = [pick(group, *[planes[4 * k + g] for g in range(4)]) for k in range(1, 4)]
     state = mul3(jnp.concatenate([state] + offsets, 1), within[...])
     chips = chip_offsets(parts)
     moved = mul3(chips[3], spread[:, 3 * W : 5 * W])
@@ -390,7 +392,7 @@
         [(72 + ROWS, 256), wide, (256, 256), square, (4 * W, W)],
     )
     groups = lax.all_gather(out, "zh")
-    pieces = lax.all_gather(groups[:, :64], "c")
+    pieces = lax.all_gather(groups[:3, :64], "c")
     root, carry, solve = call(
         top_kernel,
         [marks, groups, pieces, solve, before_low],
@@ -409,7 +411,7 @@
     )
     parts = lax.all_to_all(offset, ("x", "c"), 0, 0, tiled=True)
     (offset,) = call(offset_kernel, [marks, parts, gather, ahead], [(16, 16, W)])
-    planes = lax.all_to_all(offset, ("zh",) + LOW, 0, 0, tiled=True)
+    planes = lax.all_to_all(offset, LOW + ("zh",), 0, 0, tiled=True)
     (states,) = call(carry_kernel, [marks, planes, within, parts, spread], [(8, 32, W)])
     states = lax.all_to_all(states, ("x", "c"), 0, 0, tiled=True)
     answers, own_root = call(

time: 143 us -> 143 us (level)
  no operation moved by 1% of the time
where the time goes in v12:
time: 143 us; the launch traced here: 140 us
  blocking collectives  131 us (92%)
  Pallas kernels  7.1 us (5%)
    all_gather x1, blocking collectives, on_device(): groups = lax.all_gather(out, 'zh')  27.6 us
    all_to_all x1, blocking collectives, on_device(): planes = lax.all_to_all(offset, LOW + ('zh',), 0, 0, tiled=True)  21.5 us
    all_to_all x1, blocking collectives, on_device(): parts = lax.all_to_all(out, 'x', 0, 0, tiled=True)  17.6 us
    all_gather x1, blocking collectives, on_device(): parts = lax.all_gather(out, LOW)  16.8 us
    all_to_all x1, blocking collectives, on_device(): parts = lax.all_to_all(offset, ('x', 'c'), 0, 0, tiled=True)  10.3 us
    all_to_all x1, blocking collectives, on_device(): sums = lax.all_to_all(root, SHARE + ('x',), 0, 0, tiled=True)  9.86 us
    all_to_all x1, blocking collectives, on_device(): parts = lax.all_to_all(root, ('y', 'c'), 0, 0, tiled=True)  9.68 us
    all_to_all x1, blocking collectives, on_device(): states = lax.all_to_all(states, ('x', 'c'), 0, 0, tiled=True)  8.52 us

profile of v12, /device:TPU:6, one launch (start us, length us, event | category | flops | bytes accessed | tf_op | source)
XLA Modules:
  0.0 139.9 jit_solution(3058219526303836375)
XLA Ops:
  1.3 0.1 stack.31
  1.4 0.1 broadcast_in_dim.2.marks
  1.4 1.8 %shard_map.122 = (f32[256,256]{1,0:T(8,128)S(1)}, f32[448,256]{1,0:T(8,128)S(1)}, f32[256,256]{1,0:T(8,128)S(1)}) custom-call(s32[8,512]{1,0:T(8,128)S(1)} %broadcast_in_dim.2.marks, bf16[1,2,128,128]{3,2,1,0:T(8,128)(2,1)} %linv_in.1, bf16[1,2,128,128]{3,2,1,0:T(8,128)(2,1)} %llink_in.1, bf16[1,2,128,128]{3,2,1,0:T(8,128)(2,1)} %rhs_in.1, ...), custom_call_target="tpu_custom_call" | custom-call | tf_op jit(solution)/shard_map/pallas_call | solution.py:340
  3.3 2.5 %all-gather = f32[896,256]{1,0:T(8,128)S(1)} all-gather(f32[448,256]{1,0:T(8,128)S(1)} %get-tuple-element.27), channel_id=2, replica_groups=mesh['zh'=4,'za'=2,'zb'=2,'x'=4,'c'=2,'y'=4] {'c'}, dimensions={0}, use_global_device_ids=true | all-gather | bytes 1376256 | tf_op jit(solution)/shard_map/all_gather | solution.py:376
  5.7 0.4 shard_map.123
  6.1 17.6 %all_to_all.30.parts = f32[4,160,256]{2,1,0:T(8,128)S(1)} all-to-all(f32[4,160,256]{2,1,0:T(8,128)S(1)} %get-tuple-element.29), channel_id=1, replica_groups=mesh['zh'=4,'za'=2,'zb'=2,'x'=4,'c'=2,'y'=4] {'x'}, dimensions={0} | all-to-all | bytes 1310720 | tf_op jit(solution)/shard_map/all_to_all | solution.py:382
  23.8 2.4 %all-gather.1 = f32[8,96,256]{2,1,0:T(8,128)S(1)} all-gather(f32[4,96,256]{2,1,0:T(8,128)S(1)} %slice.12), channel_id=3, replica_groups=mesh['zh'=4,'za'=2,'zb'=2,'x'=4,'c'=2,'y'=4] {'c'}, dimensions={0}, use_global_device_ids=true | all-gather | bytes 1179648 | tf_op jit(solution)/shard_map/all_gather | solution.py:383
  26.1 0.6 shard_map.124
  26.7 16.8 %all-gather.2 = f32[640,256]{1,0:T(8,128)S(1)} all-gather(f32[160,256]{1,0:T(8,128)S(1)} %get-tuple-element.30), channel_id=4, replica_groups=mesh['zh'=4,'za'=2,'zb'=2,'x'=4,'c'=2,'y'=4] {'za','zb'}, dimensions={0}, use_global_device_ids=true | all-gather | bytes 819200 | tf_op jit(solution)/shard_map/all_gather | solution.py:387
  43.5 2.4 %all-gather.3 = f32[8,96,256]{2,1,0:T(8,128)S(1)} all-gather(f32[4,96,256]{2,1,0:T(8,128)S(1)} %slice.13), channel_id=5, replica_groups=mesh['zh'=4,'za'=2,'zb'=2,'x'=4,'c'=2,'y'=4] {'c'}, dimensions={0}, use_global_device_ids=true | all-gather | bytes 1179648 | tf_op jit(solution)/shard_map/all_gather | solution.py:388
  45.9 0.6 shard_map.125
  46.5 27.6 %all-gather.4 = f32[416,256]{1,0:T(8,128)S(1)} all-gather(f32[104,256]{1,0:T(8,128)S(1)} %get-tuple-element.33), channel_id=6, replica_groups=mesh['zh'=4,'za'=2,'zb'=2,'x'=4,'c'=2,'y'=4] {'zh'}, dimensions={0}, use_global_device_ids=true | all-gather | bytes 532480 | tf_op jit(solution)/shard_map/all_gather | solution.py:394
  74.1 2.1 %all-gather.5 = f32[6,64,256]{2,1,0:T(8,128)S(1)} all-gather(f32[3,64,256]{2,1,0:T(8,128)S(1)} %slice.14), channel_id=7, replica_groups=mesh['zh'=4,'za'=2,'zb'=2,'x'=4,'c'=2,'y'=4] {'c'}, dimensions={0}, use_global_device_ids=true | all-gather | bytes 589824 | tf_op jit(solution)/shard_map/all_gather | solution.py:395
  76.2 0.5 shard_map.126
  76.7 0.0 copy-start.1
  76.7 9.7 %all_to_all.31.parts = f32[8,32,128]{2,1,0:T(8,128)S(1)} all-to-all(f32[8,32,128]{2,1,0:T(8,128)S(1)} %get-tuple-element.36), channel_id=1, replica_groups=mesh['zh'=4,'za'=2,'zb'=2,'x'=4,'c'=2,'y'=4] {'y','c'}, dimensions={0} | all-to-all | bytes 262144 | tf_op jit(solution)/shard_map/all_to_all | solution.py:401
  86.4 0.0 copy-start.3
  86.5 0.0 copy-start.4
  86.5 9.9 %all_to_all.32.sums = f32[8,64,128]{2,1,0:T(8,128)S(1)} all-to-all(f32[8,64,128]{2,1,0:T(8,128)S(1)} %shard_map.127), channel_id=1, replica_groups=mesh['zh'=4,'za'=2,'zb'=2,'x'=4,'c'=2,'y'=4] {'zb','x'}, dimensions={0} | all-to-all | bytes 524288 | tf_op jit(solution)/shard_map/all_to_all | solution.py:403
  96.3 0.0 copy-done.2
  96.3 0.0 copy-done.5
  96.3 0.0 copy-done.1
  96.3 0.0 copy-done
  96.3 0.0 copy-done.3
  96.4 0.0 copy-done.4
  96.4 1.4 shard_map.128
  97.7 10.3 %all_to_all.33.parts = f32[8,64,128]{2,1,0:T(8,128)S(1)} all-to-all(f32[8,64,128]{2,1,0:T(8,128)S(1)} %get-tuple-element.40), channel_id=1, replica_groups=mesh['zh'=4,'za'=2,'zb'=2,'x'=4,'c'=2,'y'=4] {'x','c'}, dimensions={0} | all-to-all | bytes 524288 | tf_op jit(solution)/shard_map/all_to_all | solution.py:412
  108.0 0.6 shard_map.129
  108.6 21.5 %all_to_all.34.planes = f32[16,16,128]{2,1,0:T(8,128)S(1)} all-to-all(f32[16,16,128]{2,1,0:T(8,128)S(1)} %shard_map.129), channel_id=1, replica_groups=mesh['zh'=4,'za'=2,'zb'=2,'x'=4,'c'=2,'y'=4] {'za','zb','zh'}, dimensions={0} | all-to-all | bytes 262144 | tf_op jit(solution)/shard_map/all_to_all | solution.py:414
  130.1 0.3 shard_map.130
  130.5 8.5 %all_to_all.35.parts = f32[8,32,128]{2,1,0:T(8,128)S(1)} all-to-all(f32[8,32,128]{2,1,0:T(8,128)S(1)} %shard_map.130), channel_id=1, replica_groups=mesh['zh'=4,'za'=2,'zb'=2,'x'=4,'c'=2,'y'=4] {'x','c'}, dimensions={0} | all-to-all | bytes 262144 | tf_op jit(solution)/shard_map/all_to_all | solution.py:416
  139.0 1.0 shard_map.131
  (7 shorter events, 0.1 us)
Async XLA Ops:
  76.2 20.1 %copy-start.2 = (bf16[1,2,128,512]{3,2,1,0:T(8,128)(2,1)S(1)}, bf16[1,2,128,512]{3,2,1,0:T(8,128)(2,1)}, u32[]{:S(2)}) copy-start(bf16[1,2,128,512]{3,2,1,0:T(8,128)(2,1)} %uroot.1) | copy-start | bytes 786436
  76.2 20.1 %copy-start.5 = (bf16[512,128]{1,0:T(8,128)(2,1)S(1)}, bf16[512,128]{1,0:T(8,128)(2,1)}, u32[]{:S(2)}) copy-start(bf16[512,128]{1,0:T(8,128)(2,1)} %rhs_root.1) | copy-start | bytes 393220
  76.7 19.6 %copy-start.1 = (bf16[512,512]{1,0:T(8,128)(2,1)S(1)}, bf16[512,512]{1,0:T(8,128)(2,1)}, u32[]{:S(2)}) copy-start(bf16[512,512]{1,0:T(8,128)(2,1)} %root_upper.1) | copy-start | bytes 1572868
  86.4 9.9 %copy-start = (bf16[512,512]{1,0:T(8,128)(2,1)S(1)}, bf16[512,512]{1,0:T(8,128)(2,1)}, u32[]{:S(2)}) copy-start(bf16[512,512]{1,0:T(8,128)(2,1)} %root_lower.1) | copy-start | bytes 1572868
  86.4 9.9 %copy-start.3 = (bf16[1,2,128,128]{3,2,1,0:T(8,128)(2,1)S(1)}, bf16[1,2,128,128]{3,2,1,0:T(8,128)(2,1)}, u32[]{:S(2)}) copy-start(bf16[1,2,128,128]{3,2,1,0:T(8,128)(2,1)} %uinv.1) | copy-start | bytes 196612
  86.5 9.9 %copy-start.4 = (bf16[1,2,128,128]{3,2,1,0:T(8,128)(2,1)S(1)}, bf16[1,2,128,128]{3,2,1,0:T(8,128)(2,1)}, u32[]{:S(2)}) copy-start(bf16[1,2,128,128]{3,2,1,0:T(8,128)(2,1)} %ulink.1) | copy-start | bytes 196612
